TPU v7x, 512 devices: a whole 4x8x8 slice. The times are simulated.
512 devices in a mesh: dp: 64 (over z, x, core), mp: 8 (over y).
Axes of the slice: x: 4, y: 8, z: 8, core: 2. Of those that a mesh axis runs over, the one named last changes fastest.
Arguments:
- teacher_in: bfloat16 [64, 1024, 1408], P('dp', 'mp'), may hold values from -8 to 8
- teacher_gain: float32 [1408], replicated, may hold values from 0.5 to 1.5
- teacher_qkv: bfloat16 [3, 1408, 1408], P(None, 'mp'), may hold values from -1 to 1
- teacher_out: bfloat16 [1408, 1408], P('mp'), may hold values from -0.15625 to 0.15625
- student_in: bfloat16 [64, 1024, 1024], P('dp', None, 'mp'), may hold values from -6 to 6
- student_gain: float32 [1024], replicated, may hold values from 0.25 to 1.75
- widen_weight: bfloat16 [1024, 4096], P(None, 'mp'), may hold values from -0.1875 to 0.1875
- narrow_weight: bfloat16 [4096, 1024], P('mp'), may hold values from -0.09375 to 0.09375
- target_head: bfloat16 [1408, 1024], P('mp'), may hold values from -0.1875 to 0.1875
- positions: int32 [64, 512], P('dp'), may hold values from 0 to 1023, as said below
- counts: int32 [64], P('dp'), may hold values from 1 to 512, 16384 in all
Outputs:
- grad_widen: float32 [1024, 4096], P('dp', 'mp')
- grad_narrow: float32 [1024, 4096], P('dp', 'mp')
- losses: float32 [64], P('dp')
Inputs may be any that keep to these rules, and one draw needn't show every extreme that they name: `positions`: the entries of one image's list are distinct; only the first counts of them are live. The counts of all images sum to 16384.
All inputs are finite; a program needn't handle non-finite values. No bound on the sum of `counts` on one device may be relied on, other than what follows from the above.
Results may differ from a plain program's by a relative error of at most 0.02.
Values may be sent and summed in bfloat16 or wider, within the bound.
No kernel may reach another device: no remote copies, remote signals or barrier semaphores. Data moves between devices by JAX's collectives and lax.ppermute only.
A program may use at most 64 MiB of HBM per device.

v0:
```python
import jax
import jax.numpy as jnp
from jax import lax
from jax.sharding import PartitionSpec as P

TD = 1408
TH = 16


EPSILON = 1e-06


def in_order(tiles, dim):
    tiles = jnp.moveaxis(tiles, 0, dim)
    dims = tiles.shape
    return tiles.reshape(*dims[:dim], dims[dim] * dims[dim + 1], *dims[dim + 2 :])


def sent_to_all(array, axis):
    copies = jnp.broadcast_to(array, (lax.axis_size(axis), *array.shape))
    return lax.all_to_all(copies, axis, split_axis=0, concat_axis=0, tiled=True)


def gather_directly(array, axis, dim):
    return in_order(sent_to_all(array, axis), dim)


def rows_for(lines, peers):
    spare = -lines.shape[0] % peers
    if not spare:
        return lines
    return jnp.concatenate([lines, jnp.zeros((spare, *lines.shape[1:]), lines.dtype)])


def total_of(array, axis):
    lines = array.reshape(-1, *array.shape[1:][-1:])
    own = lax.psum_scatter(
        rows_for(lines, lax.axis_size(axis)), axis, scatter_dimension=0, tiled=True
    )
    whole = lax.all_gather(own, axis).reshape(-1, *lines.shape[1:])
    return lax.slice_in_dim(whole, 0, len(lines)).reshape(array.shape)


def of_everyone(array, axis):
    everything = sent_to_all(array, axis)
    return jnp.sum(everything, axis=0)


def packed_total(arrays, axis):
    ends = [0]
    for a in arrays:
        ends.append(ends[-1] + a.size)
    so_far = of_everyone(jnp.concatenate([a.ravel() for a in arrays]), axis)
    return tuple((so_far[b:e].reshape(a.shape) for a, b, e in zip(arrays, ends, ends[1:])))


def cut_along(array, dim, peers):
    dims = array.shape
    tiles = array.reshape(*dims[:dim], peers, dims[dim] // peers, *dims[dim + 1 :])
    return jnp.moveaxis(tiles, dim, 0)


def summed_on_arrival(array, axis, dim):
    peers = lax.axis_size(axis)
    tiles = lax.all_to_all(cut_along(array, dim, peers), axis, 0, 0, tiled=True)
    return jnp.sum(tiles, axis=0)


def layer_norm(values, gain):
    mean_val = jnp.mean(values, axis=-1, keepdims=True)
    centred = values - mean_val
    spread = jnp.mean(centred * centred, axis=-1, keepdims=True)
    return centred * lax.rsqrt(spread + EPSILON) * gain


def gelu_value(pre):
    return 0.5 * pre * (1.0 + lax.erf(pre * 0.7071067811865476))


def gelu_slope(pre):
    return 0.5 * (1.0 + lax.erf(pre * 0.7071067811865476)) + pre * 0.3989422804014327 * jnp.exp(
        -0.5 * pre * pre
    )


def on_device(
    teacher_in,
    teacher_gain,
    teacher_qkv,
    teacher_out,
    student_in,
    student_gain,
    widen_weight,
    narrow_weight,
    target_head,
    positions,
    counts,
):
    patches_local = teacher_in[0]
    slot_total = positions.shape[1]
    picked = positions[0]
    live_count = counts[0]
    head_size = TD // TH
    factor = head_size ** (-0.5)
    local_width = teacher_qkv.shape[1]
    local_heads = local_width // head_size
    gathered = lax.all_gather(patches_local, "mp", axis=0, tiled=True)
    teach_normed = layer_norm(gathered.astype(jnp.float32), teacher_gain).astype(jnp.bfloat16)
    key_rows = jnp.einsum(
        "pi,oi->po", teach_normed, teacher_qkv[1], preferred_element_type=jnp.float32
    ).astype(jnp.bfloat16)
    value_rows = jnp.einsum(
        "pi,oi->po", teach_normed, teacher_qkv[2], preferred_element_type=jnp.float32
    ).astype(jnp.bfloat16)
    query_rows = jnp.einsum(
        "pi,oi->po", teach_normed[picked], teacher_qkv[0], preferred_element_type=jnp.float32
    ).astype(jnp.bfloat16)
    query_heads = query_rows.reshape(slot_total, local_heads, head_size)
    key_heads = key_rows.reshape(-1, local_heads, head_size)
    value_heads = value_rows.reshape(-1, local_heads, head_size)
    scores = (
        jnp.einsum("shd,phd->hsp", query_heads, key_heads, preferred_element_type=jnp.float32)
        * factor
    )
    largest = jnp.max(scores, axis=-1, keepdims=True)
    soft_num = jnp.exp(scores - largest)
    soft_weights = (soft_num / jnp.sum(soft_num, axis=-1, keepdims=True)).astype(jnp.bfloat16)
    attended = jnp.einsum(
        "hsp,phd->shd", soft_weights, value_heads, preferred_element_type=jnp.float32
    )
    attended = attended.astype(jnp.bfloat16).reshape(slot_total, local_width)
    blended = jnp.einsum(
        "sw,ow->so",
        gather_directly(attended, "mp", 1),
        teacher_out,
        preferred_element_type=jnp.float32,
    )
    own_start = lax.axis_index("mp") * local_width
    residual_part = lax.dynamic_slice_in_dim(gathered[picked], own_start, local_width, 1)
    targets = (residual_part.astype(jnp.float32) + blended).astype(jnp.bfloat16)
    slot_ids = jnp.arange(slot_total, dtype=jnp.int32)
    row_weight = jnp.where(
        slot_ids < live_count, 1.0 / live_count.astype(jnp.float32), jnp.zeros((), jnp.float32)
    )
    student_rows = student_in[0][picked]
    student_full = gather_directly(student_rows, "mp", 1)
    student_f32 = student_full.astype(jnp.float32)
    normed_rows = layer_norm(student_f32, student_gain).astype(jnp.bfloat16)
    pre_act = jnp.dot(normed_rows, widen_weight, preferred_element_type=jnp.float32)
    activity = gelu_value(pre_act).astype(jnp.bfloat16)
    branch_sum = total_of(
        jnp.dot(activity, narrow_weight, preferred_element_type=jnp.float32).astype(jnp.bfloat16),
        "mp",
    ).astype(jnp.float32)
    outputs = (student_f32 + branch_sum).astype(jnp.bfloat16)
    predicted = jnp.einsum("rd,cd->rc", outputs, target_head, preferred_element_type=jnp.float32)
    targets32 = targets.astype(jnp.float32)
    inner_sum, pred_sq, target_sq = packed_total(
        (
            jnp.sum(predicted * targets32, axis=-1),
            jnp.sum(predicted * predicted, axis=-1),
            jnp.sum(targets32 * targets32, axis=-1),
        ),
        "mp",
    )
    inv_pred = lax.rsqrt(pred_sq + EPSILON)
    inv_target = lax.rsqrt(target_sq + EPSILON)
    cosine = inner_sum * inv_pred * inv_target
    row_loss = row_weight * (1.0 - cosine)
    pred_slope = (row_weight * cosine * inv_pred * inv_pred)[:, None] * predicted - (
        row_weight * inv_pred * inv_target
    )[:, None] * targets32
    pred_slope = pred_slope.astype(jnp.bfloat16)
    back_sum = lax.psum(
        jnp.einsum("rc,cd->rd", pred_slope, target_head, preferred_element_type=jnp.float32).astype(
            jnp.bfloat16
        ),
        "mp",
    )
    back_act = jnp.einsum("rd,hd->rh", back_sum, narrow_weight, preferred_element_type=jnp.float32)
    back_pre = (back_act * gelu_slope(pre_act)).astype(jnp.bfloat16)
    column_part = normed_rows
    grad_widen = summed_on_arrival(
        jnp.einsum("rd,rh->dh", column_part, back_pre, preferred_element_type=jnp.float32), "dp", 0
    )
    column_part = back_sum
    grad_narrow = summed_on_arrival(
        jnp.einsum("rd,rh->dh", column_part, activity, preferred_element_type=jnp.float32), "dp", 0
    )
    image_loss = jnp.sum(row_loss)
    return (grad_widen, grad_narrow, jnp.reshape(image_loss, (1,)))


def solution(mesh):
    placed = (
        P("dp", "mp", None),
        P(),
        P(None, "mp", None),
        P("mp", None),
        P("dp", None, "mp"),
        P(),
        P(None, "mp"),
        P("mp", None),
        P("mp", None),
        P("dp", None),
        P("dp"),
    )
    return jax.shard_map(
        on_device,
        mesh=mesh,
        in_specs=placed,
        out_specs=(P("dp", "mp"), P("dp", "mp"), P("dp")),
        check_vma=False,
    )
```

profile of v0, /device:TPU:2, one launch (start us, length us, event | category | flops | bytes accessed | tf_op | source)
XLA Modules:
  0.0 403.2 jit_solution(8823197058762961276)
XLA Ops:
  8.7 2.0 gather_fusion
  10.9 42.5 %all_to_all.26 = bf16[8,512,128]{1,2,0:T(8,128)(2,1)S(1)} all-to-all(bf16[8,512,128]{1,2,0:T(8,128)(2,1)S(1)} %broadcast_in_dim.14), channel_id=1, replica_groups=mesh['dp'=64,'mp'=8] {'mp'}, dimensions={0} | all-to-all | bytes 2097152 | tf_op jit(solution)/shard_map/all_to_all | solution.py:21
  54.6 1.7 multiply_convert_fusion
  57.2 1.7 convolution_convert_fusion.1
  58.9 13.4 %all-gather.7.cloned.1.call-done = bf16[1,1024,1408]{2,1,0:T(8,128)(2,1)} async-done(((bf16[1,128,1408]{2,1,0:T(8,128)(2,1)}), bf16[1,1024,1408]{2,1,0:T(8,128)(2,1)}) %all-gather.7.cloned.1.call-update) | async-done | bytes 2883600 | tf_op jit(solution)/shard_map/all_gather | solution.py:107
  72.3 2.4 convert_reduce_fusion
  75.8 2.5 fusion.5
  78.3 5.5 %gather_fusion.2 = bf16[512,1408]{1,0:T(8,128)(2,1)S(1)} fusion(bf16[1024,1408]{1,0:T(8,128)(2,1)} %fusion.5, s32[1024]{0:T(1024)S(1)} %pad_clamp_fusion), kind=kCustom, calls=%fused_computation.2 | custom fusion | bytes 2885632 | tf_op jit(solution)/shard_map/gather | solution.py:116
  83.9 2.4 convolution_convert_fusion.4
  86.3 3.1 convolution_convert_fusion.2
  90.5 3.4 fusion.52
  93.9 3.0 fusion.21
  98.2 4.1 %all-to-all-start.1 = ((bf16[8,512,176]{1,2,0:T(8,128)(2,1)}), bf16[8,512,176]{1,2,0:T(8,128)(2,1)S(1)}, u32[]{:S(2)}, u32[]{:S(2)}) async-start(bf16[8,512,176]{1,2,0:T(8,128)(2,1)} %broadcast_in_dim.17), calls=%async_computation.1 | async-start | bytes 2883584 | tf_op jit(solution)/shard_map/all_to_all | solution.py:21
  102.5 22.0 %reduce-scatter.4.cloned.1.call-done = bf16[64,1024]{1,0:T(8,128)(2,1)} async-done(((bf16[512,1024]{1,0:T(8,128)(2,1)}), bf16[64,1024]{1,0:T(8,128)(2,1)}) %reduce-scatter.4.cloned.1.call-update) | async-done | bytes 131088 | tf_op jit(solution)/shard_map/reduce_scatter | solution.py:37
  124.5 6.3 %gather_fusion.1 = bf16[512,1408]{1,0:T(8,128)(2,1)} fusion(bf16[1024,1408]{1,0:T(8,128)(2,1)} %bitcast.75, s32[1024]{0:T(1024)S(1)} %pad_clamp_fusion), kind=kCustom, calls=%fused_computation.1 | custom fusion | bytes 2885632 | tf_op jit(solution)/shard_map/gather | solution.py:139
  130.8 1.9 constant_dynamic-slice_fusion
  132.7 1.7 copy.42
  134.4 35.3 %all-gather.5.cloned.1.call-done = bf16[512,1024]{1,0:T(8,128)(2,1)} async-done(((bf16[64,1024]{1,0:T(8,128)(2,1)}), bf16[512,1024]{1,0:T(8,128)(2,1)}) %all-gather.5.cloned.1.call-update) | async-done | bytes 1048592 | tf_op jit(solution)/shard_map/all_gather | solution.py:40
  169.7 2.3 copy.36
  172.0 2.5 fusion.14
  174.5 1.6 fusion.20
  177.5 4.3 %all-to-all-start.2 = ((f32[8,1,1536]{2,1,0:T(1,128)}), f32[8,1,1536]{2,1,0:T(1,128)S(1)}, u32[]{:S(2)}, u32[]{:S(2)}) async-start(f32[8,1,1536]{2,1,0:T(1,128)} %broadcast_in_dim.18), calls=%async_computation.2 | async-start | bytes 98304 | tf_op jit(solution)/shard_map/all_to_all | solution.py:21
  182.6 7.5 %all-to-all-done.2 = f32[8,1,1536]{2,1,0:T(1,128)S(1)} async-done(((f32[8,1,1536]{2,1,0:T(1,128)}), f32[8,1,1536]{2,1,0:T(1,128)S(1)}, u32[]{:S(2)}, u32[]{:S(2)}) %all-to-all-start.2) | async-done | bytes 49184 | tf_op jit(solution)/shard_map/all_to_all | solution.py:21
  190.7 2.5 convolution_convert_fusion
  193.3 77.6 %all-reduce.2.cloned.1.call-done = bf16[512,1024]{1,0:T(8,128)(2,1)} async-done(((bf16[512,1024]{1,0:T(8,128)(2,1)}), bf16[512,1024]{1,0:T(8,128)(2,1)}) %all-reduce.2.cloned.1.call-update) | async-done | bytes 1048592 | tf_op jit(solution)/shard_map/psum | solution.py:174
  270.9 4.4 %fusion.22 = f32[64,16,512]{2,1,0:T(8,128)} fusion(bf16[64,16,512]{2,1,0:T(8,128)(2,1)S(1)} %bitcast.78, bf16[512,1024]{1,0:T(8,128)(2,1)} %all-reduce.2.cloned.1.call-done, bf16[512,1024]{1,0:T(8,128)(2,1)S(1)} %copy-done, f32[512,512]{1,0:T(8,128)} %get-tuple-element.13), kind=kOutput, calls=%fused_computation.40 | convolution fusion | flops 1076363264 | bytes 6291456 | tf_op jit(solution)/shard_map/rd,rh->dh/dot_general | solution.py:184
  275.3 10.9 %all-to-all-start.3 = ((f32[64,16,512]{2,1,0:T(8,128)}), f32[64,16,512]{2,1,0:T(8,128)S(1)}, u32[]{:S(2)}, u32[]{:S(2)}) async-start(f32[64,16,512]{2,1,0:T(8,128)} %fusion.22), calls=%async_computation.3 | async-start | bytes 4194304 | tf_op jit(solution)/shard_map/all_to_all | solution.py:65
  286.2 3.4 fusion.53
  289.6 47.9 %all-to-all-done.3 = f32[64,16,512]{2,1,0:T(8,128)S(1)} async-done(((f32[64,16,512]{2,1,0:T(8,128)}), f32[64,16,512]{2,1,0:T(8,128)S(1)}, u32[]{:S(2)}, u32[]{:S(2)}) %all-to-all-start.3) | async-done | bytes 2097184 | tf_op jit(solution)/shard_map/all_to_all | solution.py:65
  337.5 5.6 %all-to-all-start.4 = ((f32[64,16,512]{2,1,0:T(8,128)}), f32[64,16,512]{2,1,0:T(8,128)}, u32[]{:S(2)}, u32[]{:S(2)}) async-start(f32[64,16,512]{2,1,0:T(8,128)} %bitcast.21), calls=%async_computation.4 | async-start | bytes 4194304 | tf_op jit(solution)/shard_map/all_to_all | solution.py:65
  343.9 50.4 %all-to-all-done.4 = f32[64,16,512]{2,1,0:T(8,128)} async-done(((f32[64,16,512]{2,1,0:T(8,128)}), f32[64,16,512]{2,1,0:T(8,128)}, u32[]{:S(2)}, u32[]{:S(2)}) %all-to-all-start.4) | async-done | bytes 2097184 | tf_op jit(solution)/shard_map/all_to_all | solution.py:65
  394.3 2.3 reduce_sum.118
  (60 shorter events, 10.3 us)
Async XLA Ops:
  7.2 50.0 %copy-start = (bf16[512,1024]{1,0:T(8,128)(2,1)S(1)}, bf16[512,1024]{1,0:T(8,128)(2,1)}, u32[]{:S(2)}) copy-start(bf16[512,1024]{1,0:T(8,128)(2,1)} %param.18) | copy-start | bytes 3145732
  7.2 65.1 %all-gather.7.cloned.1.call-start = ((), (), s32[]{:S(2)}) async-start(), calls=%async_computation.8 | async-start | bytes 3244032 | tf_op jit(solution)/shard_map/all_gather | solution.py:107
  7.9 116.6 %reduce-scatter.4.cloned.1.call-start = ((), (), s32[]{:S(2)}) async-start(), calls=%async_computation.9 | async-start | bytes 1179648 | tf_op jit(solution)/shard_map/reduce_scatter | solution.py:37
  10.9 43.1 %copy-start.11 = (f32[1024]{0:T(1024)S(1)}, f32[1024]{0:T(1024)}, u32[]{:S(2)}) copy-start(f32[1024]{0:T(1024)} %param.16) | copy-start | bytes 12292
  53.4 1.2 copy-start.13
  54.6 1.7 copy-start.7
  56.4 0.8 copy-start.9
  72.2 2.7 copy-start.1
  74.7 1.2 copy-start.10
  83.9 2.5 copy-start.12
  86.3 3.1 copy-start.2
  89.4 1.1 copy-start.14
  98.2 76.3 %all-to-all-start.1 = ((bf16[8,512,176]{1,2,0:T(8,128)(2,1)}), bf16[8,512,176]{1,2,0:T(8,128)(2,1)S(1)}, u32[]{:S(2)}, u32[]{:S(2)}) async-start(bf16[8,512,176]{1,2,0:T(8,128)(2,1)} %broadcast_in_dim.17), calls=%async_computation.1 | async-start | bytes 2883584 | tf_op jit(solution)/shard_map/all_to_all | solution.py:21
  102.3 67.4 %all-gather.5.cloned.1.call-start = ((), (), s32[]{:S(2)}) async-start(), calls=%async_computation.7 | async-start | bytes 1179648 | tf_op jit(solution)/shard_map/all_gather | solution.py:40
  174.5 1.6 copy-start.3
  174.5 1.7 copy-start.5
  176.1 0.8 copy-start.4
  176.1 14.6 %copy-start.6 = (bf16[176,1024]{1,0:T(8,128)(2,1)S(1)}, bf16[176,1024]{1,0:T(8,128)(2,1)}, u32[]{:S(2)}) copy-start(bf16[176,1024]{1,0:T(8,128)(2,1)} %param.19) | copy-start | bytes 1081348
  176.9 94.0 %copy-start.8 = (bf16[512,1024]{0,1:T(8,128)(2,1)S(1)}, bf16[512,1024]{0,1:T(8,128)(2,1)}, u32[]{:S(2)}) copy-start(bf16[512,1024]{0,1:T(8,128)(2,1)} %copy-done.7) | copy-start | bytes 3145732
  177.5 12.5 %all-to-all-start.2 = ((f32[8,1,1536]{2,1,0:T(1,128)}), f32[8,1,1536]{2,1,0:T(1,128)S(1)}, u32[]{:S(2)}, u32[]{:S(2)}) async-start(f32[8,1,1536]{2,1,0:T(1,128)} %broadcast_in_dim.18), calls=%async_computation.2 | async-start | bytes 98304 | tf_op jit(solution)/shard_map/all_to_all | solution.py:21
  181.9 89.0 %all-reduce.2.cloned.1.call-start = ((), (), s32[]{:S(2)}) async-start(), calls=%async_computation.6 | async-start | bytes 2097152 | tf_op jit(solution)/shard_map/psum | solution.py:174
  275.3 62.2 %all-to-all-start.3 = ((f32[64,16,512]{2,1,0:T(8,128)}), f32[64,16,512]{2,1,0:T(8,128)S(1)}, u32[]{:S(2)}, u32[]{:S(2)}) async-start(f32[64,16,512]{2,1,0:T(8,128)} %fusion.22), calls=%async_computation.3 | async-start | bytes 4194304 | tf_op jit(solution)/shard_map/all_to_all | solution.py:65
  337.5 56.8 %all-to-all-start.4 = ((f32[64,16,512]{2,1,0:T(8,128)}), f32[64,16,512]{2,1,0:T(8,128)}, u32[]{:S(2)}, u32[]{:S(2)}) async-start(f32[64,16,512]{2,1,0:T(8,128)} %bitcast.21), calls=%async_computation.4 | async-start | bytes 4194304 | tf_op jit(solution)/shard_map/all_to_all | solution.py:65
Sparse Core Ops, SparseCore 0:
  10.1 62.1 all-gather.6
  75.1 49.3 reduce-scatter.3
  126.6 43.0 all-gather.4
  193.4 77.4 all-reduce.1
where the time goes:
time: 404 us; the launch traced here: 403 us
  waiting for transfers between devices  255 us (63%)
  blocking collectives  42.5 us (11%)
  matrix products  28.7 us (7%)
  starting transfers between devices  25.3 us (6%)
  local copies, waits for them, and re-layouts  23.6 us (6%)
  between operations  14.7 us (4%)
  other arithmetic  13.6 us (3%)
    all_to_all x2, waiting for transfers between devices, summed_on_arrival(): tiles = lax.all_to_all(cut_along(array, dim, peers), axis, 0, 0, tiled=True)  98.3 us
    psum x1, waiting for transfers between devices, on_device(): lax.psum(jnp.einsum('rc,cd->rd', pred_slope, target_head, preferred_eleme...  77.6 us
    all_to_all x1, blocking collectives, sent_to_all(): return lax.all_to_all(copies, axis, split_axis=0, concat_axis=0, tiled=True)  42.5 us
    all_gather x1, waiting for transfers between devices, total_of(): whole = lax.all_gather(own, axis).reshape(-1, *lines.shape[1:])  35.3 us
    reduce_scatter x1, waiting for transfers between devices, total_of(): lax.psum_scatter(rows_for(lines, lax.axis_size(axis)), axis, scatter_dime...  22 us
    all_to_all x2, starting transfers between devices, summed_on_arrival(): tiles = lax.all_to_all(cut_along(array, dim, peers), axis, 0, 0, tiled=True)  16.5 us
    all_gather x1, waiting for transfers between devices, on_device(): gathered = lax.all_gather(patches_local, 'mp', axis=0, tiled=True)  13.4 us
    all_to_all x2, starting transfers between devices, sent_to_all(): return lax.all_to_all(copies, axis, split_axis=0, concat_axis=0, tiled=True)  8.45 us
  transfers between devices with their start and end apart: 8, of which 7 were waited for; matrix products, arithmetic and copies ran while one was open for 13% of the time, Pallas kernels for 0%

commit v1 on v0

v1 whole, which is shorter than its diff:
```python
import jax
import jax.numpy as jnp
from jax import lax
from jax.sharding import Mesh, PartitionSpec as P

TD = 1408
TH = 16
EPSILON = 1e-06
DP = ("z", "x", "c")
BF = jnp.bfloat16
F32 = jnp.float32


def layer_norm(values, gain):
    mean_val = jnp.mean(values, axis=-1, keepdims=True)
    centred = values - mean_val
    spread = jnp.mean(centred * centred, axis=-1, keepdims=True)
    return centred * lax.rsqrt(spread + EPSILON) * gain


def gelu_value(pre):
    return 0.5 * pre * (1.0 + lax.erf(pre * 0.7071067811865476))


def gelu_slope(pre):
    return 0.5 * (1.0 + lax.erf(pre * 0.7071067811865476)) + pre * 0.3989422804014327 * jnp.exp(
        -0.5 * pre * pre
    )


def shift(amount):
    return [(i, (i + amount) % 8) for i in range(8)]


def ring(block):
    held = [block] + [None] * 7
    right = left = block
    for step in range(1, 5):
        right = lax.ppermute(right, "mp", shift(1))
        held[step] = right
        if step < 4:
            left = lax.ppermute(left, "mp", shift(-1))
            held[8 - step] = left
    return held


def reordered(stacked, me):
    return jnp.stack(
        [lax.dynamic_index_in_dim(stacked, (me - owner) % 8, 0, False) for owner in range(8)]
    )


def to_tiles(shard, per_piece):
    rows, cols = shard.shape
    tiles = shard.reshape(rows // 8, 8, cols // 128, 128).transpose(0, 2, 1, 3)
    tiles = tiles.reshape(-1, 8, 128)
    spare = 64 * per_piece - tiles.shape[0]
    tiles = jnp.concatenate([tiles, jnp.zeros((spare, 8, 128), tiles.dtype)])
    return tiles.reshape(64, per_piece, 8, 128)


def from_tiles(pieces, rows, cols):
    count = (rows // 8) * (cols // 128)
    tiles = pieces[:, :count].reshape(8, rows // 8, cols // 128, 8, 128)
    return tiles.transpose(0, 1, 3, 2, 4).reshape(8 * rows, cols)


def on_device(
    teacher_in,
    teacher_gain,
    teacher_qkv,
    teacher_out,
    student_in,
    student_gain,
    widen_weight,
    narrow_weight,
    target_head,
    positions,
    counts,
):
    me = lax.axis_index("mp")
    at = lax.axis_index(DP)
    picked = positions[0]
    live_count = counts[0]
    head = TD // TH
    factor = head ** (-0.5)

    mine = jnp.concatenate(
        [
            lax.dynamic_index_in_dim(to_tiles(teacher_out, 4), at, 0, False),
            lax.dynamic_index_in_dim(to_tiles(target_head, 3), at, 0, False),
        ]
    )
    shares = lax.all_to_all(
        jnp.broadcast_to(mine, (8, *mine.shape)), "mp", 0, 0, tiled=True
    )
    out_full = from_tiles(lax.all_gather(shares[:, :4], DP, axis=1, tiled=True), 176, 1408)
    head_full = from_tiles(lax.all_gather(shares[:, 4:], DP, axis=1, tiled=True), 176, 1024)

    rows = student_in[0][picked]
    packed = jnp.concatenate([rows[128 * g : 128 * g + 128] for g in range(4)], axis=1)
    held = ring(jnp.concatenate([teacher_in[0], packed], axis=1))

    stacked = jnp.stack([h[:, TD:] for h in held])
    by_owner = reordered(stacked, me).reshape(8, 128, 4, 128)
    student = by_owner.transpose(2, 1, 0, 3).reshape(512, 1024)
    normed_rows = layer_norm(student.astype(F32), student_gain).astype(BF)
    pre_act = jnp.dot(normed_rows, widen_weight, preferred_element_type=F32)
    activity = gelu_value(pre_act).astype(BF)
    partial = jnp.dot(activity, narrow_weight, preferred_element_type=F32).astype(BF)
    arrived = lax.all_to_all(partial.reshape(8, 64, 1024), "mp", 0, 0, tiled=True)
    branch = jnp.sum(arrived.astype(F32), axis=0)
    own_rows = lax.dynamic_slice_in_dim(student, me * 64, 64, 0)
    outputs = (own_rows.astype(F32) + branch).astype(BF)

    weights = jnp.pad(teacher_qkv.reshape(3, 2, head, TD), ((0, 0), (0, 0), (0, 128 - head), (0, 0)))
    weights = weights.reshape(768, TD)
    made = []
    for h in held:
        normed = layer_norm(h[:, :TD].astype(F32), teacher_gain).astype(BF)
        made.append(
            jnp.einsum("pi,oi->po", normed, weights, preferred_element_type=F32).astype(BF)
        )
    made = jnp.concatenate(made)
    place = ((me - picked // 128) % 8) * 128 + picked % 128
    query = made[:, :256][place].reshape(512, 2, 128)
    key = made[:, 256:512].reshape(1024, 2, 128)
    value = made[:, 512:].reshape(1024, 2, 128)
    scores = jnp.einsum("shd,phd->hsp", query, key, preferred_element_type=F32) * factor
    soft_num = jnp.exp(scores - jnp.max(scores, axis=-1, keepdims=True))
    soft = (soft_num / jnp.sum(soft_num, axis=-1, keepdims=True)).astype(BF)
    attended = jnp.einsum("hsp,phd->shd", soft, value, preferred_element_type=F32)
    attended = attended[:, :, :head].astype(BF).reshape(8, 64, 176)
    attended = lax.all_to_all(attended, "mp", 0, 0, tiled=True)
    attended = attended.transpose(1, 0, 2).reshape(64, TD)
    own_place = lax.dynamic_slice_in_dim(place, me * 64, 64, 0)
    patches = jnp.concatenate([h[:, :TD] for h in held])
    blended = jnp.einsum("sw,ow->so", attended, out_full, preferred_element_type=F32)
    targets = (patches[own_place].astype(F32) + blended).astype(BF).astype(F32)

    slot = me * 64 + jnp.arange(64, dtype=jnp.int32)
    row_weight = jnp.where(slot < live_count, 1.0 / live_count.astype(F32), jnp.zeros((), F32))
    predicted = jnp.einsum("rd,cd->rc", outputs, head_full, preferred_element_type=F32)
    inner = jnp.sum(predicted * targets, axis=-1)
    inv_pred = lax.rsqrt(jnp.sum(predicted * predicted, axis=-1) + EPSILON)
    inv_target = lax.rsqrt(jnp.sum(targets * targets, axis=-1) + EPSILON)
    cosine = inner * inv_pred * inv_target
    row_loss = row_weight * (1.0 - cosine)
    slope = (row_weight * cosine * inv_pred * inv_pred)[:, None] * predicted - (
        row_weight * inv_pred * inv_target
    )[:, None] * targets
    back_own = jnp.dot(slope.astype(BF), head_full, preferred_element_type=F32).astype(BF)
    loss_high = row_loss.astype(BF)
    loss_low = (row_loss - loss_high.astype(F32)).astype(BF)
    extra = jnp.pad(jnp.stack([loss_high, loss_low], axis=1), ((0, 0), (0, 126)))
    back_held = jnp.stack(ring(jnp.concatenate([back_own, extra], axis=1)))
    back_held = reordered(back_held, me).reshape(512, 1152)
    image_loss = jnp.sum(back_held[:, 1024:].astype(F32))
    back = back_held[:, :1024]

    back_act = jnp.einsum("rd,hd->rh", back, narrow_weight, preferred_element_type=F32)
    back_pre = (back_act * gelu_slope(pre_act)).astype(BF)
    grad_w = jnp.einsum("rd,rh->dh", normed_rows, back_pre, preferred_element_type=F32)
    grad_n = jnp.einsum("rd,rh->dh", back, activity, preferred_element_type=F32)
    grads = jnp.concatenate(
        [grad_w.astype(BF).reshape(32, 2, 16, 512), grad_n.astype(BF).reshape(32, 2, 16, 512)], 2
    )
    core = lax.axis_index("c")
    other = lax.ppermute(
        lax.dynamic_index_in_dim(grads, 1 - core, 1, False), "c", [(0, 1), (1, 0)]
    )
    kept = lax.dynamic_index_in_dim(grads, core, 1, False).astype(F32) + other.astype(F32)
    kept = kept.astype(BF).reshape(8, 4, 32, 512)
    kept = lax.all_to_all(kept, "x", 1, 0, tiled=False)
    kept = jnp.sum(kept.astype(F32), axis=0).astype(BF)
    kept = lax.all_to_all(kept, "z", 0, 0, tiled=True)
    total = jnp.sum(kept.astype(F32), axis=0)
    return (total[:16], total[16:], jnp.reshape(image_loss, (1,)))


def solution(mesh):
    grid = Mesh(mesh.devices.reshape(8, 4, 2, 8), ("z", "x", "c", "mp"))
    placed = (
        P(DP, "mp", None),
        P(),
        P(None, "mp", None),
        P("mp", None),
        P(DP, None, "mp"),
        P(),
        P(None, "mp"),
        P("mp", None),
        P("mp", None),
        P(DP, None),
        P(DP),
    )
    return jax.shard_map(
        on_device,
        mesh=grid,
        in_specs=placed,
        out_specs=(P(DP, "mp"), P(DP, "mp"), P(DP)),
        check_vma=False,
    )
```

time: 404 us -> 288 us (0.71)
  the two profiles are of different devices: /device:TPU:2 before, /device:TPU:32 now
where the time goes in v1:
time: 288 us; the launch traced here: 287 us
  starting transfers between devices  70.9 us (25%)
  waiting for transfers between devices  60.9 us (21%)
  local copies, waits for them, and re-layouts  57.7 us (20%)
  matrix products  31.6 us (11%)
  blocking collectives  30.6 us (11%)
  other arithmetic  19.4 us (7%)
  between operations  15.7 us (5%)
    unnamed x77, local copies, waits for them, and re-layouts  29.5 us
    ppermute x6, starting transfers between devices, ring(): left = lax.ppermute(left, 'mp', shift(-1))  25.8 us
    ppermute x8, starting transfers between devices, ring(): right = lax.ppermute(right, 'mp', shift(1))  23.3 us
    all_to_all x1, blocking collectives, on_device(): kept = lax.all_to_all(kept, 'x', 1, 0, tiled=False)  19.2 us
    ppermute x8, waiting for transfers between devices, ring(): right = lax.ppermute(right, 'mp', shift(1))  19.1 us
    all_gather x1, waiting for transfers between devices, on_device(): lax.all_gather(shares[:, :4], DP, axis=1, tiled=True)  16.9 us
    all_to_all x1, blocking collectives, on_device(): lax.all_to_all(jnp.broadcast_to(mine, (8, *mine.shape)), 'mp', 0, 0, tile...  11.4 us
    dot_general x8, matrix products, on_device(): jnp.einsum('pi,oi->po', normed, weights, preferred_element_type=F32)  11 us
  transfers between devices with their start and end apart: 20, of which 13 were waited for; matrix products, arithmetic and copies ran while one was open for 31% of the time, Pallas kernels for 0%

profile of v1, /device:TPU:32, one launch (start us, length us, event | category | flops | bytes accessed | tf_op | source)
XLA Modules:
  0.0 286.8 jit_solution(16037919978966261291)
XLA Ops:
  9.5 11.4 %all_to_all.29 = bf16[8,7,8,128]{3,2,1,0:T(8,128)(2,1)S(1)} all-to-all(bf16[8,7,8,128]{3,2,1,0:T(8,128)(2,1)S(1)} %broadcast_in_dim.16), channel_id=1, replica_groups=mesh['z'=8,'x'=4,'c'=2,'mp'=8] {'mp'}, dimensions={0} | all-to-all | bytes 229376 | tf_op jit(solution)/shard_map/all_to_all | solution.py:94
  26.5 3.1 %collective-permute-start = (bf16[128,1920]{1,0:T(8,128)(2,1)}, bf16[128,1920]{1,0:T(8,128)(2,1)S(1)}, u32[]{:S(2)}, u32[]{:S(2)}) collective-permute-start(bf16[128,1920]{1,0:T(8,128)(2,1)} %get-tuple-element.14), channel_id=1, source_target_pairs={{0,1},{1,2},{2,3},{3,4},{4,5},{5,6},{6,7},{7,0},{8,9},{9,10},{10,1... | collective-permute-start | bytes 1474568 | tf_op jit(solution)/shard_map/ppermute | solution.py:39
  29.6 4.0 %collective-permute-start.4 = (bf16[128,1920]{1,0:T(8,128)(2,1)}, bf16[128,1920]{1,0:T(8,128)(2,1)S(1)}, u32[]{:S(2)}, u32[]{:S(2)}) collective-permute-start(bf16[128,1920]{1,0:T(8,128)(2,1)} %get-tuple-element.14), channel_id=1, source_target_pairs={{0,7},{1,0},{2,1},{3,2},{4,3},{5,4},{6,5},{7,6},{8,15},{9,8},{10,9... | collective-permute-start | bytes 1474568 | tf_op jit(solution)/shard_map/ppermute | solution.py:42
  33.7 3.0 %pad.10 = bf16[3,2,128,1408]{3,2,1,0:T(8,128)(2,1)} pad(bf16[3,2,88,1408]{3,2,1,0:T(8,128)(2,1)} %bitcast.200, bf16[]{:T(256)} %constant.228.clone.1), padding=0_0x0_0x0_40x0_0 | pad | bytes 3649538 | tf_op jit(solution)/shard_map/jit(_pad)/pad | solution.py:116
  38.7 3.1 %fusion.18 = bf16[1024,768]{1,0:T(8,128)(2,1)} fusion(bf16[768,1408]{1,0:T(8,128)(2,1)} %bitcast.192, bf16[1,128,1408]{2,1,0:T(8,128)(2,1)S(1)} %copy-done.5, f32[1408]{0:T(1024)S(1)} %copy-done.16, f32[128]{0:T(128)S(1)} %add_rsqrt_fusion.9, f32[128]{0:T(128)S(1)} %broadcast_multiply_fusion.8), kind=kOutput, calls=%fused_computation.44 | convolution fusion | flops 277823488 | bytes 2726400 | tf_op jit(solution)/shard_map/pi,oi->po/dot_general | solution.py:122
  43.0 2.8 collective-permute-start.1
  45.7 4.3 %collective-permute-start.5 = (bf16[128,1920]{1,0:T(8,128)(2,1)S(1)}, bf16[128,1920]{1,0:T(8,128)(2,1)S(1)}, u32[]{:S(2)}, u32[]{:S(2)}) collective-permute-start(bf16[128,1920]{1,0:T(8,128)(2,1)S(1)} %collective-permute-done.4), channel_id=1, source_target_pairs={{0,7},{1,0},{2,1},{3,2},{4,3},{5,4},{6,5},{7,6},{8,15},{9,8},{10,9... | collective-permute-start | bytes 1474568 | tf_op jit(solution)/shard_map/ppermute | solution.py:42
  50.9 3.2 %fusion.17 = bf16[1024,768]{1,0:T(8,128)(2,1)} fusion(bf16[1024,768]{1,0:T(8,128)(2,1)} %fusion.18, bf16[768,1408]{1,0:T(8,128)(2,1)} %bitcast.193, f32[1408]{0:T(1024)S(1)} %copy-done.16, f32[128]{0:T(128)S(1)} %add_rsqrt_fusion.8, f32[128]{0:T(128)S(1)} %broadcast_multiply_fusion.7, bf16[128,1920]{1,0:T(8,128)(2,1)S(1)} %collective-permute-done), kind=kOutput, calls=%fused_computation.42 | convolution fusion | flops 277823488 | bytes 2728960 | tf_op jit(solution)/shard_map/pi,oi->po/dot_general | solution.py:122
  58.1 4.6 %collective-permute-start.2 = (bf16[128,1920]{1,0:T(8,128)(2,1)S(1)}, bf16[128,1920]{1,0:T(8,128)(2,1)S(1)}, u32[]{:S(2)}, u32[]{:S(2)}) collective-permute-start(bf16[128,1920]{1,0:T(8,128)(2,1)S(1)} %collective-permute-done.1), channel_id=1, source_target_pairs={{0,1},{1,2},{2,3},{3,4},{4,5},{5,6},{6,7},{7,0},{8,9},{9,10},{10,1... | collective-permute-start | bytes 1474568 | tf_op jit(solution)/shard_map/ppermute | solution.py:39
  62.7 2.5 collective-permute-start.6
  67.6 2.6 collective-permute-done.2
  70.7 2.7 collective-permute-done.6
  73.5 4.5 %collective-permute-start.3 = (bf16[128,1920]{1,0:T(8,128)(2,1)S(1)}, bf16[128,1920]{1,0:T(8,128)(2,1)S(1)}, u32[]{:S(2)}, u32[]{:S(2)}) collective-permute-start(bf16[128,1920]{1,0:T(8,128)(2,1)S(1)} %collective-permute-done.2), channel_id=1, source_target_pairs={{0,1},{1,2},{2,3},{3,4},{4,5},{5,6},{6,7},{7,0},{8,9},{9,10},{10,1... | collective-permute-start | bytes 1474568 | tf_op jit(solution)/shard_map/ppermute | solution.py:39
  80.5 5.0 %collective-permute-done.3 = bf16[128,1920]{1,0:T(8,128)(2,1)S(1)} collective-permute-done((bf16[128,1920]{1,0:T(8,128)(2,1)S(1)}, bf16[128,1920]{1,0:T(8,128)(2,1)S(1)}, u32[]{:S(2)}, u32[]{:S(2)}) %collective-permute-start.3) | collective-permute-done | bytes 491552 | tf_op jit(solution)/shard_map/ppermute | solution.py:39
  97.9 5.7 %fusion.19 = bf16[512,2,128]{0,2,1:T(8,128)(2,1)S(1)} fusion(bf16[1024,2,128]{0,2,1:T(8,128)(2,1)S(1)} %bitcast.205, f32[2,512]{1,0:T(2,128)S(1)} %fusion.164, f32[2,512,1024]{2,1,0:T(8,128)} %copy-done.2), kind=kOutput, calls=%fused_computation.45 | convolution fusion | flops 273811456 | bytes 4984832 | tf_op jit(solution)/shard_map/hsp,phd->shd/dot_general | solution.py:132
  104.6 7.4 %all-to-all-start.2 = ((bf16[8,64,176]{2,1,0:T(8,128)(2,1)}), bf16[8,64,176]{2,1,0:T(8,128)(2,1)S(1)}, u32[]{:S(2)}, u32[]{:S(2)}) async-start(bf16[8,64,176]{2,1,0:T(8,128)(2,1)} %reshape.519), calls=%async_computation.2 | async-start | bytes 524288 | tf_op jit(solution)/shard_map/all_to_all | solution.py:134
  131.4 7.4 %fusion.5 = f32[4,128]{1,0:T(4,128)S(1)} fusion(f32[4,128]{1,0:T(4,128)S(1)} %get-tuple-element.24, bf16[8,128,4,128]{3,2,1,0:T(4,128)(2,1)S(1)} %reshape.503), kind=kLoop, calls=%fused_computation.15 | loop fusion | flops 2096640 | bytes 1052672 | tf_op jit(solution)/shard_map/reduce_sum | solution.py:17
  143.6 7.3 %all-to-all-start = ((bf16[8,64,1024]{2,1,0:T(8,128)(2,1)}), bf16[8,64,1024]{2,1,0:T(8,128)(2,1)S(1)}, u32[]{:S(2)}, u32[]{:S(2)}) async-start(bf16[8,64,1024]{2,1,0:T(8,128)(2,1)} %bitcast.202), calls=%async_computation | async-start | bytes 2097152 | tf_op jit(solution)/shard_map/all_to_all | solution.py:111
  156.0 3.1 %gather_fusion.1 = bf16[64,1408]{1,0:T(8,128)(2,1)S(1)} fusion(bf16[1024,1408]{1,0:T(8,128)(2,1)} %slice_dynamic-update-slice_fusion, s32[1024]{0:T(1024)S(1)} %pad_clamp_fusion.1), kind=kCustom, calls=%fused_computation.1 | custom fusion | bytes 360704 | tf_op jit(solution)/shard_map/gather | solution.py:139
  159.5 8.6 %all-to-all-done = bf16[8,64,1024]{2,1,0:T(8,128)(2,1)S(1)} async-done(((bf16[8,64,1024]{2,1,0:T(8,128)(2,1)}), bf16[8,64,1024]{2,1,0:T(8,128)(2,1)S(1)}, u32[]{:S(2)}, u32[]{:S(2)}) %all-to-all-start) | async-done | bytes 1048608 | tf_op jit(solution)/shard_map/all_to_all | solution.py:111
  173.9 16.9 %all-gather.5.cloned.1.call-done = bf16[8,256,8,128]{3,2,1,0:T(8,128)(2,1)} async-done(((bf16[8,4,8,128]{3,2,1,0:T(8,128)(2,1)}), bf16[8,256,8,128]{3,2,1,0:T(8,128)(2,1)}) %all-gather.5.cloned.1.call-update) | async-done | bytes 4194320 | tf_op jit(solution)/shard_map/all_gather | solution.py:97
  194.6 2.5 convolution_convert_fusion.11
  197.1 2.5 collective-permute-start.7
  199.6 4.6 %collective-permute-start.11 = (bf16[64,1152]{1,0:T(8,128)(2,1)S(1)}, bf16[64,1152]{1,0:T(8,128)(2,1)S(1)}, u32[]{:S(2)}, u32[]{:S(2)}) collective-permute-start(bf16[64,1152]{1,0:T(8,128)(2,1)S(1)} %fusion.126), channel_id=1, source_target_pairs={{0,7},{1,0},{2,1},{3,2},{4,3},{5,4},{6,5},{7,6},{8,15},{9,8},{10,9... | collective-permute-start | bytes 442376 | tf_op jit(solution)/shard_map/ppermute | solution.py:42
  208.2 5.3 %collective-permute-start.12 = (bf16[64,1152]{1,0:T(8,128)(2,1)S(1)}, bf16[64,1152]{1,0:T(8,128)(2,1)S(1)}, u32[]{:S(2)}, u32[]{:S(2)}) collective-permute-start(bf16[64,1152]{1,0:T(8,128)(2,1)S(1)} %collective-permute-done.11), channel_id=1, source_target_pairs={{0,7},{1,0},{2,1},{3,2},{4,3},{5,4},{6,5},{7,6},{8,15},{9,8},{10,9... | collective-permute-start | bytes 442376 | tf_op jit(solution)/shard_map/ppermute | solution.py:42
  216.5 5.2 %collective-permute-start.13 = (bf16[64,1152]{1,0:T(8,128)(2,1)S(1)}, bf16[64,1152]{1,0:T(8,128)(2,1)S(1)}, u32[]{:S(2)}, u32[]{:S(2)}) collective-permute-start(bf16[64,1152]{1,0:T(8,128)(2,1)S(1)} %collective-permute-done.12), channel_id=1, source_target_pairs={{0,7},{1,0},{2,1},{3,2},{4,3},{5,4},{6,5},{7,6},{8,15},{9,8},{10,9... | collective-permute-start | bytes 442376 | tf_op jit(solution)/shard_map/ppermute | solution.py:42
  224.9 6.0 %collective-permute-done.10 = bf16[64,1152]{1,0:T(8,128)(2,1)S(1)} collective-permute-done((bf16[64,1152]{1,0:T(8,128)(2,1)S(1)}, bf16[64,1152]{1,0:T(8,128)(2,1)S(1)}, u32[]{:S(2)}, u32[]{:S(2)}) %collective-permute-start.10) | collective-permute-done | bytes 147488 | tf_op jit(solution)/shard_map/ppermute | solution.py:39
  232.4 3.3 %convolution_convert_fusion.1 = bf16[1024,512]{1,0:T(8,128)(2,1)S(1)} fusion(bf16[512,1024]{1,0:T(8,128)(2,1)S(1)} %copy-done, f32[512,512]{1,0:T(8,128)} %get-tuple-element.28, bf16[512,1152]{1,0:T(8,128)(2,1)} %bitcast.210, f32[1024]{0:T(1024)S(1)} %copy-done.17, f32[512]{0:T(512)S(1)} %rsqrt_bitcast_fusion, f32[512]{0:T(512)S(1)} %get-tuple-element.23, ...), kind=kOutput, calls=%fused_computation.24 | convolution fusion | flops 1079508992 | bytes 5251072 | tf_op jit(solution)/shard_map/rd,rh->dh/dot_general | solution.py:163
  238.8 3.0 %collective-permute-done.14 = bf16[32,32,512]{2,1,0:T(8,128)(2,1)} collective-permute-done((bf16[32,32,512]{2,1,0:T(8,128)(2,1)}, bf16[32,32,512]{2,1,0:T(8,128)(2,1)}, u32[]{:S(2)}, u32[]{:S(2)}) %collective-permute-start.14) | collective-permute-done | bytes 1048608 | tf_op jit(solution)/shard_map/ppermute | solution.py:169
  243.4 19.2 %all_to_all.30 = bf16[1,8,4,32,512]{4,3,1,0,2:T(8,128)(2,1)S(1)} all-to-all(bf16[1,8,4,32,512]{4,3,1,0,2:T(8,128)(2,1)S(1)} %copy.51), channel_id=1, replica_groups=mesh['z'=8,'x'=4,'c'=2,'mp'=8] {'x'}, dimensions={2} | all-to-all | bytes 2097152 | tf_op jit(solution)/shard_map/all_to_all | solution.py:174
  263.6 5.0 %all-to-all-start.4 = ((bf16[8,32,512]{2,1,0:T(8,128)(2,1)}), bf16[8,32,512]{2,1,0:T(8,128)(2,1)S(1)}, u32[]{:S(2)}, u32[]{:S(2)}) async-start(bf16[8,32,512]{2,1,0:T(8,128)(2,1)} %reduce_sum.260), calls=%async_computation.4 | async-start | bytes 524288 | tf_op jit(solution)/shard_map/all_to_all | solution.py:176
  270.2 9.2 %all-to-all-done.4 = bf16[8,32,512]{2,1,0:T(8,128)(2,1)S(1)} async-done(((bf16[8,32,512]{2,1,0:T(8,128)(2,1)}), bf16[8,32,512]{2,1,0:T(8,128)(2,1)S(1)}, u32[]{:S(2)}, u32[]{:S(2)}) %all-to-all-start.4) | async-done | bytes 262176 | tf_op jit(solution)/shard_map/all_to_all | solution.py:176
  (195 shorter events, 92.2 us)
Async XLA Ops:
  7.2 134.8 %copy-start = (bf16[512,1024]{1,0:T(8,128)(2,1)S(1)}, bf16[512,1024]{1,0:T(8,128)(2,1)}, u32[]{:S(2)}) copy-start(bf16[512,1024]{1,0:T(8,128)(2,1)} %param.18) | copy-start | bytes 3145732
  7.2 14.4 %copy-start.14 = (s32[1,512]{1,0:T(1,128)S(1)}, s32[1,512]{1,0:T(1,128)}, u32[]{:S(2)}) copy-start(s32[1,512]{1,0:T(1,128)} %param.20) | copy-start | bytes 6148
  7.2 14.5 %copy-start.3 = (bf16[1,1024,128]{2,1,0:T(8,128)(2,1)S(1)}, bf16[1,1024,128]{2,1,0:T(8,128)(2,1)}, u32[]{:S(2)}) copy-start(bf16[1,1024,128]{2,1,0:T(8,128)(2,1)} %param.15) | copy-start | bytes 786436
  7.2 15.8 %copy-start.5 = (bf16[1,128,1408]{2,1,0:T(8,128)(2,1)S(1)}, bf16[1,128,1408]{2,1,0:T(8,128)(2,1)}, u32[]{:S(2)}) copy-start(bf16[1,128,1408]{2,1,0:T(8,128)(2,1)} %param.11) | copy-start | bytes 1081348
  7.2 161.1 %all-gather.3.cloned.1.call-start = ((), (), s32[]{:S(2)}) async-start(), calls=%async_computation.5 | async-start | bytes 3194880 | tf_op jit(solution)/shard_map/all_gather | solution.py:98
  21.6 169.2 %all-gather.5.cloned.1.call-start = ((), (), s32[]{:S(2)}) async-start(), calls=%async_computation.6 | async-start | bytes 4259840 | tf_op jit(solution)/shard_map/all_gather | solution.py:97
  26.5 15.9 %collective-permute-start = (bf16[128,1920]{1,0:T(8,128)(2,1)}, bf16[128,1920]{1,0:T(8,128)(2,1)S(1)}, u32[]{:S(2)}, u32[]{:S(2)}) collective-permute-start(bf16[128,1920]{1,0:T(8,128)(2,1)} %get-tuple-element.14), channel_id=1, source_target_pairs={{0,1},{1,2},{2,3},{3,4},{4,5},{5,6},{6,7},{7,0},{8,9},{9,10},{10,1... | collective-permute-start | bytes 1474568 | tf_op jit(solution)/shard_map/ppermute | solution.py:39
  29.6 13.3 %collective-permute-start.4 = (bf16[128,1920]{1,0:T(8,128)(2,1)}, bf16[128,1920]{1,0:T(8,128)(2,1)S(1)}, u32[]{:S(2)}, u32[]{:S(2)}) collective-permute-start(bf16[128,1920]{1,0:T(8,128)(2,1)} %get-tuple-element.14), channel_id=1, source_target_pairs={{0,7},{1,0},{2,1},{3,2},{4,3},{5,4},{6,5},{7,6},{8,15},{9,8},{10,9... | collective-permute-start | bytes 1474568 | tf_op jit(solution)/shard_map/ppermute | solution.py:42
  43.0 13.2 %collective-permute-start.1 = (bf16[128,1920]{1,0:T(8,128)(2,1)S(1)}, bf16[128,1920]{1,0:T(8,128)(2,1)S(1)}, u32[]{:S(2)}, u32[]{:S(2)}) collective-permute-start(bf16[128,1920]{1,0:T(8,128)(2,1)S(1)} %collective-permute-done), channel_id=1, source_target_pairs={{0,1},{1,2},{2,3},{3,4},{4,5},{5,6},{6,7},{7,0},{8,9},{9,10},{10,1... | collective-permute-start | bytes 1474568 | tf_op jit(solution)/shard_map/ppermute | solution.py:39
  45.7 12.2 %collective-permute-start.5 = (bf16[128,1920]{1,0:T(8,128)(2,1)S(1)}, bf16[128,1920]{1,0:T(8,128)(2,1)S(1)}, u32[]{:S(2)}, u32[]{:S(2)}) collective-permute-start(bf16[128,1920]{1,0:T(8,128)(2,1)S(1)} %collective-permute-done.4), channel_id=1, source_target_pairs={{0,7},{1,0},{2,1},{3,2},{4,3},{5,4},{6,5},{7,6},{8,15},{9,8},{10,9... | collective-permute-start | bytes 1474568 | tf_op jit(solution)/shard_map/ppermute | solution.py:42
  50.9 15.1 %copy-start.10 = (bf16[3,2,128,1408]{3,2,1,0:T(8,128)(2,1)S(1)}, bf16[3,2,128,1408]{3,2,1,0:T(8,128)(2,1)}, u32[]{:S(2)}) copy-start(bf16[3,2,128,1408]{3,2,1,0:T(8,128)(2,1)} %pad.10) | copy-start | bytes 6488068
  54.2 11.9 %copy-start.11 = (bf16[1024,768]{1,0:T(8,128)(2,1)S(1)}, bf16[1024,768]{1,0:T(8,128)(2,1)}, u32[]{:S(2)}) copy-start(bf16[1024,768]{1,0:T(8,128)(2,1)} %fusion.17) | copy-start | bytes 4718596
  58.0 56.3 %copy-start.6 = (bf16[128,1920]{1,0:T(8,128)(2,1)}, bf16[128,1920]{1,0:T(8,128)(2,1)S(1)}, u32[]{:S(2)}) copy-start(bf16[128,1920]{1,0:T(8,128)(2,1)S(1)} %collective-permute-done.5) | copy-start | bytes 1474564
  58.1 12.2 %collective-permute-start.2 = (bf16[128,1920]{1,0:T(8,128)(2,1)S(1)}, bf16[128,1920]{1,0:T(8,128)(2,1)S(1)}, u32[]{:S(2)}, u32[]{:S(2)}) collective-permute-start(bf16[128,1920]{1,0:T(8,128)(2,1)S(1)} %collective-permute-done.1), channel_id=1, source_target_pairs={{0,1},{1,2},{2,3},{3,4},{4,5},{5,6},{6,7},{7,0},{8,9},{9,10},{10,1... | collective-permute-start | bytes 1474568 | tf_op jit(solution)/shard_map/ppermute | solution.py:39
  62.7 10.7 %collective-permute-start.6 = (bf16[128,1920]{1,0:T(8,128)(2,1)S(1)}, bf16[128,1920]{1,0:T(8,128)(2,1)S(1)}, u32[]{:S(2)}, u32[]{:S(2)}) collective-permute-start(bf16[128,1920]{1,0:T(8,128)(2,1)S(1)} %collective-permute-done.5), channel_id=1, source_target_pairs={{0,7},{1,0},{2,1},{3,2},{4,3},{5,4},{6,5},{7,6},{8,15},{9,8},{10,9... | collective-permute-start | bytes 1474568 | tf_op jit(solution)/shard_map/ppermute | solution.py:42
  73.4 40.2 %copy-start.8 = (bf16[128,1920]{1,0:T(8,128)(2,1)}, bf16[128,1920]{1,0:T(8,128)(2,1)S(1)}, u32[]{:S(2)}) copy-start(bf16[128,1920]{1,0:T(8,128)(2,1)S(1)} %collective-permute-done.6) | copy-start | bytes 1474564
  73.5 11.9 %collective-permute-start.3 = (bf16[128,1920]{1,0:T(8,128)(2,1)S(1)}, bf16[128,1920]{1,0:T(8,128)(2,1)S(1)}, u32[]{:S(2)}, u32[]{:S(2)}) collective-permute-start(bf16[128,1920]{1,0:T(8,128)(2,1)S(1)} %collective-permute-done.2), channel_id=1, source_target_pairs={{0,1},{1,2},{2,3},{3,4},{4,5},{5,6},{6,7},{7,0},{8,9},{9,10},{10,1... | collective-permute-start | bytes 1474568 | tf_op jit(solution)/shard_map/ppermute | solution.py:39
  104.6 39.0 %all-to-all-start.2 = ((bf16[8,64,176]{2,1,0:T(8,128)(2,1)}), bf16[8,64,176]{2,1,0:T(8,128)(2,1)S(1)}, u32[]{:S(2)}, u32[]{:S(2)}) async-start(bf16[8,64,176]{2,1,0:T(8,128)(2,1)} %reshape.519), calls=%async_computation.2 | async-start | bytes 524288 | tf_op jit(solution)/shard_map/all_to_all | solution.py:134
  129.5 9.4 %copy-start.15 = (bf16[1024,512]{1,0:T(8,128)(2,1)S(1)}, bf16[1024,512]{1,0:T(8,128)(2,1)}, u32[]{:S(2)}) copy-start(bf16[1024,512]{1,0:T(8,128)(2,1)} %param.17) | copy-start | bytes 3145732
  130.2 10.5 %copy-start.4 = (bf16[8,128,4,128]{3,0,1,2:T(8,128)(2,1)}, bf16[8,128,4,128]{3,0,1,2:T(8,128)(2,1)S(1)}, u32[]{:S(2)}) copy-start(bf16[8,128,4,128]{3,0,1,2:T(8,128)(2,1)S(1)} %copy.42) | copy-start | bytes 3145732
  143.6 10.9 %copy-start.7 = (bf16[128,1920]{1,0:T(8,128)(2,1)S(1)}, bf16[128,1920]{1,0:T(8,128)(2,1)}, u32[]{:S(2)}) copy-start(bf16[128,1920]{1,0:T(8,128)(2,1)} %copy-done.6) | copy-start | bytes 1474564
  143.6 24.5 %all-to-all-start = ((bf16[8,64,1024]{2,1,0:T(8,128)(2,1)}), bf16[8,64,1024]{2,1,0:T(8,128)(2,1)S(1)}, u32[]{:S(2)}, u32[]{:S(2)}) async-start(bf16[8,64,1024]{2,1,0:T(8,128)(2,1)} %bitcast.202), calls=%async_computation | async-start | bytes 2097152 | tf_op jit(solution)/shard_map/all_to_all | solution.py:111
  197.1 9.1 %collective-permute-start.7 = (bf16[64,1152]{1,0:T(8,128)(2,1)S(1)}, bf16[64,1152]{1,0:T(8,128)(2,1)S(1)}, u32[]{:S(2)}, u32[]{:S(2)}) collective-permute-start(bf16[64,1152]{1,0:T(8,128)(2,1)S(1)} %fusion.126), channel_id=1, source_target_pairs={{0,1},{1,2},{2,3},{3,4},{4,5},{5,6},{6,7},{7,0},{8,9},{9,10},{10,1... | collective-permute-start | bytes 442376 | tf_op jit(solution)/shard_map/ppermute | solution.py:39
  199.6 8.6 %collective-permute-start.11 = (bf16[64,1152]{1,0:T(8,128)(2,1)S(1)}, bf16[64,1152]{1,0:T(8,128)(2,1)S(1)}, u32[]{:S(2)}, u32[]{:S(2)}) collective-permute-start(bf16[64,1152]{1,0:T(8,128)(2,1)S(1)} %fusion.126), channel_id=1, source_target_pairs={{0,7},{1,0},{2,1},{3,2},{4,3},{5,4},{6,5},{7,6},{8,15},{9,8},{10,9... | collective-permute-start | bytes 442376 | tf_op jit(solution)/shard_map/ppermute | solution.py:42
  206.2 8.3 %collective-permute-start.8 = (bf16[64,1152]{1,0:T(8,128)(2,1)S(1)}, bf16[64,1152]{1,0:T(8,128)(2,1)S(1)}, u32[]{:S(2)}, u32[]{:S(2)}) collective-permute-start(bf16[64,1152]{1,0:T(8,128)(2,1)S(1)} %collective-permute-done.7), channel_id=1, source_target_pairs={{0,1},{1,2},{2,3},{3,4},{4,5},{5,6},{6,7},{7,0},{8,9},{9,10},{10,1... | collective-permute-start | bytes 442376 | tf_op jit(solution)/shard_map/ppermute | solution.py:39
  208.2 23.2 %copy-start.19 = (bf16[512,512]{1,0:T(8,128)(2,1)S(1)}, bf16[512,512]{1,0:T(8,128)(2,1)}, u32[]{:S(2)}) copy-start(bf16[512,512]{1,0:T(8,128)(2,1)} %copy-done.18) | copy-start | bytes 1572868
  208.2 8.3 %collective-permute-start.12 = (bf16[64,1152]{1,0:T(8,128)(2,1)S(1)}, bf16[64,1152]{1,0:T(8,128)(2,1)S(1)}, u32[]{:S(2)}, u32[]{:S(2)}) collective-permute-start(bf16[64,1152]{1,0:T(8,128)(2,1)S(1)} %collective-permute-done.11), channel_id=1, source_target_pairs={{0,7},{1,0},{2,1},{3,2},{4,3},{5,4},{6,5},{7,6},{8,15},{9,8},{10,9... | collective-permute-start | bytes 442376 | tf_op jit(solution)/shard_map/ppermute | solution.py:42
  214.5 8.2 %collective-permute-start.9 = (bf16[64,1152]{1,0:T(8,128)(2,1)S(1)}, bf16[64,1152]{1,0:T(8,128)(2,1)S(1)}, u32[]{:S(2)}, u32[]{:S(2)}) collective-permute-start(bf16[64,1152]{1,0:T(8,128)(2,1)S(1)} %collective-permute-done.8), channel_id=1, source_target_pairs={{0,1},{1,2},{2,3},{3,4},{4,5},{5,6},{6,7},{7,0},{8,9},{9,10},{10,1... | collective-permute-start | bytes 442376 | tf_op jit(solution)/shard_map/ppermute | solution.py:39
  216.5 14.5 %collective-permute-start.13 = (bf16[64,1152]{1,0:T(8,128)(2,1)S(1)}, bf16[64,1152]{1,0:T(8,128)(2,1)S(1)}, u32[]{:S(2)}, u32[]{:S(2)}) collective-permute-start(bf16[64,1152]{1,0:T(8,128)(2,1)S(1)} %collective-permute-done.12), channel_id=1, source_target_pairs={{0,7},{1,0},{2,1},{3,2},{4,3},{5,4},{6,5},{7,6},{8,15},{9,8},{10,9... | collective-permute-start | bytes 442376 | tf_op jit(solution)/shard_map/ppermute | solution.py:42
  222.7 8.2 %collective-permute-start.10 = (bf16[64,1152]{1,0:T(8,128)(2,1)S(1)}, bf16[64,1152]{1,0:T(8,128)(2,1)S(1)}, u32[]{:S(2)}, u32[]{:S(2)}) collective-permute-start(bf16[64,1152]{1,0:T(8,128)(2,1)S(1)} %collective-permute-done.9), channel_id=1, source_target_pairs={{0,1},{1,2},{2,3},{3,4},{4,5},{5,6},{6,7},{7,0},{8,9},{9,10},{10,1... | collective-permute-start | bytes 442376 | tf_op jit(solution)/shard_map/ppermute | solution.py:39
  236.8 4.9 %collective-permute-start.14 = (bf16[32,32,512]{2,1,0:T(8,128)(2,1)}, bf16[32,32,512]{2,1,0:T(8,128)(2,1)}, u32[]{:S(2)}, u32[]{:S(2)}) collective-permute-start(bf16[32,32,512]{2,1,0:T(8,128)(2,1)} %fusion.25), channel_id=1, source_target_pairs={{0,8},{8,0},{1,9},{9,1},{2,10},{10,2},{3,11},{11,3},{4,12},{12,4},... | collective-permute-start | bytes 3145736 | tf_op jit(solution)/shard_map/ppermute | solution.py:169
  263.6 15.8 %all-to-all-start.4 = ((bf16[8,32,512]{2,1,0:T(8,128)(2,1)}), bf16[8,32,512]{2,1,0:T(8,128)(2,1)S(1)}, u32[]{:S(2)}, u32[]{:S(2)}) async-start(bf16[8,32,512]{2,1,0:T(8,128)(2,1)} %reduce_sum.260), calls=%async_computation.4 | async-start | bytes 524288 | tf_op jit(solution)/shard_map/all_to_all | solution.py:176
  (9 other events, 26.2 us)
Sparse Core Ops, SparseCore 0:
  21.7 84.0 all-gather.2
  109.0 81.6 all-gather.4

commit v2 on v1

v2 whole, which is shorter than its diff:
```python
import jax
import jax.numpy as jnp
from jax import lax
from jax.experimental import pallas as pl
from jax.experimental.pallas import tpu as pltpu
from jax.sharding import Mesh, PartitionSpec as P

TD = 1408
TH = 16
EPSILON = 1e-06
DP = ("z", "x", "c")
BF = jnp.bfloat16
F32 = jnp.float32


def layer_norm(values, gain):
    mean_val = jnp.mean(values, axis=-1, keepdims=True)
    centred = values - mean_val
    spread = jnp.mean(centred * centred, axis=-1, keepdims=True)
    return centred * lax.rsqrt(spread + EPSILON) * gain


def shift(amount):
    return [(i, (i + amount) % 8) for i in range(8)]


def ring(block):
    held = [block] + [None] * 7
    right = left = block
    for step in range(1, 5):
        right = lax.ppermute(right, "mp", shift(1))
        held[step] = right
        if step < 4:
            left = lax.ppermute(left, "mp", shift(-1))
            held[8 - step] = left
    return held


def reordered(stacked, me):
    return jnp.stack(
        [lax.dynamic_index_in_dim(stacked, (me - owner) % 8, 0, False) for owner in range(8)]
    )


def to_tiles(shard, per_piece):
    rows, cols = shard.shape
    tiles = shard.reshape(rows // 8, 8, cols // 128, 128).transpose(0, 2, 1, 3)
    tiles = tiles.reshape(-1, 8, 128)
    spare = 64 * per_piece - tiles.shape[0]
    tiles = jnp.concatenate([tiles, jnp.zeros((spare, 8, 128), tiles.dtype)])
    return tiles.reshape(64, per_piece, 8, 128)


def from_tiles(pieces, rows, cols):
    count = (rows // 8) * (cols // 128)
    tiles = pieces[:, :count].reshape(8, rows // 8, cols // 128, 8, 128)
    return tiles.transpose(0, 1, 3, 2, 4).reshape(8 * rows, cols)


VMEM = pl.BlockSpec(memory_space=pltpu.VMEM)
SMEM = pl.BlockSpec(memory_space=pltpu.SMEM)
LANES = (((1,), (1,)), ((), ()))


def kernel_call(body, outs, scratch=(), flops=0, scalars=0, arrays=0, moved=0, limit=32):
    return pl.pallas_call(
        body,
        out_shape=outs,
        in_specs=[SMEM] * scalars + [VMEM] * arrays,
        out_specs=[VMEM] * len(outs),
        scratch_shapes=scratch,
        compiler_params=pltpu.CompilerParams(vmem_limit_bytes=limit << 20),
        cost_estimate=pl.CostEstimate(flops=flops, bytes_accessed=moved, transcendentals=0),
    )


def project_body(block, gain, weights, made):
    values = block[:, :TD].astype(F32)
    normed = layer_norm(values, gain[...]).astype(BF)
    gap = jnp.zeros((128, 40), F32)
    for j in range(3):
        part = lax.dot_general(normed, weights[j], LANES, preferred_element_type=F32)
        part = jnp.concatenate([part[:, :88], gap, part[:, 88:], gap], axis=1)
        made[:, 256 * j : 256 * j + 256] = part.astype(BF)


def project(block, gain, weights):
    return kernel_call(
        project_body,
        [jax.ShapeDtypeStruct((128, 768), BF)],
        flops=2 * 128 * 528 * TD,
        arrays=3,
        moved=2_500_000,
    )(block, gain, weights)[0]


def attend_body(place, *refs):
    made, out = refs[:8], refs[8]
    keys, values, queries = refs[9:]
    for s in range(8):
        queries[128 * s : 128 * s + 128, :] = made[s][:, :256]
        keys[128 * s : 128 * s + 128, :] = made[s][:, 256:512]
        values[128 * s : 128 * s + 128, :] = made[s][:, 512:]

    def chunk(i, _):
        rows = pl.ds(pl.multiple_of(i * 128, 128), 128)
        spots = lax.broadcasted_iota(jnp.int32, (128, 1024), 1)
        chosen = jnp.where(spots == place[rows, :], 1.0, 0.0).astype(BF)
        query = jnp.dot(chosen, queries[...], preferred_element_type=F32).astype(BF)
        heads = []
        for h in range(2):
            lanes = slice(128 * h, 128 * h + 128)
            scores = lax.dot_general(
                query[:, lanes], keys[:, lanes], LANES, preferred_element_type=F32
            ) * ((TD // TH) ** (-0.5))
            top = jnp.max(scores, axis=-1, keepdims=True)
            num = jnp.exp(scores - top)
            soft = (num * (1.0 / jnp.sum(num, axis=-1, keepdims=True))).astype(BF)
            heads.append(jnp.dot(soft, values[:, lanes], preferred_element_type=F32)[:, :88])
        out[rows, :] = jnp.concatenate(heads, axis=1).astype(BF)
        return 0

    lax.fori_loop(0, 4, chunk, 0)


def attend(place, made):
    return kernel_call(
        attend_body,
        [jax.ShapeDtypeStruct((512, 176), BF)],
        scratch=[pltpu.VMEM((1024, 256), BF)] * 3,
        flops=2 * 512 * 1024 * (256 + 256 + 256),
        arrays=9,
        moved=4_000_000,
    )(place, *made)[0]


def pick_body(place, *refs):
    held, out = refs[:8], refs[8]
    spots = lax.broadcasted_iota(jnp.int32, (64, 128), 1)
    total = jnp.zeros((64, TD), F32)
    for s in range(8):
        chosen = jnp.where(spots + 128 * s == place[...], 1.0, 0.0).astype(BF)
        total += jnp.dot(chosen, held[s][:, :TD], preferred_element_type=F32)
    out[...] = total.astype(BF)


def pick(place, held):
    return kernel_call(
        pick_body,
        [jax.ShapeDtypeStruct((64, TD), BF)],
        flops=2 * 64 * 1024 * TD,
        arrays=9,
        moved=4_000_000,
    )(place, *held)[0]


def forward_body(me_ref, *refs):
    held, (gain, widen, narrow) = refs[:8], refs[8:11]
    normed_out, active_out, slope_out, partial_out, own_out, rows_by = refs[11:]
    me = me_ref[0]
    for s in range(8):
        owner = lax.rem(me + (8 - s), 8)
        for g in range(4):
            rows_by[owner, 128 * g : 128 * g + 128, :] = held[s][
                :, TD + 128 * g : TD + 128 * g + 128
            ]
    mine = pl.ds(pl.multiple_of(me * 64, 64), 64)
    for b in range(8):
        own_out[:, 128 * b : 128 * b + 128] = rows_by[b, mine, :]

    def chunk(i, _):
        rows = pl.ds(pl.multiple_of(i * 128, 128), 128)
        values = jnp.concatenate([rows_by[b, rows, :] for b in range(8)], axis=1).astype(F32)
        normed = layer_norm(values, gain[...]).astype(BF)
        normed_out[rows, :] = normed
        pre = jnp.dot(normed, widen[...], preferred_element_type=F32)
        half = 0.5 * (1.0 + lax.erf(pre * 0.7071067811865476))
        active = (pre * half).astype(BF)
        active_out[rows, :] = active
        slope_out[rows, :] = half + pre * 0.3989422804014327 * jnp.exp(-0.5 * pre * pre)
        partial_out[rows, :] = jnp.dot(active, narrow[...], preferred_element_type=F32).astype(BF)
        return 0

    lax.fori_loop(0, 4, chunk, 0)


def forward(me, held, gain, widen, narrow):
    return kernel_call(
        forward_body,
        [
            jax.ShapeDtypeStruct((512, 1024), BF),
            jax.ShapeDtypeStruct((512, 512), BF),
            jax.ShapeDtypeStruct((512, 512), F32),
            jax.ShapeDtypeStruct((512, 1024), BF),
            jax.ShapeDtypeStruct((64, 1024), BF),
        ],
        scratch=[pltpu.VMEM((8, 512, 128), BF)],
        flops=4 * 512 * 1024 * 512,
        scalars=1,
        arrays=11,
        moved=6_000_000,
    )(me, *held, gain, widen, narrow)


def loss_body(weight, arrived, own, attended, picked, out_full, head_full, back_out):
    branch = arrived[0].astype(F32)
    for b in range(1, 8):
        branch += arrived[b].astype(F32)
    outputs = (own[...].astype(F32) + branch).astype(BF)
    joined = jnp.concatenate([attended[b].astype(F32) for b in range(8)], axis=1).astype(BF)
    blended = lax.dot_general(joined, out_full[...], LANES, preferred_element_type=F32)
    targets = (picked[...].astype(F32) + blended).astype(BF).astype(F32)
    predicted = lax.dot_general(outputs, head_full[...], LANES, preferred_element_type=F32)
    inner = jnp.sum(predicted * targets, axis=-1, keepdims=True)
    inv_pred = lax.rsqrt(jnp.sum(predicted * predicted, axis=-1, keepdims=True) + EPSILON)
    inv_target = lax.rsqrt(jnp.sum(targets * targets, axis=-1, keepdims=True) + EPSILON)
    cosine = inner * inv_pred * inv_target
    row_weight = weight[...]
    slope = (row_weight * cosine * inv_pred * inv_pred) * predicted - (
        row_weight * inv_pred * inv_target
    ) * targets
    back = jnp.dot(slope.astype(BF), head_full[...], preferred_element_type=F32)
    back_out[:, :1024] = back.astype(BF)
    row_loss = row_weight * (1.0 - cosine)
    high = row_loss.astype(BF).astype(F32)
    lane = lax.broadcasted_iota(jnp.int32, (64, 128), 1)
    extra = jnp.where(lane == 0, high, jnp.where(lane == 1, row_loss - high, 0.0))
    back_out[:, 1024:] = extra.astype(BF)


def loss_step(weight, arrived, own, attended, picked, out_full, head_full):
    return kernel_call(
        loss_body,
        [jax.ShapeDtypeStruct((64, 1152), BF)],
        flops=2 * 64 * 1408 * (1408 + 2048),
        arrays=7,
        moved=10_000_000,
    )(weight, arrived, own, attended, picked, out_full, head_full)[0]


def on_device(
    teacher_in,
    teacher_gain,
    teacher_qkv,
    teacher_out,
    student_in,
    student_gain,
    widen_weight,
    narrow_weight,
    target_head,
    positions,
    counts,
):
    me = lax.axis_index("mp")
    at = lax.axis_index(DP)
    picked = positions[0]
    live_count = counts[0]
    head = TD // TH
    factor = head ** (-0.5)

    mine = jnp.concatenate(
        [
            lax.dynamic_index_in_dim(to_tiles(teacher_out, 4), at, 0, False),
            lax.dynamic_index_in_dim(to_tiles(target_head, 3), at, 0, False),
        ]
    )
    shares = lax.all_to_all(
        jnp.broadcast_to(mine, (8, *mine.shape)), "mp", 0, 0, tiled=True
    )
    pieces = lax.all_gather(shares, DP, axis=0).reshape(64, 8, 7, 8, 128).transpose(1, 0, 2, 3, 4)
    out_full = from_tiles(pieces[:, :, :4].reshape(8, 256, 8, 128), 176, 1408)
    head_full = from_tiles(pieces[:, :, 4:].reshape(8, 192, 8, 128), 176, 1024)

    rows = student_in[0][picked]
    packed = jnp.concatenate([rows[128 * g : 128 * g + 128] for g in range(4)], axis=1)
    held = ring(jnp.concatenate([teacher_in[0], packed], axis=1))

    here = jnp.reshape(me, (1,)).astype(jnp.int32)
    normed_rows, activity, slope_pre, partial, own_rows = forward(
        here, held, student_gain.reshape(1, -1), widen_weight, narrow_weight
    )
    arrived = lax.all_to_all(partial.reshape(8, 64, 1024), "mp", 0, 0, tiled=True)

    made = [project(h, teacher_gain.reshape(1, -1), teacher_qkv) for h in held]
    place = ((me - picked // 128) % 8) * 128 + picked % 128
    attended = attend(place.reshape(512, 1), made)
    attended = lax.all_to_all(attended.reshape(8, 64, 176), "mp", 0, 0, tiled=True)
    own_place = lax.dynamic_slice_in_dim(place, me * 64, 64, 0)
    own_patches = pick(own_place.reshape(64, 1), held)

    slot = me * 64 + jnp.arange(64, dtype=jnp.int32)
    row_weight = jnp.where(slot < live_count, 1.0 / live_count.astype(F32), jnp.zeros((), F32))
    back_own = loss_step(
        row_weight.reshape(64, 1), arrived, own_rows, attended, own_patches, out_full, head_full
    )
    back_held = jnp.stack(ring(back_own))
    back_held = reordered(back_held, me).reshape(512, 1152)
    image_loss = jnp.sum(back_held[:, 1024:].astype(F32))
    back = back_held[:, :1024]

    back_act = jnp.einsum("rd,hd->rh", back, narrow_weight, preferred_element_type=F32)
    back_pre = (back_act * slope_pre).astype(BF)
    grad_w = jnp.einsum("rd,rh->dh", normed_rows, back_pre, preferred_element_type=F32)
    grad_n = jnp.einsum("rd,rh->dh", back, activity, preferred_element_type=F32)
    grads = jnp.concatenate(
        [grad_w.astype(BF).reshape(32, 2, 16, 512), grad_n.astype(BF).reshape(32, 2, 16, 512)], 2
    )
    core = lax.axis_index("c")
    other = lax.ppermute(
        lax.dynamic_index_in_dim(grads, 1 - core, 1, False), "c", [(0, 1), (1, 0)]
    )
    kept = lax.dynamic_index_in_dim(grads, core, 1, False).astype(F32) + other.astype(F32)
    kept = kept.astype(BF).reshape(8, 4, 32, 512)
    kept = lax.all_to_all(kept, "x", 1, 0, tiled=False)
    kept = jnp.sum(kept.astype(F32), axis=0).astype(BF)
    kept = lax.all_to_all(kept, "z", 0, 0, tiled=True)
    total = jnp.sum(kept.astype(F32), axis=0)
    return (total[:16], total[16:], jnp.reshape(image_loss, (1,)))


def solution(mesh):
    grid = Mesh(mesh.devices.reshape(8, 4, 2, 8), ("z", "x", "c", "mp"))
    placed = (
        P(DP, "mp", None),
        P(),
        P(None, "mp", None),
        P("mp", None),
        P(DP, None, "mp"),
        P(),
        P(None, "mp"),
        P("mp", None),
        P("mp", None),
        P(DP, None),
        P(DP),
    )
    return jax.shard_map(
        on_device,
        mesh=grid,
        in_specs=placed,
        out_specs=(P(DP, "mp"), P(DP, "mp"), P(DP)),
        check_vma=False,
    )
```

time: 288 us -> 244 us (0.85)
  the two profiles are of different devices: /device:TPU:32 before, /device:TPU:2 now
where the time goes in v2:
time: 244 us; the launch traced here: 242 us
  starting transfers between devices  65.2 us (27%)
  waiting for transfers between devices  62.4 us (26%)
  blocking collectives  34.6 us (14%)
  local copies, waits for them, and re-layouts  32 us (13%)
  Pallas kernels  21.5 us (9%)
  between operations  15.5 us (6%)
  other arithmetic  5.84 us (2%)
  matrix products  5.28 us (2%)
    ppermute x8, waiting for transfers between devices, ring(): right = lax.ppermute(right, 'mp', shift(1))  36.5 us
    ppermute x6, starting transfers between devices, ring(): left = lax.ppermute(left, 'mp', shift(-1))  22.7 us
    ppermute x8, starting transfers between devices, ring(): right = lax.ppermute(right, 'mp', shift(1))  19.6 us
    all_to_all x1, blocking collectives, on_device(): kept = lax.all_to_all(kept, 'x', 1, 0, tiled=False)  18.5 us
    unnamed x92, local copies, waits for them, and re-layouts  18.1 us
    all_to_all x1, blocking collectives, on_device(): lax.all_to_all(jnp.broadcast_to(mine, (8, *mine.shape)), 'mp', 0, 0, tile...  16 us
    all_to_all x1, starting transfers between devices, on_device(): kept = lax.all_to_all(kept, 'z', 0, 0, tiled=True)  10.2 us
    all_to_all x1, waiting for transfers between devices, on_device(): lax.all_to_all(partial.reshape(8, 64, 1024), 'mp', 0, 0, tiled=True)  9.35 us
  transfers between devices with their start and end apart: 19, of which 13 were waited for; matrix products, arithmetic and copies ran while one was open for 5% of the time, Pallas kernels for 7%

profile of v2, /device:TPU:2, one launch (start us, length us, event | category | flops | bytes accessed | tf_op | source)
XLA Modules:
  0.0 242.4 jit_solution(16483807485688060902)
XLA Ops:
  9.4 16.0 %all_to_all.29 = bf16[8,7,8,128]{3,2,1,0:T(8,128)(2,1)} all-to-all(bf16[8,7,8,128]{3,2,1,0:T(8,128)(2,1)S(1)} %broadcast_in_dim.16), channel_id=1, replica_groups=mesh['z'=8,'x'=4,'c'=2,'mp'=8] {'mp'}, dimensions={0} | all-to-all | bytes 229376 | tf_op jit(solution)/shard_map/all_to_all | solution.py:267
  27.6 2.3 collective-permute-start
  29.9 4.7 %collective-permute-start.4 = (bf16[128,1920]{1,0:T(8,128)(2,1)S(1)}, bf16[128,1920]{1,0:T(8,128)(2,1)S(1)}, u32[]{:S(2)}, u32[]{:S(2)}) collective-permute-start(bf16[128,1920]{1,0:T(8,128)(2,1)S(1)} %constant_dynamic-update-slice_fusion.refs_0_.block), channel_id=1, source_target_pairs={{0,7},{1,0},{2,1},{3,2},{4,3},{5,4},{6,5},{7,6},{8,15},{9,8},{10,9... | collective-permute-start | bytes 1474568 | tf_op jit(solution)/shard_map/ppermute | solution.py:34
  34.7 7.4 %collective-permute-done.refs_1_.block = bf16[128,1920]{1,0:T(8,128)(2,1)S(1)} collective-permute-done((bf16[128,1920]{1,0:T(8,128)(2,1)S(1)}, bf16[128,1920]{1,0:T(8,128)(2,1)S(1)}, u32[]{:S(2)}, u32[]{:S(2)}) %collective-permute-start) | collective-permute-done | bytes 491552 | tf_op jit(solution)/shard_map/ppermute | solution.py:31
  44.0 5.1 %collective-permute-start.5 = (bf16[128,1920]{1,0:T(8,128)(2,1)S(1)}, bf16[128,1920]{1,0:T(8,128)(2,1)S(1)}, u32[]{:S(2)}, u32[]{:S(2)}) collective-permute-start(bf16[128,1920]{1,0:T(8,128)(2,1)S(1)} %collective-permute-done.4.refs_7_.block), channel_id=1, source_target_pairs={{0,7},{1,0},{2,1},{3,2},{4,3},{5,4},{6,5},{7,6},{8,15},{9,8},{10,9... | collective-permute-start | bytes 1474568 | tf_op jit(solution)/shard_map/ppermute | solution.py:34
  49.2 6.5 %collective-permute-done.1.refs_2_.block = bf16[128,1920]{1,0:T(8,128)(2,1)S(1)} collective-permute-done((bf16[128,1920]{1,0:T(8,128)(2,1)S(1)}, bf16[128,1920]{1,0:T(8,128)(2,1)S(1)}, u32[]{:S(2)}, u32[]{:S(2)}) %collective-permute-start.1) | collective-permute-done | bytes 491552 | tf_op jit(solution)/shard_map/ppermute | solution.py:31
  57.6 5.1 %collective-permute-start.6 = (bf16[128,1920]{1,0:T(8,128)(2,1)S(1)}, bf16[128,1920]{1,0:T(8,128)(2,1)S(1)}, u32[]{:S(2)}, u32[]{:S(2)}) collective-permute-start(bf16[128,1920]{1,0:T(8,128)(2,1)S(1)} %collective-permute-done.5.refs_6_.block), channel_id=1, source_target_pairs={{0,7},{1,0},{2,1},{3,2},{4,3},{5,4},{6,5},{7,6},{8,15},{9,8},{10,9... | collective-permute-start | bytes 1474568 | tf_op jit(solution)/shard_map/ppermute | solution.py:34
  62.8 5.6 %collective-permute-done.2.refs_3_.block = bf16[128,1920]{1,0:T(8,128)(2,1)S(1)} collective-permute-done((bf16[128,1920]{1,0:T(8,128)(2,1)S(1)}, bf16[128,1920]{1,0:T(8,128)(2,1)S(1)}, u32[]{:S(2)}, u32[]{:S(2)}) %collective-permute-start.2) | collective-permute-done | bytes 491552 | tf_op jit(solution)/shard_map/ppermute | solution.py:31
  76.7 3.5 %collective-permute-done.3.refs_4_.block = bf16[128,1920]{1,0:T(8,128)(2,1)S(1)} collective-permute-done((bf16[128,1920]{1,0:T(8,128)(2,1)S(1)}, bf16[128,1920]{1,0:T(8,128)(2,1)S(1)}, u32[]{:S(2)}, u32[]{:S(2)}) %collective-permute-start.3) | collective-permute-done | bytes 491552 | tf_op jit(solution)/shard_map/ppermute | solution.py:31
  81.2 5.9 %shard_map.139 = bf16[512,176]{1,0:T(8,128)(2,1)S(1)} custom-call(s32[512,1]{1,0:T(8,128)S(1)} %get-tuple-element.13.place, bf16[128,768]{1,0:T(8,128)(2,1)S(1)} %shard_map.131.refs_0_, bf16[128,768]{1,0:T(8,128)(2,1)S(1)} %shard_map.132.refs_1_, bf16[128,768]{1,0:T(8,128)(2,1)S(1)} %shard_map.133.refs_2_, bf16[128,768]{1,0:T(8,128)(2,1)S(1)} %shard_map.134.refs_3_, ...), custom_call_target="tpu_custom_call" | custom-call | flops 805306368 | bytes 4000000 | tf_op jit(solution)/shard_map/pallas_call | solution.py:127
  87.9 3.4 %all-to-all-start.1 = ((bf16[8,64,176]{2,1,0:T(8,128)(2,1)}), bf16[8,64,176]{2,1,0:T(8,128)(2,1)S(1)}, u32[]{:S(2)}, u32[]{:S(2)}) async-start(bf16[8,64,176]{2,1,0:T(8,128)(2,1)} %bitcast.84), calls=%async_computation.1 | async-start | bytes 524288 | tf_op jit(solution)/shard_map/all_to_all | solution.py:287
  95.9 3.5 %shard_map.130 = (bf16[512,1024]{1,0:T(8,128)(2,1)S(1)}, bf16[512,512]{1,0:T(8,128)(2,1)S(1)}, f32[512,512]{1,0:T(8,128)S(1)}, bf16[512,1024]{1,0:T(8,128)(2,1)S(1)}, bf16[64,1024]{1,0:T(8,128)(2,1)S(1)}) custom-call(s32[1]{0:T(128)} %bitcast.me_ref, bf16[128,1920]{1,0:T(8,128)(2,1)S(1)} %constant_dynamic-update-slice_fusion.refs_0_.block, ...), custom_call_target="tpu_custom_call" | custom-call | flops 1073741824 | bytes 6000000 | tf_op jit(solution)/shard_map/pallas_call | solution.py:188
  103.8 7.3 %all-to-all-start = ((bf16[8,64,1024]{2,1,0:T(8,128)(2,1)}), bf16[8,64,1024]{2,1,0:T(8,128)(2,1)}, u32[]{:S(2)}, u32[]{:S(2)}) async-start(bf16[8,64,1024]{2,1,0:T(8,128)(2,1)} %bitcast.83), calls=%async_computation | async-start | bytes 2097152 | tf_op jit(solution)/shard_map/all_to_all | solution.py:282
  115.4 2.5 %slice.56 = bf16[8,64,3,8,128]{4,3,2,0,1:T(8,128)(2,1)S(1)} slice(bf16[8,64,7,8,128]{4,3,2,0,1:T(8,128)(2,1)} %bitcast.88), slice={[0:8], [0:64], [4:7], [0:8], [0:128]} | slice | bytes 6291456 | tf_op jit(solution)/shard_map/slice | solution.py:272
  117.9 3.1 %slice.54 = bf16[8,64,4,8,128]{4,3,2,0,1:T(8,128)(2,1)S(1)} slice(bf16[8,64,7,8,128]{4,3,2,0,1:T(8,128)(2,1)} %bitcast.89), slice={[0:8], [0:64], [0:4], [0:8], [0:128]} | slice | bytes 8388608 | tf_op jit(solution)/shard_map/slice | solution.py:271
  121.9 2.1 slice.55
  124.8 9.3 %all-to-all-done.arrived = bf16[8,64,1024]{2,1,0:T(8,128)(2,1)} async-done(((bf16[8,64,1024]{2,1,0:T(8,128)(2,1)}), bf16[8,64,1024]{2,1,0:T(8,128)(2,1)}, u32[]{:S(2)}, u32[]{:S(2)}) %all-to-all-start) | async-done | bytes 1048608 | tf_op jit(solution)/shard_map/all_to_all | solution.py:282
  134.2 2.1 copy-done.2
  138.1 4.2 %shard_map.141 = bf16[64,1152]{1,0:T(8,128)(2,1)S(1)} custom-call(f32[64,1]{1,0:T(8,128)S(1)} %fusion.18.weight, bf16[8,64,1024]{2,1,0:T(8,128)(2,1)} %all-to-all-done.arrived, bf16[64,1024]{1,0:T(8,128)(2,1)S(1)} %copy-done.23, bf16[8,64,176]{2,1,0:T(8,128)(2,1)S(1)} %all-to-all-done.1.attended, bf16[64,1408]{1,0:T(8,128)(2,1)S(1)} %copy-done.20, ...), custom_call_target="tpu_custom_call" | custom-call | flops 622854144 | bytes 10000000 | tf_op jit(solution)/shard_map/pallas_call | solution.py:232
  142.3 1.9 collective-permute-start.11
  144.2 3.9 %collective-permute-start.7 = (bf16[64,1152]{1,0:T(8,128)(2,1)S(1)}, bf16[64,1152]{1,0:T(8,128)(2,1)S(1)}, u32[]{:S(2)}, u32[]{:S(2)}) collective-permute-start(bf16[64,1152]{1,0:T(8,128)(2,1)S(1)} %shard_map.141), channel_id=1, source_target_pairs={{0,1},{1,2},{2,3},{3,4},{4,5},{5,6},{6,7},{7,0},{8,9},{9,10},{10,1... | collective-permute-start | bytes 442376 | tf_op jit(solution)/shard_map/ppermute | solution.py:31
  148.2 2.7 %collective-permute-done.11 = bf16[64,1152]{1,0:T(8,128)(2,1)S(1)} collective-permute-done((bf16[64,1152]{1,0:T(8,128)(2,1)S(1)}, bf16[64,1152]{1,0:T(8,128)(2,1)S(1)}, u32[]{:S(2)}, u32[]{:S(2)}) %collective-permute-start.11) | collective-permute-done | bytes 147488 | tf_op jit(solution)/shard_map/ppermute | solution.py:34
  152.9 3.9 %collective-permute-start.8 = (bf16[64,1152]{1,0:T(8,128)(2,1)S(1)}, bf16[64,1152]{1,0:T(8,128)(2,1)S(1)}, u32[]{:S(2)}, u32[]{:S(2)}) collective-permute-start(bf16[64,1152]{1,0:T(8,128)(2,1)S(1)} %collective-permute-done.7), channel_id=1, source_target_pairs={{0,1},{1,2},{2,3},{3,4},{4,5},{5,6},{6,7},{7,0},{8,9},{9,10},{10,1... | collective-permute-start | bytes 442376 | tf_op jit(solution)/shard_map/ppermute | solution.py:31
  158.6 3.9 %collective-permute-start.13 = (bf16[64,1152]{1,0:T(8,128)(2,1)S(1)}, bf16[64,1152]{1,0:T(8,128)(2,1)S(1)}, u32[]{:S(2)}, u32[]{:S(2)}) collective-permute-start(bf16[64,1152]{1,0:T(8,128)(2,1)S(1)} %collective-permute-done.12), channel_id=1, source_target_pairs={{0,7},{1,0},{2,1},{3,2},{4,3},{5,4},{6,5},{7,6},{8,15},{9,8},{10,9... | collective-permute-start | bytes 442376 | tf_op jit(solution)/shard_map/ppermute | solution.py:34
  164.6 7.0 %collective-permute-done.9 = bf16[64,1152]{1,0:T(8,128)(2,1)S(1)} collective-permute-done((bf16[64,1152]{1,0:T(8,128)(2,1)S(1)}, bf16[64,1152]{1,0:T(8,128)(2,1)S(1)}, u32[]{:S(2)}, u32[]{:S(2)}) %collective-permute-start.9) | collective-permute-done | bytes 147488 | tf_op jit(solution)/shard_map/ppermute | solution.py:31
  173.5 6.3 %collective-permute-done.10 = bf16[64,1152]{1,0:T(8,128)(2,1)S(1)} collective-permute-done((bf16[64,1152]{1,0:T(8,128)(2,1)S(1)}, bf16[64,1152]{1,0:T(8,128)(2,1)S(1)}, u32[]{:S(2)}, u32[]{:S(2)}) %collective-permute-start.10) | collective-permute-done | bytes 147488 | tf_op jit(solution)/shard_map/ppermute | solution.py:31
  183.2 3.6 %convolution_convert_fusion.1 = bf16[1024,512]{1,0:T(8,128)(2,1)} fusion(bf16[512,1024]{1,0:T(8,128)(2,1)S(1)} %copy-done.26, f32[512,512]{1,0:T(8,128)S(1)} %copy-done.28, bf16[512,1024]{1,0:T(8,128)(2,1)S(1)} %copy-done.18, bf16[512,1152]{1,0:T(8,128)(2,1)} %bitcast.100), kind=kOutput, calls=%fused_computation.8 | convolution fusion | flops 1074790400 | bytes 5242880 | tf_op jit(solution)/shard_map/rd,rh->dh/dot_general | solution.py:303
  186.8 2.4 %fusion.2 = bf16[32,32,512]{2,1,0:T(8,128)(2,1)} fusion(s32[]{:T(128)S(6)} %select_n.166, bf16[32,2,16,512]{3,2,1,0:T(8,128)(2,1)} %bitcast.92, bf16[32,2,16,512]{3,2,1,0:T(8,128)(2,1)} %bitcast.90), kind=kLoop, calls=%fused_computation.10 | loop fusion | flops 2097152 | bytes 3145732 | tf_op jit(solution)/shard_map/jit(dynamic_index_in_dim)/squeeze | solution.py:310
  191.1 2.8 %collective-permute-done.14 = bf16[32,32,512]{2,1,0:T(8,128)(2,1)S(1)} collective-permute-done((bf16[32,32,512]{2,1,0:T(8,128)(2,1)}, bf16[32,32,512]{2,1,0:T(8,128)(2,1)S(1)}, u32[]{:S(2)}, u32[]{:S(2)}) %collective-permute-start.14) | collective-permute-done | bytes 1048608 | tf_op jit(solution)/shard_map/ppermute | solution.py:309
  194.4 18.5 %all_to_all.30 = bf16[1,8,4,32,512]{4,3,1,0,2:T(8,128)(2,1)S(1)} all-to-all(bf16[1,8,4,32,512]{4,3,1,0,2:T(8,128)(2,1)S(1)} %copy.63), channel_id=1, replica_groups=mesh['z'=8,'x'=4,'c'=2,'mp'=8] {'x'}, dimensions={2} | all-to-all | bytes 2097152 | tf_op jit(solution)/shard_map/all_to_all | solution.py:314
  213.9 10.2 %all-to-all-start.4 = ((bf16[8,32,512]{2,1,0:T(8,128)(2,1)}), bf16[8,32,512]{2,1,0:T(8,128)(2,1)S(1)}, u32[]{:S(2)}, u32[]{:S(2)}) async-start(bf16[8,32,512]{2,1,0:T(8,128)(2,1)} %reduce_sum.30), calls=%async_computation.4 | async-start | bytes 524288 | tf_op jit(solution)/shard_map/all_to_all | solution.py:316
  225.7 9.2 %all-to-all-done.4 = bf16[8,32,512]{2,1,0:T(8,128)(2,1)S(1)} async-done(((bf16[8,32,512]{2,1,0:T(8,128)(2,1)}), bf16[8,32,512]{2,1,0:T(8,128)(2,1)S(1)}, u32[]{:S(2)}, u32[]{:S(2)}) %all-to-all-start.4) | async-done | bytes 262176 | tf_op jit(solution)/shard_map/all_to_all | solution.py:316
  (146 shorter events, 50.6 us)
Async XLA Ops:
  7.2 19.0 %copy-start = (bf16[1,1024,128]{2,1,0:T(8,128)(2,1)S(1)}, bf16[1,1024,128]{2,1,0:T(8,128)(2,1)}, u32[]{:S(2)}) copy-start(bf16[1,1024,128]{2,1,0:T(8,128)(2,1)} %param.15) | copy-start | bytes 786436
  7.2 18.3 %copy-start.35 = (s32[1,512]{1,0:T(1,128)S(1)}, s32[1,512]{1,0:T(1,128)}, u32[]{:S(2)}) copy-start(s32[1,512]{1,0:T(1,128)} %param.20) | copy-start | bytes 6148
  7.2 108.2 %all-gather.3.cloned.1.call-start = ((), (), s32[]{:S(2)}) async-start(), calls=%async_computation.5 | async-start | bytes 7454720 | tf_op jit(solution)/shard_map/all_gather | solution.py:270
  9.4 18.1 %copy-start.33 = (bf16[1,128,1408]{2,1,0:T(8,128)(2,1)S(1)}, bf16[1,128,1408]{2,1,0:T(8,128)(2,1)}, u32[]{:S(2)}) copy-start(bf16[1,128,1408]{2,1,0:T(8,128)(2,1)} %param.11) | copy-start | bytes 1081348
  26.1 44.1 %copy-start.36 = (f32[1408]{0:T(1024)S(1)}, f32[1408]{0:T(1024)}, u32[]{:S(2)}) copy-start(f32[1408]{0:T(1024)} %param.12) | copy-start | bytes 16900
  26.1 44.2 %copy-start.1 = (bf16[3,176,1408]{2,1,0:T(8,128)(2,1)S(1)}, bf16[3,176,1408]{2,1,0:T(8,128)(2,1)}, u32[]{:S(2)}) copy-start(bf16[3,176,1408]{2,1,0:T(8,128)(2,1)} %weights.15) | copy-start | bytes 4460548
  27.6 14.5 %collective-permute-start = (bf16[128,1920]{1,0:T(8,128)(2,1)S(1)}, bf16[128,1920]{1,0:T(8,128)(2,1)S(1)}, u32[]{:S(2)}, u32[]{:S(2)}) collective-permute-start(bf16[128,1920]{1,0:T(8,128)(2,1)S(1)} %constant_dynamic-update-slice_fusion.refs_0_.block), channel_id=1, source_target_pairs={{0,1},{1,2},{2,3},{3,4},{4,5},{5,6},{6,7},{7,0},{8,9},{9,10},{10,1... | collective-permute-start | bytes 1474568 | tf_op jit(solution)/shard_map/ppermute | solution.py:31
  29.9 14.1 %collective-permute-start.4 = (bf16[128,1920]{1,0:T(8,128)(2,1)S(1)}, bf16[128,1920]{1,0:T(8,128)(2,1)S(1)}, u32[]{:S(2)}, u32[]{:S(2)}) collective-permute-start(bf16[128,1920]{1,0:T(8,128)(2,1)S(1)} %constant_dynamic-update-slice_fusion.refs_0_.block), channel_id=1, source_target_pairs={{0,7},{1,0},{2,1},{3,2},{4,3},{5,4},{6,5},{7,6},{8,15},{9,8},{10,9... | collective-permute-start | bytes 1474568 | tf_op jit(solution)/shard_map/ppermute | solution.py:34
  42.1 13.6 %collective-permute-start.1 = (bf16[128,1920]{1,0:T(8,128)(2,1)S(1)}, bf16[128,1920]{1,0:T(8,128)(2,1)S(1)}, u32[]{:S(2)}, u32[]{:S(2)}) collective-permute-start(bf16[128,1920]{1,0:T(8,128)(2,1)S(1)} %collective-permute-done.refs_1_.block), channel_id=1, source_target_pairs={{0,1},{1,2},{2,3},{3,4},{4,5},{5,6},{6,7},{7,0},{8,9},{9,10},{10,1... | collective-permute-start | bytes 1474568 | tf_op jit(solution)/shard_map/ppermute | solution.py:31
  44.0 13.6 %collective-permute-start.5 = (bf16[128,1920]{1,0:T(8,128)(2,1)S(1)}, bf16[128,1920]{1,0:T(8,128)(2,1)S(1)}, u32[]{:S(2)}, u32[]{:S(2)}) collective-permute-start(bf16[128,1920]{1,0:T(8,128)(2,1)S(1)} %collective-permute-done.4.refs_7_.block), channel_id=1, source_target_pairs={{0,7},{1,0},{2,1},{3,2},{4,3},{5,4},{6,5},{7,6},{8,15},{9,8},{10,9... | collective-permute-start | bytes 1474568 | tf_op jit(solution)/shard_map/ppermute | solution.py:34
  55.7 18.3 %copy-start.3 = (bf16[128,1920]{1,0:T(8,128)(2,1)}, bf16[128,1920]{1,0:T(8,128)(2,1)S(1)}, u32[]{:S(2)}) copy-start(bf16[128,1920]{1,0:T(8,128)(2,1)S(1)} %collective-permute-done.1.refs_2_.block) | copy-start | bytes 1474564
  55.7 12.6 %collective-permute-start.2 = (bf16[128,1920]{1,0:T(8,128)(2,1)S(1)}, bf16[128,1920]{1,0:T(8,128)(2,1)S(1)}, u32[]{:S(2)}, u32[]{:S(2)}) collective-permute-start(bf16[128,1920]{1,0:T(8,128)(2,1)S(1)} %collective-permute-done.1.refs_2_.block), channel_id=1, source_target_pairs={{0,1},{1,2},{2,3},{3,4},{4,5},{5,6},{6,7},{7,0},{8,9},{9,10},{10,1... | collective-permute-start | bytes 1474568 | tf_op jit(solution)/shard_map/ppermute | solution.py:31
  57.6 15.4 %copy-start.5 = (bf16[128,1920]{1,0:T(8,128)(2,1)}, bf16[128,1920]{1,0:T(8,128)(2,1)S(1)}, u32[]{:S(2)}) copy-start(bf16[128,1920]{1,0:T(8,128)(2,1)S(1)} %collective-permute-done.5.refs_6_.block) | copy-start | bytes 1474564
  57.6 18.2 %collective-permute-start.6 = (bf16[128,1920]{1,0:T(8,128)(2,1)S(1)}, bf16[128,1920]{1,0:T(8,128)(2,1)S(1)}, u32[]{:S(2)}, u32[]{:S(2)}) collective-permute-start(bf16[128,1920]{1,0:T(8,128)(2,1)S(1)} %collective-permute-done.5.refs_6_.block), channel_id=1, source_target_pairs={{0,7},{1,0},{2,1},{3,2},{4,3},{5,4},{6,5},{7,6},{8,15},{9,8},{10,9... | collective-permute-start | bytes 1474568 | tf_op jit(solution)/shard_map/ppermute | solution.py:34
  68.3 11.9 %collective-permute-start.3 = (bf16[128,1920]{1,0:T(8,128)(2,1)S(1)}, bf16[128,1920]{1,0:T(8,128)(2,1)S(1)}, u32[]{:S(2)}, u32[]{:S(2)}) collective-permute-start(bf16[128,1920]{1,0:T(8,128)(2,1)S(1)} %collective-permute-done.2.refs_3_.block), channel_id=1, source_target_pairs={{0,1},{1,2},{2,3},{3,4},{4,5},{5,6},{6,7},{7,0},{8,9},{9,10},{10,1... | collective-permute-start | bytes 1474568 | tf_op jit(solution)/shard_map/ppermute | solution.py:31
  81.2 10.1 %copy-start.4 = (bf16[128,1920]{1,0:T(8,128)(2,1)S(1)}, bf16[128,1920]{1,0:T(8,128)(2,1)}, u32[]{:S(2)}) copy-start(bf16[128,1920]{1,0:T(8,128)(2,1)} %copy-done.3) | copy-start | bytes 1474564
  81.2 10.1 %copy-start.6 = (bf16[128,1920]{1,0:T(8,128)(2,1)S(1)}, bf16[128,1920]{1,0:T(8,128)(2,1)}, u32[]{:S(2)}) copy-start(bf16[128,1920]{1,0:T(8,128)(2,1)} %copy-done.5) | copy-start | bytes 1474564
  81.2 10.1 %copy-start.8 = (bf16[128,1920]{1,0:T(8,128)(2,1)S(1)}, bf16[128,1920]{1,0:T(8,128)(2,1)}, u32[]{:S(2)}) copy-start(bf16[128,1920]{1,0:T(8,128)(2,1)} %copy-done.7) | copy-start | bytes 1474564
  81.2 10.1 %copy-start.24 = (f32[1024]{0:T(1024)S(1)}, f32[1024]{0:T(1024)}, u32[]{:S(2)}) copy-start(f32[1024]{0:T(1024)} %param.16) | copy-start | bytes 12292
  87.9 15.9 %all-to-all-start.1 = ((bf16[8,64,176]{2,1,0:T(8,128)(2,1)}), bf16[8,64,176]{2,1,0:T(8,128)(2,1)S(1)}, u32[]{:S(2)}, u32[]{:S(2)}) async-start(bf16[8,64,176]{2,1,0:T(8,128)(2,1)} %bitcast.84), calls=%async_computation.1 | async-start | bytes 524288 | tf_op jit(solution)/shard_map/all_to_all | solution.py:287
  103.8 30.3 %all-to-all-start = ((bf16[8,64,1024]{2,1,0:T(8,128)(2,1)}), bf16[8,64,1024]{2,1,0:T(8,128)(2,1)}, u32[]{:S(2)}, u32[]{:S(2)}) async-start(bf16[8,64,1024]{2,1,0:T(8,128)(2,1)} %bitcast.83), calls=%async_computation | async-start | bytes 2097152 | tf_op jit(solution)/shard_map/all_to_all | solution.py:282
  142.3 8.6 %collective-permute-start.11 = (bf16[64,1152]{1,0:T(8,128)(2,1)S(1)}, bf16[64,1152]{1,0:T(8,128)(2,1)S(1)}, u32[]{:S(2)}, u32[]{:S(2)}) collective-permute-start(bf16[64,1152]{1,0:T(8,128)(2,1)S(1)} %shard_map.141), channel_id=1, source_target_pairs={{0,7},{1,0},{2,1},{3,2},{4,3},{5,4},{6,5},{7,6},{8,15},{9,8},{10,9... | collective-permute-start | bytes 442376 | tf_op jit(solution)/shard_map/ppermute | solution.py:34
  144.2 8.6 %collective-permute-start.7 = (bf16[64,1152]{1,0:T(8,128)(2,1)S(1)}, bf16[64,1152]{1,0:T(8,128)(2,1)S(1)}, u32[]{:S(2)}, u32[]{:S(2)}) collective-permute-start(bf16[64,1152]{1,0:T(8,128)(2,1)S(1)} %shard_map.141), channel_id=1, source_target_pairs={{0,1},{1,2},{2,3},{3,4},{4,5},{5,6},{6,7},{7,0},{8,9},{9,10},{10,1... | collective-permute-start | bytes 442376 | tf_op jit(solution)/shard_map/ppermute | solution.py:31
  150.9 7.7 %collective-permute-start.12 = (bf16[64,1152]{1,0:T(8,128)(2,1)S(1)}, bf16[64,1152]{1,0:T(8,128)(2,1)S(1)}, u32[]{:S(2)}, u32[]{:S(2)}) collective-permute-start(bf16[64,1152]{1,0:T(8,128)(2,1)S(1)} %collective-permute-done.11), channel_id=1, source_target_pairs={{0,7},{1,0},{2,1},{3,2},{4,3},{5,4},{6,5},{7,6},{8,15},{9,8},{10,9... | collective-permute-start | bytes 442376 | tf_op jit(solution)/shard_map/ppermute | solution.py:34
  152.9 9.8 %collective-permute-start.8 = (bf16[64,1152]{1,0:T(8,128)(2,1)S(1)}, bf16[64,1152]{1,0:T(8,128)(2,1)S(1)}, u32[]{:S(2)}, u32[]{:S(2)}) collective-permute-start(bf16[64,1152]{1,0:T(8,128)(2,1)S(1)} %collective-permute-done.7), channel_id=1, source_target_pairs={{0,1},{1,2},{2,3},{3,4},{4,5},{5,6},{6,7},{7,0},{8,9},{9,10},{10,1... | collective-permute-start | bytes 442376 | tf_op jit(solution)/shard_map/ppermute | solution.py:31
  158.6 21.3 %collective-permute-start.13 = (bf16[64,1152]{1,0:T(8,128)(2,1)S(1)}, bf16[64,1152]{1,0:T(8,128)(2,1)S(1)}, u32[]{:S(2)}, u32[]{:S(2)}) collective-permute-start(bf16[64,1152]{1,0:T(8,128)(2,1)S(1)} %collective-permute-done.12), channel_id=1, source_target_pairs={{0,7},{1,0},{2,1},{3,2},{4,3},{5,4},{6,5},{7,6},{8,15},{9,8},{10,9... | collective-permute-start | bytes 442376 | tf_op jit(solution)/shard_map/ppermute | solution.py:34
  162.6 9.0 %collective-permute-start.9 = (bf16[64,1152]{1,0:T(8,128)(2,1)S(1)}, bf16[64,1152]{1,0:T(8,128)(2,1)S(1)}, u32[]{:S(2)}, u32[]{:S(2)}) collective-permute-start(bf16[64,1152]{1,0:T(8,128)(2,1)S(1)} %collective-permute-done.8), channel_id=1, source_target_pairs={{0,1},{1,2},{2,3},{3,4},{4,5},{5,6},{6,7},{7,0},{8,9},{9,10},{10,1... | collective-permute-start | bytes 442376 | tf_op jit(solution)/shard_map/ppermute | solution.py:31
  171.6 8.2 %collective-permute-start.10 = (bf16[64,1152]{1,0:T(8,128)(2,1)S(1)}, bf16[64,1152]{1,0:T(8,128)(2,1)S(1)}, u32[]{:S(2)}, u32[]{:S(2)}) collective-permute-start(bf16[64,1152]{1,0:T(8,128)(2,1)S(1)} %collective-permute-done.9), channel_id=1, source_target_pairs={{0,1},{1,2},{2,3},{3,4},{4,5},{5,6},{6,7},{7,0},{8,9},{9,10},{10,1... | collective-permute-start | bytes 442376 | tf_op jit(solution)/shard_map/ppermute | solution.py:31
  186.8 7.2 %copy-start.31 = (bf16[1024,512]{1,0:T(8,128)(2,1)S(1)}, bf16[1024,512]{1,0:T(8,128)(2,1)}, u32[]{:S(2)}) copy-start(bf16[1024,512]{1,0:T(8,128)(2,1)} %convolution_convert_fusion) | copy-start | bytes 3145732
  186.8 7.2 %copy-start.32 = (bf16[1024,512]{1,0:T(8,128)(2,1)S(1)}, bf16[1024,512]{1,0:T(8,128)(2,1)}, u32[]{:S(2)}) copy-start(bf16[1024,512]{1,0:T(8,128)(2,1)} %convolution_convert_fusion.1) | copy-start | bytes 3145732
  189.2 4.8 %collective-permute-start.14 = (bf16[32,32,512]{2,1,0:T(8,128)(2,1)}, bf16[32,32,512]{2,1,0:T(8,128)(2,1)S(1)}, u32[]{:S(2)}, u32[]{:S(2)}) collective-permute-start(bf16[32,32,512]{2,1,0:T(8,128)(2,1)} %fusion.2), channel_id=1, source_target_pairs={{0,8},{8,0},{1,9},{9,1},{2,10},{10,2},{3,11},{11,3},{4,12},{12,4},... | collective-permute-start | bytes 3145736 | tf_op jit(solution)/shard_map/ppermute | solution.py:309
  213.9 21.0 %all-to-all-start.4 = ((bf16[8,32,512]{2,1,0:T(8,128)(2,1)}), bf16[8,32,512]{2,1,0:T(8,128)(2,1)S(1)}, u32[]{:S(2)}, u32[]{:S(2)}) async-start(bf16[8,32,512]{2,1,0:T(8,128)(2,1)} %reduce_sum.30), calls=%async_computation.4 | async-start | bytes 524288 | tf_op jit(solution)/shard_map/all_to_all | solution.py:316
  (24 other events, 44.4 us)
Sparse Core Ops, SparseCore 0:
  25.6 86.3 all-gather.2

commit v3 on v2

v3 whole, which is shorter than its diff:
```python
import jax
import jax.numpy as jnp
from jax import lax
from jax.experimental import pallas as pl
from jax.experimental.pallas import tpu as pltpu
from jax.sharding import Mesh, PartitionSpec as P

TD = 1408
TH = 16
EPSILON = 1e-06
DP = ("z", "x", "c")
BF = jnp.bfloat16
F32 = jnp.float32


def layer_norm(values, gain):
    mean_val = jnp.mean(values, axis=-1, keepdims=True)
    centred = values - mean_val
    spread = jnp.mean(centred * centred, axis=-1, keepdims=True)
    return centred * lax.rsqrt(spread + EPSILON) * gain


def shift(amount):
    return [(i, (i + amount) % 8) for i in range(8)]


def ring(block):
    held = [block] + [None] * 7
    right = left = block
    for step in range(1, 5):
        right = lax.ppermute(right, "mp", shift(1))
        held[step] = right
        if step < 4:
            left = lax.ppermute(left, "mp", shift(-1))
            held[8 - step] = left
    return held


def to_tiles(shard, per_piece):
    rows, cols = shard.shape
    tiles = shard.reshape(rows // 16, 16, cols // 128, 128).transpose(0, 2, 1, 3)
    tiles = tiles.reshape(-1, 16, 128)
    spare = 16 * per_piece - tiles.shape[0]
    tiles = jnp.concatenate([tiles, jnp.zeros((spare, 16, 128), tiles.dtype)])
    return tiles.reshape(16, per_piece, 16, 128)


VMEM = pl.BlockSpec(memory_space=pltpu.VMEM)
SMEM = pl.BlockSpec(memory_space=pltpu.SMEM)
LANES = (((1,), (1,)), ((), ()))


def kernel_call(body, outs, scratch=(), flops=0, scalars=0, arrays=0, moved=0, limit=8):
    return pl.pallas_call(
        body,
        out_shape=outs,
        in_specs=[SMEM] * scalars + [VMEM] * arrays,
        out_specs=[VMEM] * len(outs),
        scratch_shapes=scratch,
        compiler_params=pltpu.CompilerParams(vmem_limit_bytes=limit << 20),
        cost_estimate=pl.CostEstimate(flops=flops, bytes_accessed=moved, transcendentals=0),
    )


def project_body(block, gain, weights, made):
    values = block[:, :TD].astype(F32)
    normed = layer_norm(values, gain[...]).astype(BF)
    gap = jnp.zeros((128, 40), F32)
    for j in range(3):
        part = lax.dot_general(normed, weights[j], LANES, preferred_element_type=F32)
        part = jnp.concatenate([part[:, :88], gap, part[:, 88:], gap], axis=1)
        made[:, 256 * j : 256 * j + 256] = part.astype(BF)


def project(block, gain, weights):
    return kernel_call(
        project_body,
        [jax.ShapeDtypeStruct((128, 768), BF)],
        flops=2 * 128 * 528 * TD,
        arrays=3,
        moved=2_500_000,
    )(block, gain, weights)[0]


def middle_body(me_ref, *refs):
    held, made, (place, gain, widen, narrow) = refs[:8], refs[8:16], refs[16:20]
    normed_out, active_out, slope_out, joint, own_out, picked_out = refs[20:26]
    rows_by, queries, keys, values = refs[26:]
    me = me_ref[0]
    mine = pl.ds(pl.multiple_of(me * 64, 64), 64)

    for s in range(8):
        owner = lax.rem(me + (8 - s), 8)
        for g in range(4):
            rows_by[owner, 128 * g : 128 * g + 128, :] = held[s][
                :, TD + 128 * g : TD + 128 * g + 128
            ]
    for b in range(8):
        own_out[:, 128 * b : 128 * b + 128] = rows_by[b, mine, :]

    spots = lax.broadcasted_iota(jnp.int32, (64, 128), 1)
    own_place = place[mine, :]
    total = jnp.zeros((64, TD), F32)
    for s in range(8):
        chosen = jnp.where(spots + 128 * s == own_place, 1.0, 0.0).astype(BF)
        total += jnp.dot(chosen, held[s][:, :TD], preferred_element_type=F32)
    picked_out[...] = total.astype(BF)

    for s in range(8):
        queries[128 * s : 128 * s + 128, :] = made[s][:, :256]
        keys[128 * s : 128 * s + 128, :] = made[s][:, 256:512]
        values[128 * s : 128 * s + 128, :] = made[s][:, 512:]

    def chunk(i, _):
        rows = pl.ds(pl.multiple_of(i * 128, 128), 128)
        student = jnp.concatenate([rows_by[b, rows, :] for b in range(8)], axis=1).astype(F32)
        normed = layer_norm(student, gain[...]).astype(BF)
        normed_out[rows, :] = normed
        pre = jnp.dot(normed, widen[...], preferred_element_type=F32)
        half = 0.5 * (1.0 + lax.erf(pre * 0.7071067811865476))
        active = (pre * half).astype(BF)
        active_out[rows, :] = active
        slope_out[rows, :] = half + pre * 0.3989422804014327 * jnp.exp(-0.5 * pre * pre)
        joint[rows, :1024] = jnp.dot(active, narrow[...], preferred_element_type=F32).astype(BF)

        spots = lax.broadcasted_iota(jnp.int32, (128, 1024), 1)
        chosen = jnp.where(spots == place[rows, :], 1.0, 0.0).astype(BF)
        query = jnp.dot(chosen, queries[...], preferred_element_type=F32).astype(BF)
        heads = []
        for h in range(2):
            lanes = slice(128 * h, 128 * h + 128)
            scores = lax.dot_general(
                query[:, lanes], keys[:, lanes], LANES, preferred_element_type=F32
            ) * ((TD // TH) ** (-0.5))
            top = jnp.max(scores, axis=-1, keepdims=True)
            num = jnp.exp(scores - top)
            soft = (num * (1.0 / jnp.sum(num, axis=-1, keepdims=True))).astype(BF)
            heads.append(jnp.dot(soft, values[:, lanes], preferred_element_type=F32)[:, :88])
        heads.append(jnp.zeros((128, 80), F32))
        joint[rows, 1024:] = jnp.concatenate(heads, axis=1).astype(BF)
        return 0

    lax.fori_loop(0, 4, chunk, 0)


def middle(me, held, made, place, gain, widen, narrow):
    return kernel_call(
        middle_body,
        [
            jax.ShapeDtypeStruct((512, 1024), BF),
            jax.ShapeDtypeStruct((512, 512), BF),
            jax.ShapeDtypeStruct((512, 512), F32),
            jax.ShapeDtypeStruct((512, 1280), BF),
            jax.ShapeDtypeStruct((64, 1024), BF),
            jax.ShapeDtypeStruct((64, TD), BF),
        ],
        scratch=[pltpu.VMEM((8, 512, 128), BF)] + [pltpu.VMEM((1024, 256), BF)] * 3,
        flops=2 * 512 * 1024 * (1024 + 768) + 2 * 64 * 1024 * TD,
        scalars=1,
        arrays=20,
        moved=12_000_000,
        limit=12,
    )(me, *held, *made, place, gain, widen, narrow)


def loss_body(weight, arrived, own, picked, out_full, head_full, back_out):
    branch = arrived[0, :, :1024].astype(F32)
    for b in range(1, 8):
        branch += arrived[b, :, :1024].astype(F32)
    outputs = (own[...].astype(F32) + branch).astype(BF)
    joined = jnp.concatenate([arrived[b, :, 1024:].astype(F32)[:, :176] for b in range(8)], axis=1).astype(BF)
    blended = lax.dot_general(joined, out_full[...], LANES, preferred_element_type=F32)
    targets = (picked[...].astype(F32) + blended).astype(BF).astype(F32)
    predicted = lax.dot_general(outputs, head_full[...], LANES, preferred_element_type=F32)
    inner = jnp.sum(predicted * targets, axis=-1, keepdims=True)
    inv_pred = lax.rsqrt(jnp.sum(predicted * predicted, axis=-1, keepdims=True) + EPSILON)
    inv_target = lax.rsqrt(jnp.sum(targets * targets, axis=-1, keepdims=True) + EPSILON)
    cosine = inner * inv_pred * inv_target
    row_weight = weight[...]
    slope = (row_weight * cosine * inv_pred * inv_pred) * predicted - (
        row_weight * inv_pred * inv_target
    ) * targets
    back = jnp.dot(slope.astype(BF), head_full[...], preferred_element_type=F32).astype(BF)
    loss = jnp.sum(row_weight * (1.0 - cosine), axis=0, keepdims=True)
    high = loss.astype(BF).astype(F32)
    lane = lax.broadcasted_iota(jnp.int32, (16, 128), 1)
    row = lax.broadcasted_iota(jnp.int32, (16, 128), 0)
    extra = jnp.where(lane == 0, high, jnp.where(lane == 1, loss - high, 0.0))
    extra = jnp.where(row == 0, extra, 0.0).astype(BF)
    for peer in range(8):
        for t in range(32):
            r, c = 16 * (t // 8), 128 * (t % 8)
            back_out[peer, t] = back[r : r + 16, c : c + 128]
        back_out[peer, 32] = extra


def loss_step(weight, arrived, own, picked, out_full, head_full):
    return kernel_call(
        loss_body,
        [jax.ShapeDtypeStruct((8, 33, 16, 128), BF)],
        flops=2 * 64 * 1408 * (1408 + 2048),
        arrays=6,
        moved=10_000_000,
    )(weight, arrived, own, picked, out_full, head_full)[0]


def assemble_body(pieces, out_full, head_full):
    def shard(y, _):
        for t in range(121):
            rows = pl.ds(pl.multiple_of(y * 176 + 16 * (t // 11), 16), 16)
            col = 128 * (t % 11)
            out_full[rows, col : col + 128] = pieces[t // 8, y, t % 8]
        for t in range(88):
            rows = pl.ds(pl.multiple_of(y * 176 + 16 * (t // 8), 16), 16)
            col = 128 * (t % 8)
            head_full[rows, col : col + 128] = pieces[t // 6, y, 8 + t % 6]
        return 0

    lax.fori_loop(0, 8, shard, 0)


def assemble(pieces):
    return kernel_call(
        assemble_body,
        [jax.ShapeDtypeStruct((TD, TD), BF), jax.ShapeDtypeStruct((TD, 1024), BF)],
        arrays=1,
        moved=14_000_000,
    )(pieces)


def tail_body(core_ref, back_in, normed, active, slope, narrow, keep, send, loss, back, pre):
    core = core_ref[0]
    for y in range(8):
        for t in range(32):
            r, c = 64 * y + 16 * (t // 8), 128 * (t % 8)
            back[r : r + 16, c : c + 128] = back_in[y, t]
    total = back_in[0, 32].astype(F32)
    for y in range(1, 8):
        total += back_in[y, 32].astype(F32)
    loss[0] = jnp.sum(total)

    def rows_chunk(i, _):
        rows = pl.ds(pl.multiple_of(i * 128, 128), 128)
        got = lax.dot_general(back[rows, :], narrow[...], LANES, preferred_element_type=F32)
        pre[rows, :] = (got * slope[rows, :]).astype(BF)
        return 0

    lax.fori_loop(0, 4, rows_chunk, 0)
    over_rows = (((0,), (0,)), ((), ()))

    def column_chunk(j, _):
        cols = pl.ds(pl.multiple_of(j * 128, 128), 128)
        grad_w = lax.dot_general(
            normed[:, cols], pre[...], over_rows, preferred_element_type=F32
        ).astype(BF)
        grad_n = lax.dot_general(
            back[:, cols], active[...], over_rows, preferred_element_type=F32
        ).astype(BF)

        def put(even, odd):
            for q in range(8):
                target = odd if q % 2 else even
                target[4 * j + q // 2, :16, :] = grad_w[16 * q : 16 * q + 16]
                target[4 * j + q // 2, 16:, :] = grad_n[16 * q : 16 * q + 16]

        pl.when(core == 0)(lambda: put(keep, send))
        pl.when(core == 1)(lambda: put(send, keep))
        return 0

    lax.fori_loop(0, 8, column_chunk, 0)


def tail(core, back, normed, active, slope, narrow):
    half = jax.ShapeDtypeStruct((32, 32, 512), BF)
    return pl.pallas_call(
        tail_body,
        out_shape=[half, half, jax.ShapeDtypeStruct((1,), F32)],
        in_specs=[SMEM] + [VMEM] * 5,
        out_specs=[VMEM, VMEM, SMEM],
        scratch_shapes=[pltpu.VMEM((512, 1024), BF), pltpu.VMEM((512, 512), BF)],
        compiler_params=pltpu.CompilerParams(vmem_limit_bytes=12 << 20),
        cost_estimate=pl.CostEstimate(
            flops=6 * 512 * 1024 * 512, bytes_accessed=8_000_000, transcendentals=0
        ),
    )(core, back, normed, active, slope, narrow)


def on_device(
    teacher_in,
    teacher_gain,
    teacher_qkv,
    teacher_out,
    student_in,
    student_gain,
    widen_weight,
    narrow_weight,
    target_head,
    positions,
    counts,
):
    me = lax.axis_index("mp")
    picked = positions[0]
    live_count = counts[0]

    rows = student_in[0][picked]
    packed = jnp.concatenate([rows[128 * g : 128 * g + 128] for g in range(4)], axis=1)
    held = ring(jnp.concatenate([teacher_in[0], packed], axis=1))

    at = lax.axis_index(("z", "c"))
    mine = jnp.concatenate(
        [
            lax.dynamic_index_in_dim(to_tiles(teacher_out, 8), at, 0, False),
            lax.dynamic_index_in_dim(to_tiles(target_head, 6), at, 0, False),
        ]
    )
    shares = lax.all_to_all(
        jnp.broadcast_to(mine, (8, *mine.shape)), "mp", 0, 0, tiled=True
    )
    shares, _, _ = lax.optimization_barrier((shares, held[1], held[7]))
    out_full, head_full = assemble(lax.all_gather(shares, ("z", "c"), axis=0))

    here = jnp.reshape(me, (1,)).astype(jnp.int32)
    made = [project(h, teacher_gain.reshape(1, -1), teacher_qkv) for h in held]
    place = ((me - picked // 128) % 8) * 128 + picked % 128
    normed_rows, activity, slope_pre, joint, own_rows, own_patches = middle(
        here,
        held,
        made,
        place.reshape(512, 1),
        student_gain.reshape(1, -1),
        widen_weight,
        narrow_weight,
    )
    arrived = lax.all_to_all(joint.reshape(8, 64, 1280), "mp", 0, 0, tiled=True)

    slot = me * 64 + jnp.arange(64, dtype=jnp.int32)
    row_weight = jnp.where(slot < live_count, 1.0 / live_count.astype(F32), jnp.zeros((), F32))
    back_own = loss_step(
        row_weight.reshape(64, 1), arrived, own_rows, own_patches, out_full, head_full
    )
    back = lax.all_to_all(back_own, "mp", 0, 0, tiled=True)

    core = jnp.reshape(lax.axis_index("c"), (1,)).astype(jnp.int32)
    keep, send, image_loss = tail(core, back, normed_rows, activity, slope_pre, narrow_weight)
    other = lax.ppermute(send, "c", [(0, 1), (1, 0)])
    kept = (keep.astype(F32) + other.astype(F32)).astype(BF)
    kept = lax.all_to_all(kept, ("z", "x"), 0, 0, tiled=True)
    total = jnp.sum(kept.astype(F32), axis=0)
    return (total[:16], total[16:], image_loss)


def solution(mesh):
    grid = Mesh(mesh.devices.reshape(8, 4, 2, 8), ("z", "x", "c", "mp"))
    placed = (
        P(DP, "mp", None),
        P(),
        P(None, "mp", None),
        P("mp", None),
        P(DP, None, "mp"),
        P(),
        P(None, "mp"),
        P("mp", None),
        P("mp", None),
        P(DP, None),
        P(DP),
    )
    return jax.shard_map(
        on_device,
        mesh=grid,
        in_specs=placed,
        out_specs=(P(DP, "mp"), P(DP, "mp"), P(DP)),
        check_vma=False,
    )
```

time: 244 us -> 235 us (0.963)
  blocking collectives: 34.6 us -> 71.9 us
  starting transfers between devices: 65.2 us -> 38.3 us
  local copies, waits for them, and re-layouts: 32 us -> 20.6 us
  matrix products: 5.28 us -> 0 us
  other arithmetic: 5.84 us -> 1.04 us
  Pallas kernels: 21.5 us -> 26.2 us
    all_to_all x2, blocking collectives: 34.6 us -> 71.9 us  [the longest x1 42.1 us: on_device(): kept = lax.all_to_all(kept, ('z', 'x'), 0, 0, tiled=True)]
    ppermute x8 -> x4, starting transfers between devices: 19.6 us -> 9.85 us  [ring(): right = lax.ppermute(right, 'mp', shift(1))]
    ppermute x6 -> x3, starting transfers between devices: 22.7 us -> 13.2 us  [ring(): left = lax.ppermute(left, 'mp', shift(-1))]
    slice x7 -> x1, local copies, waits for them, and re-layouts: 10 us -> 0.63 us  [on_device(): return (total[:16], total[16:], image_loss)]
    all_to_all x3 -> x2, starting transfers between devices: 20.9 us -> 13.3 us  [the longest x1 7.23 us: on_device(): lax.all_to_all(jnp.broadcast_to(mine, (8, *mine.shape)), 'mp', 0, 0, tile...]
    dot_general x2 -> x0, matrix products: 5.28 us -> none  [the longest x1 3.56 us: on_device(): jnp.einsum('rd,rh->dh', normed_rows, back_pre, preferred_element_type=F32)]
    pallas_call x4, Pallas kernels: 14.2 us -> 18.9 us  [the longest x1 8.98 us: middle(): kernel_call(middle_body, [jax.ShapeDtypeStruct((512, 1024), BF), jax.Shap...]
    ppermute x6 -> x3, waiting for transfers between devices: 4.52 us -> 0.01 us  [ring(): left = lax.ppermute(left, 'mp', shift(-1))]
  transfers between devices with their start and end apart: 19 -> 11, of which waited for: 13 -> 6; matrix products, arithmetic and copies ran while one was open for 5% -> 1% of each run, Pallas kernels for 7% -> 7%
where the time goes in v3:
time: 235 us; the launch traced here: 234 us
  blocking collectives  71.9 us (31%)
  waiting for transfers between devices  61.1 us (26%)
  starting transfers between devices  38.3 us (16%)
  Pallas kernels  26.2 us (11%)
  local copies, waits for them, and re-layouts  20.6 us (9%)
  between operations  15.3 us (7%)
    all_to_all x1, blocking collectives, on_device(): kept = lax.all_to_all(kept, ('z', 'x'), 0, 0, tiled=True)  42.1 us
    ppermute x4, waiting for transfers between devices, ring(): right = lax.ppermute(right, 'mp', shift(1))  35.4 us
    all_to_all x1, blocking collectives, on_device(): back = lax.all_to_all(back_own, 'mp', 0, 0, tiled=True)  29.7 us
    all_to_all x1, waiting for transfers between devices, on_device(): arrived = lax.all_to_all(joint.reshape(8, 64, 1280), 'mp', 0, 0, tiled=True)  23 us
    unnamed x57, local copies, waits for them, and re-layouts  15.8 us
    ppermute x3, starting transfers between devices, ring(): left = lax.ppermute(left, 'mp', shift(-1))  13.2 us
    ppermute x4, starting transfers between devices, ring(): right = lax.ppermute(right, 'mp', shift(1))  9.85 us
    pallas_call x1, Pallas kernels, middle(): kernel_call(middle_body, [jax.ShapeDtypeStruct((512, 1024), BF), jax.Shap...  8.98 us
  transfers between devices with their start and end apart: 11, of which 6 were waited for; matrix products, arithmetic and copies ran while one was open for 1% of the time, Pallas kernels for 7%

profile of v3, /device:TPU:2, one launch (start us, length us, event | category | flops | bytes accessed | tf_op | source)
XLA Modules:
  0.0 234.2 jit_solution(15379177568721263367)
XLA Ops:
  7.2 1.5 reshape.225
  10.0 7.2 %all-to-all-start.1 = ((bf16[8,14,16,128]{3,2,1,0:T(8,128)(2,1)}), bf16[8,14,16,128]{3,2,1,0:T(8,128)(2,1)}, u32[]{:S(2)}, u32[]{:S(2)}) async-start(bf16[8,14,16,128]{3,2,1,0:T(8,128)(2,1)} %broadcast_in_dim.16), calls=%async_computation.1 | async-start | bytes 917504 | tf_op jit(solution)/shard_map/all_to_all | solution.py:316
  17.9 1.3 gather_fusion
  19.4 3.9 %collective-permute-start = (bf16[128,1920]{1,0:T(8,128)(2,1)S(1)}, bf16[128,1920]{1,0:T(8,128)(2,1)S(1)}, u32[]{:S(2)}, u32[]{:S(2)}) collective-permute-start(bf16[128,1920]{1,0:T(8,128)(2,1)S(1)} %slice_dynamic-update-slice_fusion.block.refs_0_), channel_id=1, source_target_pairs={{0,1},{1,2},{2,3},{3,4},{4,5},{5,6},{6,7},{7,0},{8,9},{9,10},{10,1... | collective-permute-start | bytes 1474568 | tf_op jit(solution)/shard_map/ppermute | solution.py:31
  23.3 3.2 %collective-permute-start.4 = (bf16[128,1920]{1,0:T(8,128)(2,1)S(1)}, bf16[128,1920]{1,0:T(8,128)(2,1)S(1)}, u32[]{:S(2)}, u32[]{:S(2)}) collective-permute-start(bf16[128,1920]{1,0:T(8,128)(2,1)S(1)} %slice_dynamic-update-slice_fusion.block.refs_0_), channel_id=1, source_target_pairs={{0,7},{1,0},{2,1},{3,2},{4,3},{5,4},{6,5},{7,6},{8,15},{9,8},{10,9... | collective-permute-start | bytes 1474568 | tf_op jit(solution)/shard_map/ppermute | solution.py:34
  26.4 14.7 %collective-permute-done.block.refs_1_ = bf16[128,1920]{1,0:T(8,128)(2,1)S(1)} collective-permute-done((bf16[128,1920]{1,0:T(8,128)(2,1)S(1)}, bf16[128,1920]{1,0:T(8,128)(2,1)S(1)}, u32[]{:S(2)}, u32[]{:S(2)}) %collective-permute-start) | collective-permute-done | bytes 491552 | tf_op jit(solution)/shard_map/ppermute | solution.py:31
  41.2 2.2 collective-permute-start.1
  43.3 4.9 %collective-permute-start.5 = (bf16[128,1920]{1,0:T(8,128)(2,1)S(1)}, bf16[128,1920]{1,0:T(8,128)(2,1)S(1)}, u32[]{:S(2)}, u32[]{:S(2)}) collective-permute-start(bf16[128,1920]{1,0:T(8,128)(2,1)S(1)} %collective-permute-done.4.block.refs_7_), channel_id=1, source_target_pairs={{0,7},{1,0},{2,1},{3,2},{4,3},{5,4},{6,5},{7,6},{8,15},{9,8},{10,9... | collective-permute-start | bytes 1474568 | tf_op jit(solution)/shard_map/ppermute | solution.py:34
  48.3 8.2 %collective-permute-done.1.block.refs_2_ = bf16[128,1920]{1,0:T(8,128)(2,1)S(1)} collective-permute-done((bf16[128,1920]{1,0:T(8,128)(2,1)S(1)}, bf16[128,1920]{1,0:T(8,128)(2,1)S(1)}, u32[]{:S(2)}, u32[]{:S(2)}) %collective-permute-start.1) | collective-permute-done | bytes 491552 | tf_op jit(solution)/shard_map/ppermute | solution.py:31
  56.5 1.9 collective-permute-start.2
  58.4 5.1 %collective-permute-start.6 = (bf16[128,1920]{1,0:T(8,128)(2,1)S(1)}, bf16[128,1920]{1,0:T(8,128)(2,1)S(1)}, u32[]{:S(2)}, u32[]{:S(2)}) collective-permute-start(bf16[128,1920]{1,0:T(8,128)(2,1)S(1)} %collective-permute-done.5.block.refs_6_), channel_id=1, source_target_pairs={{0,7},{1,0},{2,1},{3,2},{4,3},{5,4},{6,5},{7,6},{8,15},{9,8},{10,9... | collective-permute-start | bytes 1474568 | tf_op jit(solution)/shard_map/ppermute | solution.py:34
  63.5 7.3 %collective-permute-done.2.block.refs_3_ = bf16[128,1920]{1,0:T(8,128)(2,1)S(1)} collective-permute-done((bf16[128,1920]{1,0:T(8,128)(2,1)S(1)}, bf16[128,1920]{1,0:T(8,128)(2,1)S(1)}, u32[]{:S(2)}, u32[]{:S(2)}) %collective-permute-start.2) | collective-permute-done | bytes 491552 | tf_op jit(solution)/shard_map/ppermute | solution.py:31
  70.8 1.9 collective-permute-start.3
  79.2 5.2 %collective-permute-done.3.block.refs_4_ = bf16[128,1920]{1,0:T(8,128)(2,1)S(1)} collective-permute-done((bf16[128,1920]{1,0:T(8,128)(2,1)S(1)}, bf16[128,1920]{1,0:T(8,128)(2,1)S(1)}, u32[]{:S(2)}, u32[]{:S(2)}) %collective-permute-start.3) | collective-permute-done | bytes 491552 | tf_op jit(solution)/shard_map/ppermute | solution.py:31
  85.3 9.0 %shard_map.138 = (bf16[512,1024]{1,0:T(8,128)(2,1)S(1)}, bf16[512,512]{1,0:T(8,128)(2,1)S(1)}, f32[512,512]{1,0:T(8,128)S(1)}, bf16[512,1280]{1,0:T(8,128)(2,1)S...) custom-call(s32[1]{0:T(128)} %bitcast.2.me_ref, ...), custom_call_target="tpu_custom_call" | custom-call | flops 2063597568 | bytes 12000000 | tf_op jit(solution)/shard_map/pallas_call | solution.py:147
  94.3 1.1 copy-done.7
  96.8 1.0 copy-done.16
  97.7 1.0 copy-done.18
  99.5 6.0 %all-to-all-start = ((bf16[8,64,1280]{2,1,0:T(8,128)(2,1)}), bf16[8,64,1280]{2,1,0:T(8,128)(2,1)S(1)}, u32[]{:S(2)}, u32[]{:S(2)}) async-start(bf16[8,64,1280]{2,1,0:T(8,128)(2,1)} %bitcast.30), calls=%async_computation | async-start | bytes 2621440 | tf_op jit(solution)/shard_map/all_to_all | solution.py:334
  106.3 3.1 %copy-done.2 = bf16[128,14,16,128]{3,2,1,0:T(8,128)(2,1)S(1)} copy-done((bf16[128,14,16,128]{3,2,1,0:T(8,128)(2,1)S(1)}, bf16[128,14,16,128]{3,2,1,0:T(8,128)(2,1)}, u32[]{:S(2)}) %copy-start.2) | copy-done | bytes 7340056
  109.3 1.2 shard_map.139
  110.6 1.9 copy-done.3
  112.5 1.6 copy-done.5
  114.0 23.0 %all-to-all-done.arrived = bf16[8,64,1280]{2,1,0:T(8,128)(2,1)S(1)} async-done(((bf16[8,64,1280]{2,1,0:T(8,128)(2,1)}), bf16[8,64,1280]{2,1,0:T(8,128)(2,1)S(1)}, u32[]{:S(2)}, u32[]{:S(2)}) %all-to-all-start) | async-done | bytes 1310752 | tf_op jit(solution)/shard_map/all_to_all | solution.py:334
  137.0 2.1 copy-done.4
  139.2 1.8 copy-done.6
  141.0 3.0 %shard_map.140 = bf16[8,33,16,128]{3,2,1,0:T(8,128)(2,1)S(1)} custom-call(f32[64,1]{1,0:T(8,128)S(1)} %fusion.6.weight, bf16[8,64,1280]{2,1,0:T(8,128)(2,1)S(1)} %all-to-all-done.arrived, bf16[64,1024]{1,0:T(8,128)(2,1)S(1)} %copy-done.14, bf16[64,1408]{1,0:T(8,128)(2,1)S(1)} %copy-done.12, bf16[1408,1408]{1,0:T(8,128)(2,1)S(1)} %copy-done.4, ...), custom_call_target="tpu_custom_call" | custom-call | flops 622854144 | bytes 10000000 | tf_op jit(solution)/shard_map/pallas_call | solution.py:198
  144.0 29.7 %all_to_all.20.back_in = bf16[8,33,16,128]{3,2,1,0:T(8,128)(2,1)S(1)} all-to-all(bf16[8,33,16,128]{3,2,1,0:T(8,128)(2,1)S(1)} %shard_map.140), channel_id=1, replica_groups=mesh['z'=8,'x'=4,'c'=2,'mp'=8] {'mp'}, dimensions={0} | all-to-all | bytes 2162688 | tf_op jit(solution)/shard_map/all_to_all | solution.py:341
  173.7 5.8 %shard_map.141 = (bf16[32,32,512]{2,1,0:T(8,128)(2,1)S(1)}, bf16[32,32,512]{2,1,0:T(8,128)(2,1)S(1)}, f32[1]{0:T(128)}) custom-call(s32[1]{0:T(128)} %bitcast.core_ref, bf16[8,33,16,128]{3,2,1,0:T(8,128)(2,1)S(1)} %all_to_all.20.back_in, bf16[512,1024]{1,0:T(8,128)(2,1)S(1)} %copy-done.17, bf16[512,512]{1,0:T(8,128)(2,1)S(1)} %copy-done.21, ...), custom_call_target="tpu_custom_call" | custom-call | flops 1610612736 | bytes 8000000 | tf_op jit(solution)/shard_map/pallas_call | solution.py:275
  179.5 1.9 collective-permute-start.7
  181.4 2.6 %collective-permute-done.7 = bf16[32,32,512]{2,1,0:T(8,128)(2,1)S(1)} collective-permute-done((bf16[32,32,512]{2,1,0:T(8,128)(2,1)S(1)}, bf16[32,32,512]{2,1,0:T(8,128)(2,1)S(1)}, u32[]{:S(2)}, u32[]{:S(2)}) %collective-permute-start.7) | collective-permute-done | bytes 1048608 | tf_op jit(solution)/shard_map/ppermute | solution.py:345
  184.5 42.1 %all_to_all.21 = bf16[32,32,512]{2,1,0:T(8,128)(2,1)S(1)} all-to-all(bf16[32,32,512]{2,1,0:T(8,128)(2,1)S(1)} %add_convert_fusion), channel_id=1, replica_groups=mesh['z'=8,'x'=4,'c'=2,'mp'=8] {'z','x'}, dimensions={0} | all-to-all | bytes 2097152 | tf_op jit(solution)/shard_map/all_to_all | solution.py:347
  (82 shorter events, 12.7 us)
Async XLA Ops:
  7.2 10.8 %copy-start = (bf16[1,1024,128]{2,1,0:T(8,128)(2,1)S(1)}, bf16[1,1024,128]{2,1,0:T(8,128)(2,1)}, u32[]{:S(2)}) copy-start(bf16[1,1024,128]{2,1,0:T(8,128)(2,1)} %param.15) | copy-start | bytes 786436
  7.2 1.6 copy-start.22
  8.9 8.4 %copy-start.25 = (s32[1,512]{1,0:T(1,128)S(1)}, s32[1,512]{1,0:T(1,128)}, u32[]{:S(2)}) copy-start(s32[1,512]{1,0:T(1,128)} %param.20) | copy-start | bytes 6148
  9.0 8.9 %copy-start.23 = (bf16[1,128,1408]{2,1,0:T(8,128)(2,1)S(1)}, bf16[1,128,1408]{2,1,0:T(8,128)(2,1)}, u32[]{:S(2)}) copy-start(bf16[1,128,1408]{2,1,0:T(8,128)(2,1)} %param.11) | copy-start | bytes 1081348
  10.0 62.8 %copy-start.24 = (f32[1408]{0:T(1024)S(1)}, f32[1408]{0:T(1024)}, u32[]{:S(2)}) copy-start(f32[1408]{0:T(1024)} %param.12) | copy-start | bytes 16900
  10.0 62.8 %copy-start.1 = (bf16[3,176,1408]{2,1,0:T(8,128)(2,1)S(1)}, bf16[3,176,1408]{2,1,0:T(8,128)(2,1)}, u32[]{:S(2)}) copy-start(bf16[3,176,1408]{2,1,0:T(8,128)(2,1)} %weights.15) | copy-start | bytes 4460548
  10.0 31.2 %all-to-all-start.1 = ((bf16[8,14,16,128]{3,2,1,0:T(8,128)(2,1)}), bf16[8,14,16,128]{3,2,1,0:T(8,128)(2,1)}, u32[]{:S(2)}, u32[]{:S(2)}) async-start(bf16[8,14,16,128]{3,2,1,0:T(8,128)(2,1)} %broadcast_in_dim.16), calls=%async_computation.1 | async-start | bytes 917504 | tf_op jit(solution)/shard_map/all_to_all | solution.py:316
  17.2 89.0 %all-gather.3.cloned.1.call-start = ((), (), s32[]{:S(2)}) async-start(), calls=%async_computation.4 | async-start | bytes 7798784 | tf_op jit(solution)/shard_map/all_gather | solution.py:320
  19.4 21.8 %collective-permute-start = (bf16[128,1920]{1,0:T(8,128)(2,1)S(1)}, bf16[128,1920]{1,0:T(8,128)(2,1)S(1)}, u32[]{:S(2)}, u32[]{:S(2)}) collective-permute-start(bf16[128,1920]{1,0:T(8,128)(2,1)S(1)} %slice_dynamic-update-slice_fusion.block.refs_0_), channel_id=1, source_target_pairs={{0,1},{1,2},{2,3},{3,4},{4,5},{5,6},{6,7},{7,0},{8,9},{9,10},{10,1... | collective-permute-start | bytes 1474568 | tf_op jit(solution)/shard_map/ppermute | solution.py:31
  23.3 17.9 %collective-permute-start.4 = (bf16[128,1920]{1,0:T(8,128)(2,1)S(1)}, bf16[128,1920]{1,0:T(8,128)(2,1)S(1)}, u32[]{:S(2)}, u32[]{:S(2)}) collective-permute-start(bf16[128,1920]{1,0:T(8,128)(2,1)S(1)} %slice_dynamic-update-slice_fusion.block.refs_0_), channel_id=1, source_target_pairs={{0,7},{1,0},{2,1},{3,2},{4,3},{5,4},{6,5},{7,6},{8,15},{9,8},{10,9... | collective-permute-start | bytes 1474568 | tf_op jit(solution)/shard_map/ppermute | solution.py:34
  41.2 15.3 %collective-permute-start.1 = (bf16[128,1920]{1,0:T(8,128)(2,1)S(1)}, bf16[128,1920]{1,0:T(8,128)(2,1)S(1)}, u32[]{:S(2)}, u32[]{:S(2)}) collective-permute-start(bf16[128,1920]{1,0:T(8,128)(2,1)S(1)} %collective-permute-done.block.refs_1_), channel_id=1, source_target_pairs={{0,1},{1,2},{2,3},{3,4},{4,5},{5,6},{6,7},{7,0},{8,9},{9,10},{10,1... | collective-permute-start | bytes 1474568 | tf_op jit(solution)/shard_map/ppermute | solution.py:31
  43.3 15.1 %collective-permute-start.5 = (bf16[128,1920]{1,0:T(8,128)(2,1)S(1)}, bf16[128,1920]{1,0:T(8,128)(2,1)S(1)}, u32[]{:S(2)}, u32[]{:S(2)}) collective-permute-start(bf16[128,1920]{1,0:T(8,128)(2,1)S(1)} %collective-permute-done.4.block.refs_7_), channel_id=1, source_target_pairs={{0,7},{1,0},{2,1},{3,2},{4,3},{5,4},{6,5},{7,6},{8,15},{9,8},{10,9... | collective-permute-start | bytes 1474568 | tf_op jit(solution)/shard_map/ppermute | solution.py:34
  56.5 14.4 %collective-permute-start.2 = (bf16[128,1920]{1,0:T(8,128)(2,1)S(1)}, bf16[128,1920]{1,0:T(8,128)(2,1)S(1)}, u32[]{:S(2)}, u32[]{:S(2)}) collective-permute-start(bf16[128,1920]{1,0:T(8,128)(2,1)S(1)} %collective-permute-done.1.block.refs_2_), channel_id=1, source_target_pairs={{0,1},{1,2},{2,3},{3,4},{4,5},{5,6},{6,7},{7,0},{8,9},{9,10},{10,1... | collective-permute-start | bytes 1474568 | tf_op jit(solution)/shard_map/ppermute | solution.py:31
  58.4 19.9 %collective-permute-start.6 = (bf16[128,1920]{1,0:T(8,128)(2,1)S(1)}, bf16[128,1920]{1,0:T(8,128)(2,1)S(1)}, u32[]{:S(2)}, u32[]{:S(2)}) collective-permute-start(bf16[128,1920]{1,0:T(8,128)(2,1)S(1)} %collective-permute-done.5.block.refs_6_), channel_id=1, source_target_pairs={{0,7},{1,0},{2,1},{3,2},{4,3},{5,4},{6,5},{7,6},{8,15},{9,8},{10,9... | collective-permute-start | bytes 1474568 | tf_op jit(solution)/shard_map/ppermute | solution.py:34
  70.8 13.5 %collective-permute-start.3 = (bf16[128,1920]{1,0:T(8,128)(2,1)S(1)}, bf16[128,1920]{1,0:T(8,128)(2,1)S(1)}, u32[]{:S(2)}, u32[]{:S(2)}) collective-permute-start(bf16[128,1920]{1,0:T(8,128)(2,1)S(1)} %collective-permute-done.2.block.refs_3_), channel_id=1, source_target_pairs={{0,1},{1,2},{2,3},{3,4},{4,5},{5,6},{6,7},{7,0},{8,9},{9,10},{10,1... | collective-permute-start | bytes 1474568 | tf_op jit(solution)/shard_map/ppermute | solution.py:31
  78.3 7.0 %copy-start.8 = (bf16[1024,512]{1,0:T(8,128)(2,1)S(1)}, bf16[1024,512]{1,0:T(8,128)(2,1)}, u32[]{:S(2)}) copy-start(bf16[1024,512]{1,0:T(8,128)(2,1)} %refs_18_.1) | copy-start | bytes 3145732
  78.3 7.0 %copy-start.9 = (bf16[512,1024]{1,0:T(8,128)(2,1)S(1)}, bf16[512,1024]{1,0:T(8,128)(2,1)}, u32[]{:S(2)}) copy-start(bf16[512,1024]{1,0:T(8,128)(2,1)} %narrow.1) | copy-start | bytes 3145732
  78.3 7.0 %copy-start.15 = (f32[1024]{0:T(1024)S(1)}, f32[1024]{0:T(1024)}, u32[]{:S(2)}) copy-start(f32[1024]{0:T(1024)} %param.16) | copy-start | bytes 12292
  94.3 1.1 copy-start.7
  99.5 37.5 %all-to-all-start = ((bf16[8,64,1280]{2,1,0:T(8,128)(2,1)}), bf16[8,64,1280]{2,1,0:T(8,128)(2,1)S(1)}, u32[]{:S(2)}, u32[]{:S(2)}) async-start(bf16[8,64,1280]{2,1,0:T(8,128)(2,1)} %bitcast.30), calls=%async_computation | async-start | bytes 2621440 | tf_op jit(solution)/shard_map/all_to_all | solution.py:334
  106.3 3.1 %copy-start.2 = (bf16[128,14,16,128]{3,2,1,0:T(8,128)(2,1)S(1)}, bf16[128,14,16,128]{3,2,1,0:T(8,128)(2,1)}, u32[]{:S(2)}) copy-start(bf16[128,14,16,128]{3,2,1,0:T(8,128)(2,1)} %all-gather.3.cloned.1.call-done) | copy-start | bytes 22020100
  109.3 27.7 %copy-start.12 = (bf16[64,1408]{1,0:T(8,128)(2,1)S(1)}, bf16[64,1408]{1,0:T(8,128)(2,1)}, u32[]{:S(2)}) copy-start(bf16[64,1408]{1,0:T(8,128)(2,1)} %copy-done.11) | copy-start | bytes 540676
  109.3 27.7 %copy-start.14 = (bf16[64,1024]{1,0:T(8,128)(2,1)S(1)}, bf16[64,1024]{1,0:T(8,128)(2,1)}, u32[]{:S(2)}) copy-start(bf16[64,1024]{1,0:T(8,128)(2,1)} %copy-done.13) | copy-start | bytes 393220
  110.6 1.9 copy-start.3
  112.5 1.6 copy-start.5
  137.0 2.1 copy-start.4
  139.2 1.8 copy-start.6
  141.0 32.7 %copy-start.19 = (f32[512,512]{1,0:T(8,128)S(1)}, f32[512,512]{1,0:T(8,128)}, u32[]{:S(2)}) copy-start(f32[512,512]{1,0:T(8,128)} %copy-done.18) | copy-start | bytes 3145732
  141.0 32.7 %copy-start.21 = (bf16[512,512]{1,0:T(8,128)(2,1)S(1)}, bf16[512,512]{1,0:T(8,128)(2,1)}, u32[]{:S(2)}) copy-start(bf16[512,512]{1,0:T(8,128)(2,1)} %copy-done.20) | copy-start | bytes 1572868
  144.0 29.7 %copy-start.10 = (bf16[512,1024]{1,0:T(8,128)(2,1)S(1)}, bf16[512,1024]{1,0:T(8,128)(2,1)}, u32[]{:S(2)}) copy-start(bf16[512,1024]{1,0:T(8,128)(2,1)} %narrow.1) | copy-start | bytes 3145732
  144.0 29.7 %copy-start.17 = (bf16[512,1024]{1,0:T(8,128)(2,1)S(1)}, bf16[512,1024]{1,0:T(8,128)(2,1)}, u32[]{:S(2)}) copy-start(bf16[512,1024]{1,0:T(8,128)(2,1)} %copy-done.16) | copy-start | bytes 3145732
  179.5 4.6 %collective-permute-start.7 = (bf16[32,32,512]{2,1,0:T(8,128)(2,1)S(1)}, bf16[32,32,512]{2,1,0:T(8,128)(2,1)S(1)}, u32[]{:S(2)}, u32[]{:S(2)}) collective-permute-start(bf16[32,32,512]{2,1,0:T(8,128)(2,1)S(1)} %get-tuple-element.25), channel_id=1, source_target_pairs={{0,8},{8,0},{1,9},{9,1},{2,10},{10,2},{3,11},{11,3},{4,12},{12,4},... | collective-permute-start | bytes 3145736 | tf_op jit(solution)/shard_map/ppermute | solution.py:345
  (5 other events, 4.1 us)
Sparse Core Ops, SparseCore 0:
  41.3 56.4 all-gather.2

commit v4 on v3

--- a/solution.py
+++ b/solution.py
@@ -86,67 +86,73 @@
     held, made, (place, gain, widen, narrow) = refs[:8], refs[8:16], refs[16:20]
     normed_out, active_out, slope_out, joint, own_out, picked_out = refs[20:26]
     rows_by, queries, keys, values = refs[26:]
-    me = me_ref[0]
-    mine = pl.ds(pl.multiple_of(me * 64, 64), 64)
-
-    for s in range(8):
-        owner = lax.rem(me + (8 - s), 8)
-        for g in range(4):
-            rows_by[owner, 128 * g : 128 * g + 128, :] = held[s][
-                :, TD + 128 * g : TD + 128 * g + 128
-            ]
-    for b in range(8):
-        own_out[:, 128 * b : 128 * b + 128] = rows_by[b, mine, :]
-
-    spots = lax.broadcasted_iota(jnp.int32, (64, 128), 1)
-    own_place = place[mine, :]
-    total = jnp.zeros((64, TD), F32)
-    for s in range(8):
-        chosen = jnp.where(spots + 128 * s == own_place, 1.0, 0.0).astype(BF)
-        total += jnp.dot(chosen, held[s][:, :TD], preferred_element_type=F32)
-    picked_out[...] = total.astype(BF)
-
-    for s in range(8):
-        queries[128 * s : 128 * s + 128, :] = made[s][:, :256]
-        keys[128 * s : 128 * s + 128, :] = made[s][:, 256:512]
-        values[128 * s : 128 * s + 128, :] = made[s][:, 512:]
-
-    def chunk(i, _):
-        rows = pl.ds(pl.multiple_of(i * 128, 128), 128)
-        student = jnp.concatenate([rows_by[b, rows, :] for b in range(8)], axis=1).astype(F32)
-        normed = layer_norm(student, gain[...]).astype(BF)
-        normed_out[rows, :] = normed
-        pre = jnp.dot(normed, widen[...], preferred_element_type=F32)
-        half = 0.5 * (1.0 + lax.erf(pre * 0.7071067811865476))
-        active = (pre * half).astype(BF)
-        active_out[rows, :] = active
-        slope_out[rows, :] = half + pre * 0.3989422804014327 * jnp.exp(-0.5 * pre * pre)
-        joint[rows, :1024] = jnp.dot(active, narrow[...], preferred_element_type=F32).astype(BF)
-
-        spots = lax.broadcasted_iota(jnp.int32, (128, 1024), 1)
-        chosen = jnp.where(spots == place[rows, :], 1.0, 0.0).astype(BF)
-        query = jnp.dot(chosen, queries[...], preferred_element_type=F32).astype(BF)
-        heads = []
-        for h in range(2):
-            lanes = slice(128 * h, 128 * h + 128)
-            scores = lax.dot_general(
-                query[:, lanes], keys[:, lanes], LANES, preferred_element_type=F32
-            ) * ((TD // TH) ** (-0.5))
-            top = jnp.max(scores, axis=-1, keepdims=True)
-            num = jnp.exp(scores - top)
-            soft = (num * (1.0 / jnp.sum(num, axis=-1, keepdims=True))).astype(BF)
-            heads.append(jnp.dot(soft, values[:, lanes], preferred_element_type=F32)[:, :88])
-        heads.append(jnp.zeros((128, 80), F32))
-        joint[rows, 1024:] = jnp.concatenate(heads, axis=1).astype(BF)
-        return 0
-
-    lax.fori_loop(0, 4, chunk, 0)
+    def prepare():
+        me = me_ref[0]
+        mine = pl.ds(pl.multiple_of(me * 64, 64), 64)
+
+        for s in range(8):
+            owner = lax.rem(me + (8 - s), 8)
+            for g in range(4):
+                rows_by[owner, 128 * g : 128 * g + 128, :] = held[s][
+                    :, TD + 128 * g : TD + 128 * g + 128
+                ]
+        for b in range(8):
+            own_out[:, 128 * b : 128 * b + 128] = rows_by[b, mine, :]
+
+        spots = lax.broadcasted_iota(jnp.int32, (64, 128), 1)
+        own_place = place[mine, :]
+        total = jnp.zeros((64, TD), F32)
+        for s in range(8):
+            chosen = jnp.where(spots + 128 * s == own_place, 1.0, 0.0).astype(BF)
+            total += jnp.dot(chosen, held[s][:, :TD], preferred_element_type=F32)
+        picked_out[...] = total.astype(BF)
+
+        for s in range(8):
+            queries[128 * s : 128 * s + 128, :] = made[s][:, :256]
+            keys[128 * s : 128 * s + 128, :] = made[s][:, 256:512]
+            values[128 * s : 128 * s + 128, :] = made[s][:, 512:]
+
+    step = pl.program_id(0)
+    pl.when(step == 0)(prepare)
+    rows = pl.ds(pl.multiple_of(step * 128, 128), 128)
+    student = jnp.concatenate([rows_by[b, rows, :] for b in range(8)], axis=1).astype(F32)
+    normed = layer_norm(student, gain[...]).astype(BF)
+    normed_out[...] = normed
+    pre = jnp.dot(normed, widen[...], preferred_element_type=F32)
+    half = 0.5 * (1.0 + lax.erf(pre * 0.7071067811865476))
+    active = (pre * half).astype(BF)
+    active_out[...] = active
+    slope_out[...] = half + pre * 0.3989422804014327 * jnp.exp(-0.5 * pre * pre)
+    joint[:, :1024] = jnp.dot(active, narrow[...], preferred_element_type=F32).astype(BF)
+
+    spots = lax.broadcasted_iota(jnp.int32, (128, 1024), 1)
+    chosen = jnp.where(spots == place[rows, :], 1.0, 0.0).astype(BF)
+    query = jnp.dot(chosen, queries[...], preferred_element_type=F32).astype(BF)
+    heads = []
+    for h in range(2):
+        lanes = slice(128 * h, 128 * h + 128)
+        scores = lax.dot_general(
+            query[:, lanes], keys[:, lanes], LANES, preferred_element_type=F32
+        ) * ((TD // TH) ** (-0.5))
+        top = jnp.max(scores, axis=-1, keepdims=True)
+        num = jnp.exp(scores - top)
+        soft = (num * (1.0 / jnp.sum(num, axis=-1, keepdims=True))).astype(BF)
+        heads.append(jnp.dot(soft, values[:, lanes], preferred_element_type=F32)[:, :88])
+    heads.append(jnp.zeros((128, 80), F32))
+    joint[:, 1024:] = jnp.concatenate(heads, axis=1).astype(BF)
 
 
 def middle(me, held, made, place, gain, widen, narrow):
-    return kernel_call(
+    def banded(width):
+        return pl.BlockSpec((128, width), lambda i: (i, 0))
+
+    def once(width):
+        return pl.BlockSpec((64, width), lambda i: (0, 0))
+
+    return pl.pallas_call(
         middle_body,
-        [
+        grid=(4,),
+        out_shape=[
             jax.ShapeDtypeStruct((512, 1024), BF),
             jax.ShapeDtypeStruct((512, 512), BF),
             jax.ShapeDtypeStruct((512, 512), F32),
@@ -154,12 +160,15 @@
             jax.ShapeDtypeStruct((64, 1024), BF),
             jax.ShapeDtypeStruct((64, TD), BF),
         ],
-        scratch=[pltpu.VMEM((8, 512, 128), BF)] + [pltpu.VMEM((1024, 256), BF)] * 3,
-        flops=2 * 512 * 1024 * (1024 + 768) + 2 * 64 * 1024 * TD,
-        scalars=1,
-        arrays=20,
-        moved=12_000_000,
-        limit=12,
+        in_specs=[SMEM] + [VMEM] * 20,
+        out_specs=[banded(1024), banded(512), banded(512), banded(1280), once(1024), once(TD)],
+        scratch_shapes=[pltpu.VMEM((8, 512, 128), BF)] + [pltpu.VMEM((1024, 256), BF)] * 3,
+        compiler_params=pltpu.CompilerParams(vmem_limit_bytes=14 << 20),
+        cost_estimate=pl.CostEstimate(
+            flops=2 * 512 * 1024 * (1024 + 768) + 2 * 64 * 1024 * TD,
+            bytes_accessed=12_000_000,
+            transcendentals=0,
+        ),
     )(me, *held, *made, place, gain, widen, narrow)
 
 
@@ -313,11 +322,8 @@
             lax.dynamic_index_in_dim(to_tiles(target_head, 6), at, 0, False),
         ]
     )
-    shares = lax.all_to_all(
-        jnp.broadcast_to(mine, (8, *mine.shape)), "mp", 0, 0, tiled=True
-    )
-    shares, _, _ = lax.optimization_barrier((shares, held[1], held[7]))
-    out_full, head_full = assemble(lax.all_gather(shares, ("z", "c"), axis=0))
+    pieces = lax.all_gather(mine, ("z", "c", "mp"), axis=0)
+    out_full, head_full = assemble(pieces.reshape(16, 8, 14, 16, 128))
 
     here = jnp.reshape(me, (1,)).astype(jnp.int32)
     made = [project(h, teacher_gain.reshape(1, -1), teacher_qkv) for h in held]

time: 235 us -> 219 us (0.932)
  blocking collectives: 71.9 us -> 63.6 us
  starting transfers between devices: 38.3 us -> 33.2 us
  local copies, waits for them, and re-layouts: 20.6 us -> 17.4 us
    all_gather x1, waiting for transfers between devices: 0.02 us -> 17.2 us  [on_device(): pieces = lax.all_gather(mine, ('z', 'c', 'mp'), axis=0)]
    all_to_all x1, waiting for transfers between devices: 23 us -> 7.84 us  [on_device(): arrived = lax.all_to_all(joint.reshape(8, 64, 1280), 'mp', 0, 0, tiled=True)]
    all_to_all x1, blocking collectives: 42.1 us -> 34.2 us  [on_device(): kept = lax.all_to_all(kept, ('z', 'x'), 0, 0, tiled=True)]
    all_to_all x1 -> x0, starting transfers between devices: 7.23 us -> none  [on_device(): lax.all_to_all(jnp.broadcast_to(mine, (8, *mine.shape)), 'mp', 0, 0, tile...]
    ppermute x4, waiting for transfers between devices: 35.4 us -> 32.4 us  [ring(): right = lax.ppermute(right, 'mp', shift(1))]
    unnamed x57 -> x45, local copies, waits for them, and re-layouts: 15.8 us -> 13.4 us
  transfers between devices with their start and end apart: 11 -> 10, of which waited for: 6 -> 7; matrix products, arithmetic and copies ran while one was open for 1% -> 1% of each run, Pallas kernels for 7% -> 8%
where the time goes in v4:
time: 219 us; the launch traced here: 218 us
  blocking collectives  63.6 us (29%)
  waiting for transfers between devices  60.1 us (27%)
  starting transfers between devices  33.2 us (15%)
  Pallas kernels  27.2 us (12%)
  local copies, waits for them, and re-layouts  17.4 us (8%)
  between operations  15.2 us (7%)
    all_to_all x1, blocking collectives, on_device(): kept = lax.all_to_all(kept, ('z', 'x'), 0, 0, tiled=True)  34.2 us
    ppermute x4, waiting for transfers between devices, ring(): right = lax.ppermute(right, 'mp', shift(1))  32.4 us
    all_to_all x1, blocking collectives, on_device(): back = lax.all_to_all(back_own, 'mp', 0, 0, tiled=True)  29.4 us
    all_gather x1, waiting for transfers between devices, on_device(): pieces = lax.all_gather(mine, ('z', 'c', 'mp'), axis=0)  17.2 us
    ppermute x3, starting transfers between devices, ring(): left = lax.ppermute(left, 'mp', shift(-1))  14.1 us
    unnamed x45, local copies, waits for them, and re-layouts  13.4 us
    pallas_call x1, Pallas kernels, middle(): pl.pallas_call(middle_body, grid=(4,), out_shape=[jax.ShapeDtypeStruct((5...  9.89 us
    ppermute x4, starting transfers between devices, ring(): right = lax.ppermute(right, 'mp', shift(1))  9.21 us
  transfers between devices with their start and end apart: 10, of which 7 were waited for; matrix products, arithmetic and copies ran while one was open for 1% of the time, Pallas kernels for 8%

profile of v4, /device:TPU:2, one launch (start us, length us, event | category | flops | bytes accessed | tf_op | source)
XLA Modules:
  0.0 218.3 jit_solution(13663422243154174073)
XLA Ops:
  7.2 1.5 reshape.228
  10.5 1.3 gather_fusion
  12.0 3.5 %collective-permute-start = (bf16[128,1920]{1,0:T(8,128)(2,1)S(1)}, bf16[128,1920]{1,0:T(8,128)(2,1)S(1)}, u32[]{:S(2)}, u32[]{:S(2)}) collective-permute-start(bf16[128,1920]{1,0:T(8,128)(2,1)S(1)} %slice_dynamic-update-slice_fusion.block.refs_0_), channel_id=1, source_target_pairs={{0,1},{1,2},{2,3},{3,4},{4,5},{5,6},{6,7},{7,0},{8,9},{9,10},{10,1... | collective-permute-start | bytes 1474568 | tf_op jit(solution)/shard_map/ppermute | solution.py:31
  15.5 3.8 %collective-permute-start.4 = (bf16[128,1920]{1,0:T(8,128)(2,1)S(1)}, bf16[128,1920]{1,0:T(8,128)(2,1)S(1)}, u32[]{:S(2)}, u32[]{:S(2)}) collective-permute-start(bf16[128,1920]{1,0:T(8,128)(2,1)S(1)} %slice_dynamic-update-slice_fusion.block.refs_0_), channel_id=1, source_target_pairs={{0,7},{1,0},{2,1},{3,2},{4,3},{5,4},{6,5},{7,6},{8,15},{9,8},{10,9... | collective-permute-start | bytes 1474568 | tf_op jit(solution)/shard_map/ppermute | solution.py:34
  19.3 9.3 %collective-permute-done.block.refs_1_ = bf16[128,1920]{1,0:T(8,128)(2,1)S(1)} collective-permute-done((bf16[128,1920]{1,0:T(8,128)(2,1)S(1)}, bf16[128,1920]{1,0:T(8,128)(2,1)S(1)}, u32[]{:S(2)}, u32[]{:S(2)}) %collective-permute-start) | collective-permute-done | bytes 491552 | tf_op jit(solution)/shard_map/ppermute | solution.py:31
  28.6 1.9 collective-permute-start.1
  30.5 5.1 %collective-permute-start.5 = (bf16[128,1920]{1,0:T(8,128)(2,1)S(1)}, bf16[128,1920]{1,0:T(8,128)(2,1)S(1)}, u32[]{:S(2)}, u32[]{:S(2)}) collective-permute-start(bf16[128,1920]{1,0:T(8,128)(2,1)S(1)} %collective-permute-done.4.block.refs_7_), channel_id=1, source_target_pairs={{0,7},{1,0},{2,1},{3,2},{4,3},{5,4},{6,5},{7,6},{8,15},{9,8},{10,9... | collective-permute-start | bytes 1474568 | tf_op jit(solution)/shard_map/ppermute | solution.py:34
  35.6 9.4 %collective-permute-done.1.block.refs_2_ = bf16[128,1920]{1,0:T(8,128)(2,1)S(1)} collective-permute-done((bf16[128,1920]{1,0:T(8,128)(2,1)S(1)}, bf16[128,1920]{1,0:T(8,128)(2,1)S(1)}, u32[]{:S(2)}, u32[]{:S(2)}) %collective-permute-start.1) | collective-permute-done | bytes 491552 | tf_op jit(solution)/shard_map/ppermute | solution.py:31
  45.0 1.9 collective-permute-start.2
  46.9 5.1 %collective-permute-start.6 = (bf16[128,1920]{1,0:T(8,128)(2,1)S(1)}, bf16[128,1920]{1,0:T(8,128)(2,1)S(1)}, u32[]{:S(2)}, u32[]{:S(2)}) collective-permute-start(bf16[128,1920]{1,0:T(8,128)(2,1)S(1)} %collective-permute-done.5.block.refs_6_), channel_id=1, source_target_pairs={{0,7},{1,0},{2,1},{3,2},{4,3},{5,4},{6,5},{7,6},{8,15},{9,8},{10,9... | collective-permute-start | bytes 1474568 | tf_op jit(solution)/shard_map/ppermute | solution.py:34
  52.1 8.2 %collective-permute-done.2.block.refs_3_ = bf16[128,1920]{1,0:T(8,128)(2,1)S(1)} collective-permute-done((bf16[128,1920]{1,0:T(8,128)(2,1)S(1)}, bf16[128,1920]{1,0:T(8,128)(2,1)S(1)}, u32[]{:S(2)}, u32[]{:S(2)}) %collective-permute-start.2) | collective-permute-done | bytes 491552 | tf_op jit(solution)/shard_map/ppermute | solution.py:31
  60.3 1.9 collective-permute-start.3
  63.2 0.9 shard_map.131.refs_9_
  68.8 5.5 %collective-permute-done.3.block.refs_4_ = bf16[128,1920]{1,0:T(8,128)(2,1)S(1)} collective-permute-done((bf16[128,1920]{1,0:T(8,128)(2,1)S(1)}, bf16[128,1920]{1,0:T(8,128)(2,1)S(1)}, u32[]{:S(2)}, u32[]{:S(2)}) %collective-permute-start.3) | collective-permute-done | bytes 491552 | tf_op jit(solution)/shard_map/ppermute | solution.py:31
  75.2 9.9 %shard_map.138 = (bf16[512,1024]{1,0:T(8,128)(2,1)S(1)}, bf16[512,512]{1,0:T(8,128)(2,1)S(1)}, f32[512,512]{1,0:T(8,128)S(1)}, bf16[512,1280]{1,0:T(8,128)(2,1)}...) custom-call(s32[1]{0:T(128)} %bitcast.2.me_ref, ...), custom_call_target="tpu_custom_call" | custom-call | flops 2063597568 | bytes 12000000 | tf_op jit(solution)/shard_map/pallas_call | solution.py:152
  85.1 1.0 copy-done.10
  86.1 1.0 copy-done.12
  87.8 8.0 %all-to-all-start = ((bf16[8,64,1280]{2,1,0:T(8,128)(2,1)}), bf16[8,64,1280]{2,1,0:T(8,128)(2,1)S(1)}, u32[]{:S(2)}, u32[]{:S(2)}) async-start(bf16[8,64,1280]{2,1,0:T(8,128)(2,1)} %bitcast.7), calls=%async_computation | async-start | bytes 2621440 | tf_op jit(solution)/shard_map/all_to_all | solution.py:340
  96.5 17.2 %all-gather.3.cloned.1.call-done = bf16[1792,16,128]{2,1,0:T(8,128)(2,1)} async-done(((bf16[14,16,128]{2,1,0:T(8,128)(2,1)}), bf16[1792,16,128]{2,1,0:T(8,128)(2,1)}) %all-gather.3.cloned.1.call-update) | async-done | bytes 7340048 | tf_op jit(solution)/shard_map/all_gather | solution.py:325
  113.7 3.1 %copy-done.2 = bf16[1792,16,128]{2,1,0:T(8,128)(2,1)S(1)} copy-done((bf16[1792,16,128]{2,1,0:T(8,128)(2,1)S(1)}, bf16[1792,16,128]{2,1,0:T(8,128)(2,1)}, u32[]{:S(2)}) %copy-start.2) | copy-done | bytes 7340056
  116.8 1.2 shard_map.139
  118.0 1.9 copy-done.3
  119.9 1.6 copy-done.5
  121.5 7.8 %all-to-all-done.arrived = bf16[8,64,1280]{2,1,0:T(8,128)(2,1)S(1)} async-done(((bf16[8,64,1280]{2,1,0:T(8,128)(2,1)}), bf16[8,64,1280]{2,1,0:T(8,128)(2,1)S(1)}, u32[]{:S(2)}, u32[]{:S(2)}) %all-to-all-start) | async-done | bytes 1310752 | tf_op jit(solution)/shard_map/all_to_all | solution.py:340
  129.3 2.1 copy-done.4
  131.5 1.8 copy-done.6
  133.3 3.0 %shard_map.140 = bf16[8,33,16,128]{3,2,1,0:T(8,128)(2,1)S(1)} custom-call(f32[64,1]{1,0:T(8,128)S(1)} %fusion.6.weight, bf16[8,64,1280]{2,1,0:T(8,128)(2,1)S(1)} %all-to-all-done.arrived, bf16[64,1024]{1,0:T(8,128)(2,1)S(1)} %get-tuple-element.15.own, bf16[64,1408]{1,0:T(8,128)(2,1)S(1)} %get-tuple-element.16.picked, bf16[1408,1408]{1,0:T(8,128)(2,1)S(1)} %copy-done.4, ...), custom_call_target="tpu_custom_call" | custom-call | flops 622854144 | bytes 10000000 | tf_op jit(solution)/shard_map/pallas_call | solution.py:207
  136.3 29.4 %all_to_all.15.back_in = bf16[8,33,16,128]{3,2,1,0:T(8,128)(2,1)S(1)} all-to-all(bf16[8,33,16,128]{3,2,1,0:T(8,128)(2,1)S(1)} %shard_map.140), channel_id=1, replica_groups=mesh['z'=8,'x'=4,'c'=2,'mp'=8] {'mp'}, dimensions={0} | all-to-all | bytes 2162688 | tf_op jit(solution)/shard_map/all_to_all | solution.py:347
  165.7 5.8 %shard_map.141 = (bf16[32,32,512]{2,1,0:T(8,128)(2,1)S(1)}, bf16[32,32,512]{2,1,0:T(8,128)(2,1)S(1)}, f32[1]{0:T(128)}) custom-call(s32[1]{0:T(128)} %bitcast.core_ref, bf16[8,33,16,128]{3,2,1,0:T(8,128)(2,1)S(1)} %all_to_all.15.back_in, bf16[512,1024]{1,0:T(8,128)(2,1)S(1)} %copy-done.11, bf16[512,512]{1,0:T(8,128)(2,1)S(1)} %copy-done.15, ...), custom_call_target="tpu_custom_call" | custom-call | flops 1610612736 | bytes 8000000 | tf_op jit(solution)/shard_map/pallas_call | solution.py:284
  171.5 1.9 collective-permute-start.7
  173.4 2.6 %collective-permute-done.7 = bf16[32,32,512]{2,1,0:T(8,128)(2,1)S(1)} collective-permute-done((bf16[32,32,512]{2,1,0:T(8,128)(2,1)S(1)}, bf16[32,32,512]{2,1,0:T(8,128)(2,1)S(1)}, u32[]{:S(2)}, u32[]{:S(2)}) %collective-permute-start.7) | collective-permute-done | bytes 1048608 | tf_op jit(solution)/shard_map/ppermute | solution.py:351
  176.4 34.2 %all_to_all.16 = bf16[32,32,512]{2,1,0:T(8,128)(2,1)S(1)} all-to-all(bf16[32,32,512]{2,1,0:T(8,128)(2,1)S(1)} %add_convert_fusion), channel_id=1, replica_groups=mesh['z'=8,'x'=4,'c'=2,'mp'=8] {'z','x'}, dimensions={0} | all-to-all | bytes 2097152 | tf_op jit(solution)/shard_map/all_to_all | solution.py:353
  (67 shorter events, 10.2 us)
Async XLA Ops:
  7.2 3.3 %copy-start = (bf16[1,1024,128]{2,1,0:T(8,128)(2,1)S(1)}, bf16[1,1024,128]{2,1,0:T(8,128)(2,1)}, u32[]{:S(2)}) copy-start(bf16[1,1024,128]{2,1,0:T(8,128)(2,1)} %param.15) | copy-start | bytes 786436
  7.2 1.7 copy-start.16
  7.2 106.5 %all-gather.3.cloned.1.call-start = ((), (), s32[]{:S(2)}) async-start(), calls=%async_computation.3 | async-start | bytes 7397376 | tf_op jit(solution)/shard_map/all_gather | solution.py:325
  8.9 1.0 copy-start.19
  9.1 2.8 %copy-start.17 = (bf16[1,128,1408]{2,1,0:T(8,128)(2,1)S(1)}, bf16[1,128,1408]{2,1,0:T(8,128)(2,1)}, u32[]{:S(2)}) copy-start(bf16[1,128,1408]{2,1,0:T(8,128)(2,1)} %param.11) | copy-start | bytes 1081348
  9.1 53.1 %copy-start.18 = (f32[1408]{0:T(1024)S(1)}, f32[1408]{0:T(1024)}, u32[]{:S(2)}) copy-start(f32[1408]{0:T(1024)} %param.12) | copy-start | bytes 16900
  9.1 53.1 %copy-start.1 = (bf16[3,176,1408]{2,1,0:T(8,128)(2,1)S(1)}, bf16[3,176,1408]{2,1,0:T(8,128)(2,1)}, u32[]{:S(2)}) copy-start(bf16[3,176,1408]{2,1,0:T(8,128)(2,1)} %weights.15) | copy-start | bytes 4460548
  12.0 16.6 %collective-permute-start = (bf16[128,1920]{1,0:T(8,128)(2,1)S(1)}, bf16[128,1920]{1,0:T(8,128)(2,1)S(1)}, u32[]{:S(2)}, u32[]{:S(2)}) collective-permute-start(bf16[128,1920]{1,0:T(8,128)(2,1)S(1)} %slice_dynamic-update-slice_fusion.block.refs_0_), channel_id=1, source_target_pairs={{0,1},{1,2},{2,3},{3,4},{4,5},{5,6},{6,7},{7,0},{8,9},{9,10},{10,1... | collective-permute-start | bytes 1474568 | tf_op jit(solution)/shard_map/ppermute | solution.py:31
  15.5 15.0 %collective-permute-start.4 = (bf16[128,1920]{1,0:T(8,128)(2,1)S(1)}, bf16[128,1920]{1,0:T(8,128)(2,1)S(1)}, u32[]{:S(2)}, u32[]{:S(2)}) collective-permute-start(bf16[128,1920]{1,0:T(8,128)(2,1)S(1)} %slice_dynamic-update-slice_fusion.block.refs_0_), channel_id=1, source_target_pairs={{0,7},{1,0},{2,1},{3,2},{4,3},{5,4},{6,5},{7,6},{8,15},{9,8},{10,9... | collective-permute-start | bytes 1474568 | tf_op jit(solution)/shard_map/ppermute | solution.py:34
  28.6 16.5 %collective-permute-start.1 = (bf16[128,1920]{1,0:T(8,128)(2,1)S(1)}, bf16[128,1920]{1,0:T(8,128)(2,1)S(1)}, u32[]{:S(2)}, u32[]{:S(2)}) collective-permute-start(bf16[128,1920]{1,0:T(8,128)(2,1)S(1)} %collective-permute-done.block.refs_1_), channel_id=1, source_target_pairs={{0,1},{1,2},{2,3},{3,4},{4,5},{5,6},{6,7},{7,0},{8,9},{9,10},{10,1... | collective-permute-start | bytes 1474568 | tf_op jit(solution)/shard_map/ppermute | solution.py:31
  30.5 16.5 %collective-permute-start.5 = (bf16[128,1920]{1,0:T(8,128)(2,1)S(1)}, bf16[128,1920]{1,0:T(8,128)(2,1)S(1)}, u32[]{:S(2)}, u32[]{:S(2)}) collective-permute-start(bf16[128,1920]{1,0:T(8,128)(2,1)S(1)} %collective-permute-done.4.block.refs_7_), channel_id=1, source_target_pairs={{0,7},{1,0},{2,1},{3,2},{4,3},{5,4},{6,5},{7,6},{8,15},{9,8},{10,9... | collective-permute-start | bytes 1474568 | tf_op jit(solution)/shard_map/ppermute | solution.py:34
  45.0 15.3 %collective-permute-start.2 = (bf16[128,1920]{1,0:T(8,128)(2,1)S(1)}, bf16[128,1920]{1,0:T(8,128)(2,1)S(1)}, u32[]{:S(2)}, u32[]{:S(2)}) collective-permute-start(bf16[128,1920]{1,0:T(8,128)(2,1)S(1)} %collective-permute-done.1.block.refs_2_), channel_id=1, source_target_pairs={{0,1},{1,2},{2,3},{3,4},{4,5},{5,6},{6,7},{7,0},{8,9},{9,10},{10,1... | collective-permute-start | bytes 1474568 | tf_op jit(solution)/shard_map/ppermute | solution.py:31
  46.9 20.9 %collective-permute-start.6 = (bf16[128,1920]{1,0:T(8,128)(2,1)S(1)}, bf16[128,1920]{1,0:T(8,128)(2,1)S(1)}, u32[]{:S(2)}, u32[]{:S(2)}) collective-permute-start(bf16[128,1920]{1,0:T(8,128)(2,1)S(1)} %collective-permute-done.5.block.refs_6_), channel_id=1, source_target_pairs={{0,7},{1,0},{2,1},{3,2},{4,3},{5,4},{6,5},{7,6},{8,15},{9,8},{10,9... | collective-permute-start | bytes 1474568 | tf_op jit(solution)/shard_map/ppermute | solution.py:34
  60.3 13.9 %collective-permute-start.3 = (bf16[128,1920]{1,0:T(8,128)(2,1)S(1)}, bf16[128,1920]{1,0:T(8,128)(2,1)S(1)}, u32[]{:S(2)}, u32[]{:S(2)}) collective-permute-start(bf16[128,1920]{1,0:T(8,128)(2,1)S(1)} %collective-permute-done.2.block.refs_3_), channel_id=1, source_target_pairs={{0,1},{1,2},{2,3},{3,4},{4,5},{5,6},{6,7},{7,0},{8,9},{9,10},{10,1... | collective-permute-start | bytes 1474568 | tf_op jit(solution)/shard_map/ppermute | solution.py:31
  67.8 7.4 %copy-start.7 = (bf16[1024,512]{1,0:T(8,128)(2,1)S(1)}, bf16[1024,512]{1,0:T(8,128)(2,1)}, u32[]{:S(2)}) copy-start(bf16[1024,512]{1,0:T(8,128)(2,1)} %refs_18_.1) | copy-start | bytes 3145732
  67.8 7.4 %copy-start.8 = (bf16[512,1024]{1,0:T(8,128)(2,1)S(1)}, bf16[512,1024]{1,0:T(8,128)(2,1)}, u32[]{:S(2)}) copy-start(bf16[512,1024]{1,0:T(8,128)(2,1)} %narrow.1) | copy-start | bytes 3145732
  67.8 7.4 %copy-start.9 = (f32[1024]{0:T(1024)S(1)}, f32[1024]{0:T(1024)}, u32[]{:S(2)}) copy-start(f32[1024]{0:T(1024)} %param.16) | copy-start | bytes 12292
  85.1 1.0 copy-start.10
  86.1 1.0 copy-start.12
  87.0 0.8 copy-start.14
  87.8 41.5 %all-to-all-start = ((bf16[8,64,1280]{2,1,0:T(8,128)(2,1)}), bf16[8,64,1280]{2,1,0:T(8,128)(2,1)S(1)}, u32[]{:S(2)}, u32[]{:S(2)}) async-start(bf16[8,64,1280]{2,1,0:T(8,128)(2,1)} %bitcast.7), calls=%async_computation | async-start | bytes 2621440 | tf_op jit(solution)/shard_map/all_to_all | solution.py:340
  113.7 3.1 %copy-start.2 = (bf16[1792,16,128]{2,1,0:T(8,128)(2,1)S(1)}, bf16[1792,16,128]{2,1,0:T(8,128)(2,1)}, u32[]{:S(2)}) copy-start(bf16[1792,16,128]{2,1,0:T(8,128)(2,1)} %all-gather.3.cloned.1.call-done) | copy-start | bytes 22020100
  118.0 1.9 copy-start.3
  119.9 1.6 copy-start.5
  129.3 2.1 copy-start.4
  131.5 1.8 copy-start.6
  133.3 32.4 %copy-start.15 = (bf16[512,512]{1,0:T(8,128)(2,1)S(1)}, bf16[512,512]{1,0:T(8,128)(2,1)}, u32[]{:S(2)}) copy-start(bf16[512,512]{1,0:T(8,128)(2,1)} %copy-done.14) | copy-start | bytes 1572868
  136.3 29.4 %copy-start.11 = (bf16[512,1024]{1,0:T(8,128)(2,1)S(1)}, bf16[512,1024]{1,0:T(8,128)(2,1)}, u32[]{:S(2)}) copy-start(bf16[512,1024]{1,0:T(8,128)(2,1)} %copy-done.10) | copy-start | bytes 3145732
  136.3 29.4 %copy-start.13 = (f32[512,512]{1,0:T(8,128)S(1)}, f32[512,512]{1,0:T(8,128)}, u32[]{:S(2)}) copy-start(f32[512,512]{1,0:T(8,128)} %copy-done.12) | copy-start | bytes 3145732
  171.5 4.6 %collective-permute-start.7 = (bf16[32,32,512]{2,1,0:T(8,128)(2,1)S(1)}, bf16[32,32,512]{2,1,0:T(8,128)(2,1)S(1)}, u32[]{:S(2)}, u32[]{:S(2)}) collective-permute-start(bf16[32,32,512]{2,1,0:T(8,128)(2,1)S(1)} %get-tuple-element.23), channel_id=1, source_target_pairs={{0,8},{8,0},{1,9},{9,1},{2,10},{10,2},{3,11},{11,3},{4,12},{12,4},... | collective-permute-start | bytes 3145736 | tf_op jit(solution)/shard_map/ppermute | solution.py:351
Sparse Core Ops, SparseCore 0:
  11.2 102.4 all-gather.2

commit v5 on v4

--- a/solution.py
+++ b/solution.py
@@ -36,16 +36,22 @@
     return held
 
 
-def to_tiles(shard, per_piece):
+def to_tiles(shard):
     rows, cols = shard.shape
     tiles = shard.reshape(rows // 16, 16, cols // 128, 128).transpose(0, 2, 1, 3)
     tiles = tiles.reshape(-1, 16, 128)
-    spare = 16 * per_piece - tiles.shape[0]
+    spare = 128 - tiles.shape[0]
     tiles = jnp.concatenate([tiles, jnp.zeros((spare, 16, 128), tiles.dtype)])
-    return tiles.reshape(16, per_piece, 16, 128)
+    return tiles.reshape(64, 2, 16, 128)
+
+
+def to_everyone(array, axis, peers):
+    copies = jnp.broadcast_to(array, (peers, *array.shape))
+    return lax.all_to_all(copies, axis, 0, 0, tiled=True)
 
 
 VMEM = pl.BlockSpec(memory_space=pltpu.VMEM)
+HBM = pl.BlockSpec(memory_space=pltpu.HBM)
 SMEM = pl.BlockSpec(memory_space=pltpu.SMEM)
 LANES = (((1,), (1,)), ((), ()))
 
@@ -84,8 +90,9 @@
 
 def middle_body(me_ref, *refs):
     held, made, (place, gain, widen, narrow) = refs[:8], refs[8:16], refs[16:20]
-    normed_out, active_out, slope_out, joint, own_out, picked_out = refs[20:26]
-    rows_by, queries, keys, values = refs[26:]
+    *far, joint, own_out, picked_out = refs[20:26]
+    rows_by, queries, keys, values, normed_out, active_out, slope_out, sent = refs[26:]
+
     def prepare():
         me = me_ref[0]
         mine = pl.ds(pl.multiple_of(me * 64, 64), 64)
@@ -117,12 +124,12 @@
     rows = pl.ds(pl.multiple_of(step * 128, 128), 128)
     student = jnp.concatenate([rows_by[b, rows, :] for b in range(8)], axis=1).astype(F32)
     normed = layer_norm(student, gain[...]).astype(BF)
-    normed_out[...] = normed
+    normed_out[rows, :] = normed
     pre = jnp.dot(normed, widen[...], preferred_element_type=F32)
     half = 0.5 * (1.0 + lax.erf(pre * 0.7071067811865476))
     active = (pre * half).astype(BF)
-    active_out[...] = active
-    slope_out[...] = half + pre * 0.3989422804014327 * jnp.exp(-0.5 * pre * pre)
+    active_out[rows, :] = active
+    slope_out[rows, :] = half + pre * 0.3989422804014327 * jnp.exp(-0.5 * pre * pre)
     joint[:, :1024] = jnp.dot(active, narrow[...], preferred_element_type=F32).astype(BF)
 
     spots = lax.broadcasted_iota(jnp.int32, (128, 1024), 1)
@@ -141,6 +148,23 @@
     heads.append(jnp.zeros((128, 80), F32))
     joint[:, 1024:] = jnp.concatenate(heads, axis=1).astype(BF)
 
+    def sending(k, band):
+        near = (normed_out, active_out, slope_out)[k]
+        band_rows = pl.ds(pl.multiple_of(band * 128, 128), 128)
+        return pltpu.make_async_copy(
+            near.at[band_rows, :], far[k].at[band_rows, :], sent.at[k, band]
+        )
+
+    for k in range(3):
+        sending(k, step).start()
+
+    def finish():
+        for k in range(3):
+            for band in range(4):
+                sending(k, band).wait()
+
+    pl.when(step == 3)(finish)
+
 
 def middle(me, held, made, place, gain, widen, narrow):
     def banded(width):
@@ -161,9 +185,16 @@
             jax.ShapeDtypeStruct((64, TD), BF),
         ],
         in_specs=[SMEM] + [VMEM] * 20,
-        out_specs=[banded(1024), banded(512), banded(512), banded(1280), once(1024), once(TD)],
-        scratch_shapes=[pltpu.VMEM((8, 512, 128), BF)] + [pltpu.VMEM((1024, 256), BF)] * 3,
-        compiler_params=pltpu.CompilerParams(vmem_limit_bytes=14 << 20),
+        out_specs=[HBM, HBM, HBM, banded(1280), once(1024), once(TD)],
+        scratch_shapes=[pltpu.VMEM((8, 512, 128), BF)]
+        + [pltpu.VMEM((1024, 256), BF)] * 3
+        + [
+            pltpu.VMEM((512, 1024), BF),
+            pltpu.VMEM((512, 512), BF),
+            pltpu.VMEM((512, 512), F32),
+            pltpu.SemaphoreType.DMA((3, 4)),
+        ],
+        compiler_params=pltpu.CompilerParams(vmem_limit_bytes=48 << 20),
         cost_estimate=pl.CostEstimate(
             flops=2 * 512 * 1024 * (1024 + 768) + 2 * 64 * 1024 * TD,
             bytes_accessed=12_000_000,
@@ -172,14 +203,22 @@
     )(me, *held, *made, place, gain, widen, narrow)
 
 
-def loss_body(weight, arrived, own, picked, out_full, head_full, back_out):
+def loss_body(
+    weight, arrived, own, picked, out_far, head_far, back_out, out_full, head_full, arrivals
+):
+    out_copy = pltpu.make_async_copy(out_far, out_full, arrivals.at[0])
+    head_copy = pltpu.make_async_copy(head_far, head_full, arrivals.at[1])
+    out_copy.start()
+    head_copy.start()
     branch = arrived[0, :, :1024].astype(F32)
     for b in range(1, 8):
         branch += arrived[b, :, :1024].astype(F32)
     outputs = (own[...].astype(F32) + branch).astype(BF)
     joined = jnp.concatenate([arrived[b, :, 1024:].astype(F32)[:, :176] for b in range(8)], axis=1).astype(BF)
+    out_copy.wait()
     blended = lax.dot_general(joined, out_full[...], LANES, preferred_element_type=F32)
     targets = (picked[...].astype(F32) + blended).astype(BF).astype(F32)
+    head_copy.wait()
     predicted = lax.dot_general(outputs, head_full[...], LANES, preferred_element_type=F32)
     inner = jnp.sum(predicted * targets, axis=-1, keepdims=True)
     inv_pred = lax.rsqrt(jnp.sum(predicted * predicted, axis=-1, keepdims=True) + EPSILON)
@@ -204,13 +243,21 @@
 
 
 def loss_step(weight, arrived, own, picked, out_full, head_full):
-    return kernel_call(
+    return pl.pallas_call(
         loss_body,
-        [jax.ShapeDtypeStruct((8, 33, 16, 128), BF)],
-        flops=2 * 64 * 1408 * (1408 + 2048),
-        arrays=6,
-        moved=10_000_000,
-    )(weight, arrived, own, picked, out_full, head_full)[0]
+        out_shape=jax.ShapeDtypeStruct((8, 33, 16, 128), BF),
+        in_specs=[VMEM] * 4 + [HBM] * 2,
+        out_specs=VMEM,
+        scratch_shapes=[
+            pltpu.VMEM((TD, TD), BF),
+            pltpu.VMEM((TD, 1024), BF),
+            pltpu.SemaphoreType.DMA((2,)),
+        ],
+        compiler_params=pltpu.CompilerParams(vmem_limit_bytes=51 << 20),
+        cost_estimate=pl.CostEstimate(
+            flops=2 * 64 * 1408 * (1408 + 2048), bytes_accessed=10_000_000, transcendentals=0
+        ),
+    )(weight, arrived, own, picked, out_full, head_full)
 
 
 def assemble_body(pieces, out_full, head_full):
@@ -218,11 +265,11 @@
         for t in range(121):
             rows = pl.ds(pl.multiple_of(y * 176 + 16 * (t // 11), 16), 16)
             col = 128 * (t % 11)
-            out_full[rows, col : col + 128] = pieces[t // 8, y, t % 8]
+            out_full[rows, col : col + 128] = pieces[t // 8, t // 2 % 4, y, t % 2]
         for t in range(88):
             rows = pl.ds(pl.multiple_of(y * 176 + 16 * (t // 8), 16), 16)
             col = 128 * (t % 8)
-            head_full[rows, col : col + 128] = pieces[t // 6, y, 8 + t % 6]
+            head_full[rows, col : col + 128] = pieces[t // 8, t // 2 % 4, y, 2 + t % 2]
         return 0
 
     lax.fori_loop(0, 8, shard, 0)
@@ -315,15 +362,16 @@
     packed = jnp.concatenate([rows[128 * g : 128 * g + 128] for g in range(4)], axis=1)
     held = ring(jnp.concatenate([teacher_in[0], packed], axis=1))
 
-    at = lax.axis_index(("z", "c"))
+    at = lax.axis_index(("z", "c", "x"))
     mine = jnp.concatenate(
         [
-            lax.dynamic_index_in_dim(to_tiles(teacher_out, 8), at, 0, False),
-            lax.dynamic_index_in_dim(to_tiles(target_head, 6), at, 0, False),
+            lax.dynamic_index_in_dim(to_tiles(teacher_out), at, 0, False),
+            lax.dynamic_index_in_dim(to_tiles(target_head), at, 0, False),
         ]
     )
-    pieces = lax.all_gather(mine, ("z", "c", "mp"), axis=0)
-    out_full, head_full = assemble(pieces.reshape(16, 8, 14, 16, 128))
+    shares = to_everyone(to_everyone(mine, "mp", 8), "x", 4)
+    shares, _, _ = lax.optimization_barrier((shares, held[1], held[7]))
+    out_full, head_full = assemble(lax.all_gather(shares, ("z", "c"), axis=0))
 
     here = jnp.reshape(me, (1,)).astype(jnp.int32)
     made = [project(h, teacher_gain.reshape(1, -1), teacher_qkv) for h in held]

time: 219 us -> 222 us (1.014)
  waiting for transfers between devices: 60.1 us -> 42.1 us
  starting transfers between devices: 33.2 us -> 46 us
  blocking collectives: 63.6 us -> 70.2 us
  Pallas kernels: 27.2 us -> 32 us
  local copies, waits for them, and re-layouts: 17.4 us -> 14.7 us
    ppermute x4, waiting for transfers between devices: 32.4 us -> 14.4 us  [ring(): right = lax.ppermute(right, 'mp', shift(1))]
    all_gather x1, waiting for transfers between devices: 17.2 us -> 2.46 us  [on_device(): out_full, head_full = assemble(lax.all_gather(shares, ('z', 'c'), axis=0))]
    all_to_all x0 -> x2, starting transfers between devices: none -> 14.2 us  [to_everyone(): return lax.all_to_all(copies, axis, 0, 0, tiled=True)]
    all_to_all x1, blocking collectives: 34.2 us -> 43.6 us  [on_device(): kept = lax.all_to_all(kept, ('z', 'x'), 0, 0, tiled=True)]
    all_to_all x1, waiting for transfers between devices: 7.84 us -> 15.8 us  [on_device(): arrived = lax.all_to_all(joint.reshape(8, 64, 1280), 'mp', 0, 0, tiled=True)]
    unnamed x45 -> x41, local copies, waits for them, and re-layouts: 13.4 us -> 8.36 us
    all_to_all x0 -> x2, waiting for transfers between devices: none -> 5.02 us  [to_everyone(): return lax.all_to_all(copies, axis, 0, 0, tiled=True)]
    all_to_all x1, blocking collectives: 29.4 us -> 26.6 us  [on_device(): back = lax.all_to_all(back_own, 'mp', 0, 0, tiled=True)]
  transfers between devices with their start and end apart: 10 -> 12, of which waited for: 7 -> 9; matrix products, arithmetic and copies ran while one was open for 1% -> 2% of each run, Pallas kernels for 8% -> 9%
where the time goes in v5:
time: 222 us; the launch traced here: 221 us
  blocking collectives  70.2 us (32%)
  starting transfers between devices  46 us (21%)
  waiting for transfers between devices  42.1 us (19%)
  Pallas kernels  32 us (14%)
  between operations  15.2 us (7%)
  local copies, waits for them, and re-layouts  14.7 us (7%)
    all_to_all x1, blocking collectives, on_device(): kept = lax.all_to_all(kept, ('z', 'x'), 0, 0, tiled=True)  43.6 us
    all_to_all x1, blocking collectives, on_device(): back = lax.all_to_all(back_own, 'mp', 0, 0, tiled=True)  26.6 us
    all_to_all x1, waiting for transfers between devices, on_device(): arrived = lax.all_to_all(joint.reshape(8, 64, 1280), 'mp', 0, 0, tiled=True)  15.8 us
    ppermute x4, waiting for transfers between devices, ring(): right = lax.ppermute(right, 'mp', shift(1))  14.4 us
    all_to_all x2, starting transfers between devices, to_everyone(): return lax.all_to_all(copies, axis, 0, 0, tiled=True)  14.2 us
    ppermute x3, starting transfers between devices, ring(): left = lax.ppermute(left, 'mp', shift(-1))  13.3 us
    pallas_call x1, Pallas kernels, middle(): pl.pallas_call(middle_body, grid=(4,), out_shape=[jax.ShapeDtypeStruct((5...  12.2 us
    ppermute x4, starting transfers between devices, ring(): right = lax.ppermute(right, 'mp', shift(1))  10 us
  transfers between devices with their start and end apart: 12, of which 9 were waited for; matrix products, arithmetic and copies ran while one was open for 2% of the time, Pallas kernels for 9%

profile of v5, /device:TPU:2, one launch (start us, length us, event | category | flops | bytes accessed | tf_op | source)
XLA Modules:
  0.0 221.2 jit_solution(5664931145399812552)
XLA Ops:
  7.2 1.5 reshape.225
  9.8 7.1 %all-to-all-start.1 = ((bf16[8,4,16,128]{3,2,1,0:T(8,128)(2,1)}), bf16[8,4,16,128]{3,2,1,0:T(8,128)(2,1)}, u32[]{:S(2)}, u32[]{:S(2)}) async-start(bf16[8,4,16,128]{3,2,1,0:T(8,128)(2,1)} %broadcast_in_dim.19), calls=%async_computation.1 | async-start | bytes 262144 | tf_op jit(solution)/shard_map/all_to_all | solution.py:50
  17.6 1.3 gather_fusion
  19.0 3.9 %collective-permute-start = (bf16[128,1920]{1,0:T(8,128)(2,1)S(1)}, bf16[128,1920]{1,0:T(8,128)(2,1)S(1)}, u32[]{:S(2)}, u32[]{:S(2)}) collective-permute-start(bf16[128,1920]{1,0:T(8,128)(2,1)S(1)} %slice_dynamic-update-slice_fusion.block.refs_0_), channel_id=1, source_target_pairs={{0,1},{1,2},{2,3},{3,4},{4,5},{5,6},{6,7},{7,0},{8,9},{9,10},{10,1... | collective-permute-start | bytes 1474568 | tf_op jit(solution)/shard_map/ppermute | solution.py:31
  22.9 3.1 %collective-permute-start.4 = (bf16[128,1920]{1,0:T(8,128)(2,1)S(1)}, bf16[128,1920]{1,0:T(8,128)(2,1)S(1)}, u32[]{:S(2)}, u32[]{:S(2)}) collective-permute-start(bf16[128,1920]{1,0:T(8,128)(2,1)S(1)} %slice_dynamic-update-slice_fusion.block.refs_0_), channel_id=1, source_target_pairs={{0,7},{1,0},{2,1},{3,2},{4,3},{5,4},{6,5},{7,6},{8,15},{9,8},{10,9... | collective-permute-start | bytes 1474568 | tf_op jit(solution)/shard_map/ppermute | solution.py:34
  26.2 1.8 broadcast_in_dim.20
  28.0 7.1 %all-to-all-start.2 = ((bf16[4,8,4,16,128]{4,3,2,1,0:T(8,128)(2,1)}), bf16[4,8,4,16,128]{4,3,2,1,0:T(8,128)(2,1)}, u32[]{:S(2)}, u32[]{:S(2)}) async-start(bf16[4,8,4,16,128]{4,3,2,1,0:T(8,128)(2,1)} %broadcast_in_dim.20), calls=%async_computation.2 | async-start | bytes 1048576 | tf_op jit(solution)/shard_map/all_to_all | solution.py:50
  35.1 1.8 collective-permute-done.4.block.refs_7_
  37.0 4.9 %all-to-all-done.2 = bf16[4,8,4,16,128]{4,3,2,1,0:T(8,128)(2,1)} async-done(((bf16[4,8,4,16,128]{4,3,2,1,0:T(8,128)(2,1)}), bf16[4,8,4,16,128]{4,3,2,1,0:T(8,128)(2,1)}, u32[]{:S(2)}, u32[]{:S(2)}) %all-to-all-start.2) | async-done | bytes 524320 | tf_op jit(solution)/shard_map/all_to_all | solution.py:50
  41.9 2.3 %collective-permute-start.1 = (bf16[128,1920]{1,0:T(8,128)(2,1)S(1)}, bf16[128,1920]{1,0:T(8,128)(2,1)S(1)}, u32[]{:S(2)}, u32[]{:S(2)}) collective-permute-start(bf16[128,1920]{1,0:T(8,128)(2,1)S(1)} %collective-permute-done.block.refs_1_), channel_id=1, source_target_pairs={{0,1},{1,2},{2,3},{3,4},{4,5},{5,6},{6,7},{7,0},{8,9},{9,10},{10,1... | collective-permute-start | bytes 1474568 | tf_op jit(solution)/shard_map/ppermute | solution.py:31
  44.2 4.8 %collective-permute-start.5 = (bf16[128,1920]{1,0:T(8,128)(2,1)S(1)}, bf16[128,1920]{1,0:T(8,128)(2,1)S(1)}, u32[]{:S(2)}, u32[]{:S(2)}) collective-permute-start(bf16[128,1920]{1,0:T(8,128)(2,1)S(1)} %collective-permute-done.4.block.refs_7_), channel_id=1, source_target_pairs={{0,7},{1,0},{2,1},{3,2},{4,3},{5,4},{6,5},{7,6},{8,15},{9,8},{10,9... | collective-permute-start | bytes 1474568 | tf_op jit(solution)/shard_map/ppermute | solution.py:34
  48.9 5.0 %collective-permute-done.1.block.refs_2_ = bf16[128,1920]{1,0:T(8,128)(2,1)S(1)} collective-permute-done((bf16[128,1920]{1,0:T(8,128)(2,1)S(1)}, bf16[128,1920]{1,0:T(8,128)(2,1)S(1)}, u32[]{:S(2)}, u32[]{:S(2)}) %collective-permute-start.1) | collective-permute-done | bytes 491552 | tf_op jit(solution)/shard_map/ppermute | solution.py:31
  53.9 1.9 collective-permute-start.2
  55.9 5.4 %collective-permute-start.6 = (bf16[128,1920]{1,0:T(8,128)(2,1)S(1)}, bf16[128,1920]{1,0:T(8,128)(2,1)S(1)}, u32[]{:S(2)}, u32[]{:S(2)}) collective-permute-start(bf16[128,1920]{1,0:T(8,128)(2,1)S(1)} %collective-permute-done.5.block.refs_6_), channel_id=1, source_target_pairs={{0,7},{1,0},{2,1},{3,2},{4,3},{5,4},{6,5},{7,6},{8,15},{9,8},{10,9... | collective-permute-start | bytes 1474568 | tf_op jit(solution)/shard_map/ppermute | solution.py:34
  61.3 5.8 %collective-permute-done.2.block.refs_3_ = bf16[128,1920]{1,0:T(8,128)(2,1)S(1)} collective-permute-done((bf16[128,1920]{1,0:T(8,128)(2,1)S(1)}, bf16[128,1920]{1,0:T(8,128)(2,1)S(1)}, u32[]{:S(2)}, u32[]{:S(2)}) %collective-permute-start.2) | collective-permute-done | bytes 491552 | tf_op jit(solution)/shard_map/ppermute | solution.py:31
  67.1 1.9 collective-permute-start.3
  73.6 0.9 shard_map.133.refs_11_
  75.4 3.6 %collective-permute-done.3.block.refs_4_ = bf16[128,1920]{1,0:T(8,128)(2,1)S(1)} collective-permute-done((bf16[128,1920]{1,0:T(8,128)(2,1)S(1)}, bf16[128,1920]{1,0:T(8,128)(2,1)S(1)}, u32[]{:S(2)}, u32[]{:S(2)}) %collective-permute-start.3) | collective-permute-done | bytes 491552 | tf_op jit(solution)/shard_map/ppermute | solution.py:31
  79.9 12.2 %shard_map.138 = (bf16[512,1024]{1,0:T(8,128)(2,1)}, bf16[512,512]{1,0:T(8,128)(2,1)}, f32[512,512]{1,0:T(8,128)}, bf16[512,1280]{1,0:T(8,128)(2,1)}, bf16[64,10...) custom-call(s32[1]{0:T(128)} %bitcast.2.me_ref, bf16[128,1920]{1,0:T(8,128)(2,1)S(1)} %slice_dynamic-update-slice_fusion.block.refs_0_, ...), custom_call_target="tpu_custom_call" | custom-call | flops 2063597568 | bytes 12000000 | tf_op jit(solution)/shard_map/pallas_call | solution.py:176
  93.4 6.6 %all-to-all-start = ((bf16[8,64,1280]{2,1,0:T(8,128)(2,1)}), bf16[8,64,1280]{2,1,0:T(8,128)(2,1)S(1)}, u32[]{:S(2)}, u32[]{:S(2)}) async-start(bf16[8,64,1280]{2,1,0:T(8,128)(2,1)} %bitcast.35), calls=%async_computation | async-start | bytes 2621440 | tf_op jit(solution)/shard_map/all_to_all | solution.py:388
  100.7 2.5 %all-gather.3.cloned.1.call-done = bf16[64,8,4,16,128]{4,3,2,1,0:T(8,128)(2,1)} async-done(((bf16[4,8,4,16,128]{4,3,2,1,0:T(8,128)(2,1)}), bf16[64,8,4,16,128]{4,3,2,1,0:T(8,128)(2,1)}) %all-gather.3.cloned.1.call-update) | async-done | bytes 8388624 | tf_op jit(solution)/shard_map/all_gather | solution.py:374
  103.2 3.4 %copy-done.2 = bf16[64,8,4,16,128]{4,3,2,1,0:T(8,128)(2,1)S(1)} copy-done((bf16[64,8,4,16,128]{4,3,2,1,0:T(8,128)(2,1)S(1)}, bf16[64,8,4,16,128]{4,3,2,1,0:T(8,128)(2,1)}, u32[]{:S(2)}) %copy-start.2) | copy-done | bytes 8388632
  106.6 1.2 shard_map.139
  107.8 1.9 copy-done.3
  109.7 1.6 copy-done.4
  111.3 15.8 %all-to-all-done.arrived = bf16[8,64,1280]{2,1,0:T(8,128)(2,1)S(1)} async-done(((bf16[8,64,1280]{2,1,0:T(8,128)(2,1)}), bf16[8,64,1280]{2,1,0:T(8,128)(2,1)S(1)}, u32[]{:S(2)}, u32[]{:S(2)}) %all-to-all-start) | async-done | bytes 1310752 | tf_op jit(solution)/shard_map/all_to_all | solution.py:388
  127.1 5.5 %shard_map.140 = bf16[8,33,16,128]{3,2,1,0:T(8,128)(2,1)S(1)} custom-call(f32[64,1]{1,0:T(8,128)S(1)} %fusion.6.weight, bf16[8,64,1280]{2,1,0:T(8,128)(2,1)S(1)} %all-to-all-done.arrived, bf16[64,1024]{1,0:T(8,128)(2,1)S(1)} %copy-done.9, bf16[64,1408]{1,0:T(8,128)(2,1)S(1)} %copy-done.7, bf16[1408,1408]{1,0:T(8,128)(2,1)} %copy-done.3, ...), custom_call_target="tpu_custom_call" | custom-call | flops 622854144 | bytes 10000000 | tf_op jit(solution)/shard_map/pallas_call | solution.py:246
  132.6 26.6 %all_to_all.25.back_in = bf16[8,33,16,128]{3,2,1,0:T(8,128)(2,1)S(1)} all-to-all(bf16[8,33,16,128]{3,2,1,0:T(8,128)(2,1)S(1)} %shard_map.140), channel_id=1, replica_groups=mesh['z'=8,'x'=4,'c'=2,'mp'=8] {'mp'}, dimensions={0} | all-to-all | bytes 2162688 | tf_op jit(solution)/shard_map/all_to_all | solution.py:395
  159.2 5.8 %shard_map.141 = (bf16[32,32,512]{2,1,0:T(8,128)(2,1)S(1)}, bf16[32,32,512]{2,1,0:T(8,128)(2,1)S(1)}, f32[1]{0:T(128)}) custom-call(s32[1]{0:T(128)} %bitcast.core_ref, bf16[8,33,16,128]{3,2,1,0:T(8,128)(2,1)S(1)} %all_to_all.25.back_in, bf16[512,1024]{1,0:T(8,128)(2,1)S(1)} %copy-done.11, bf16[512,512]{1,0:T(8,128)(2,1)S(1)} %copy-done.13, ...), custom_call_target="tpu_custom_call" | custom-call | flops 1610612736 | bytes 8000000 | tf_op jit(solution)/shard_map/pallas_call | solution.py:331
  165.0 1.9 collective-permute-start.7
  166.9 2.6 %collective-permute-done.7 = bf16[32,32,512]{2,1,0:T(8,128)(2,1)S(1)} collective-permute-done((bf16[32,32,512]{2,1,0:T(8,128)(2,1)S(1)}, bf16[32,32,512]{2,1,0:T(8,128)(2,1)S(1)}, u32[]{:S(2)}, u32[]{:S(2)}) %collective-permute-start.7) | collective-permute-done | bytes 1048608 | tf_op jit(solution)/shard_map/ppermute | solution.py:399
  170.0 43.6 %all_to_all.26 = bf16[32,32,512]{2,1,0:T(8,128)(2,1)S(1)} all-to-all(bf16[32,32,512]{2,1,0:T(8,128)(2,1)S(1)} %add_convert_fusion), channel_id=1, replica_groups=mesh['z'=8,'x'=4,'c'=2,'mp'=8] {'z','x'}, dimensions={0} | all-to-all | bytes 2097152 | tf_op jit(solution)/shard_map/all_to_all | solution.py:401
  (68 shorter events, 10.8 us)
Async XLA Ops:
  7.2 10.4 %copy-start = (bf16[1,1024,128]{2,1,0:T(8,128)(2,1)S(1)}, bf16[1,1024,128]{2,1,0:T(8,128)(2,1)}, u32[]{:S(2)}) copy-start(bf16[1,1024,128]{2,1,0:T(8,128)(2,1)} %param.15) | copy-start | bytes 786436
  7.2 1.6 copy-start.14
  8.9 8.0 %copy-start.17 = (s32[1,512]{1,0:T(1,128)S(1)}, s32[1,512]{1,0:T(1,128)}, u32[]{:S(2)}) copy-start(s32[1,512]{1,0:T(1,128)} %param.20) | copy-start | bytes 6148
  8.9 8.6 %copy-start.15 = (bf16[1,128,1408]{2,1,0:T(8,128)(2,1)S(1)}, bf16[1,128,1408]{2,1,0:T(8,128)(2,1)}, u32[]{:S(2)}) copy-start(bf16[1,128,1408]{2,1,0:T(8,128)(2,1)} %param.11) | copy-start | bytes 1081348
  9.8 16.4 %all-to-all-start.1 = ((bf16[8,4,16,128]{3,2,1,0:T(8,128)(2,1)}), bf16[8,4,16,128]{3,2,1,0:T(8,128)(2,1)}, u32[]{:S(2)}, u32[]{:S(2)}) async-start(bf16[8,4,16,128]{3,2,1,0:T(8,128)(2,1)} %broadcast_in_dim.19), calls=%async_computation.1 | async-start | bytes 262144 | tf_op jit(solution)/shard_map/all_to_all | solution.py:50
  17.5 51.5 %copy-start.16 = (f32[1408]{0:T(1024)S(1)}, f32[1408]{0:T(1024)}, u32[]{:S(2)}) copy-start(f32[1408]{0:T(1024)} %param.12) | copy-start | bytes 16900
  17.5 51.5 %copy-start.1 = (bf16[3,176,1408]{2,1,0:T(8,128)(2,1)S(1)}, bf16[3,176,1408]{2,1,0:T(8,128)(2,1)}, u32[]{:S(2)}) copy-start(bf16[3,176,1408]{2,1,0:T(8,128)(2,1)} %weights.15) | copy-start | bytes 4460548
  19.0 16.1 %collective-permute-start = (bf16[128,1920]{1,0:T(8,128)(2,1)S(1)}, bf16[128,1920]{1,0:T(8,128)(2,1)S(1)}, u32[]{:S(2)}, u32[]{:S(2)}) collective-permute-start(bf16[128,1920]{1,0:T(8,128)(2,1)S(1)} %slice_dynamic-update-slice_fusion.block.refs_0_), channel_id=1, source_target_pairs={{0,1},{1,2},{2,3},{3,4},{4,5},{5,6},{6,7},{7,0},{8,9},{9,10},{10,1... | collective-permute-start | bytes 1474568 | tf_op jit(solution)/shard_map/ppermute | solution.py:31
  22.9 14.0 %collective-permute-start.4 = (bf16[128,1920]{1,0:T(8,128)(2,1)S(1)}, bf16[128,1920]{1,0:T(8,128)(2,1)S(1)}, u32[]{:S(2)}, u32[]{:S(2)}) collective-permute-start(bf16[128,1920]{1,0:T(8,128)(2,1)S(1)} %slice_dynamic-update-slice_fusion.block.refs_0_), channel_id=1, source_target_pairs={{0,7},{1,0},{2,1},{3,2},{4,3},{5,4},{6,5},{7,6},{8,15},{9,8},{10,9... | collective-permute-start | bytes 1474568 | tf_op jit(solution)/shard_map/ppermute | solution.py:34
  28.0 13.8 %all-to-all-start.2 = ((bf16[4,8,4,16,128]{4,3,2,1,0:T(8,128)(2,1)}), bf16[4,8,4,16,128]{4,3,2,1,0:T(8,128)(2,1)}, u32[]{:S(2)}, u32[]{:S(2)}) async-start(bf16[4,8,4,16,128]{4,3,2,1,0:T(8,128)(2,1)} %broadcast_in_dim.20), calls=%async_computation.2 | async-start | bytes 1048576 | tf_op jit(solution)/shard_map/all_to_all | solution.py:50
  35.1 68.1 %all-gather.3.cloned.1.call-start = ((), (), s32[]{:S(2)}) async-start(), calls=%async_computation.5 | async-start | bytes 8912896 | tf_op jit(solution)/shard_map/all_gather | solution.py:374
  41.9 12.1 %collective-permute-start.1 = (bf16[128,1920]{1,0:T(8,128)(2,1)S(1)}, bf16[128,1920]{1,0:T(8,128)(2,1)S(1)}, u32[]{:S(2)}, u32[]{:S(2)}) collective-permute-start(bf16[128,1920]{1,0:T(8,128)(2,1)S(1)} %collective-permute-done.block.refs_1_), channel_id=1, source_target_pairs={{0,1},{1,2},{2,3},{3,4},{4,5},{5,6},{6,7},{7,0},{8,9},{9,10},{10,1... | collective-permute-start | bytes 1474568 | tf_op jit(solution)/shard_map/ppermute | solution.py:31
  44.2 11.7 %collective-permute-start.5 = (bf16[128,1920]{1,0:T(8,128)(2,1)S(1)}, bf16[128,1920]{1,0:T(8,128)(2,1)S(1)}, u32[]{:S(2)}, u32[]{:S(2)}) collective-permute-start(bf16[128,1920]{1,0:T(8,128)(2,1)S(1)} %collective-permute-done.4.block.refs_7_), channel_id=1, source_target_pairs={{0,7},{1,0},{2,1},{3,2},{4,3},{5,4},{6,5},{7,6},{8,15},{9,8},{10,9... | collective-permute-start | bytes 1474568 | tf_op jit(solution)/shard_map/ppermute | solution.py:34
  53.9 13.1 %collective-permute-start.2 = (bf16[128,1920]{1,0:T(8,128)(2,1)S(1)}, bf16[128,1920]{1,0:T(8,128)(2,1)S(1)}, u32[]{:S(2)}, u32[]{:S(2)}) collective-permute-start(bf16[128,1920]{1,0:T(8,128)(2,1)S(1)} %collective-permute-done.1.block.refs_2_), channel_id=1, source_target_pairs={{0,1},{1,2},{2,3},{3,4},{4,5},{5,6},{6,7},{7,0},{8,9},{9,10},{10,1... | collective-permute-start | bytes 1474568 | tf_op jit(solution)/shard_map/ppermute | solution.py:31
  55.9 18.6 %collective-permute-start.6 = (bf16[128,1920]{1,0:T(8,128)(2,1)S(1)}, bf16[128,1920]{1,0:T(8,128)(2,1)S(1)}, u32[]{:S(2)}, u32[]{:S(2)}) collective-permute-start(bf16[128,1920]{1,0:T(8,128)(2,1)S(1)} %collective-permute-done.5.block.refs_6_), channel_id=1, source_target_pairs={{0,7},{1,0},{2,1},{3,2},{4,3},{5,4},{6,5},{7,6},{8,15},{9,8},{10,9... | collective-permute-start | bytes 1474568 | tf_op jit(solution)/shard_map/ppermute | solution.py:34
  67.1 11.9 %collective-permute-start.3 = (bf16[128,1920]{1,0:T(8,128)(2,1)S(1)}, bf16[128,1920]{1,0:T(8,128)(2,1)S(1)}, u32[]{:S(2)}, u32[]{:S(2)}) collective-permute-start(bf16[128,1920]{1,0:T(8,128)(2,1)S(1)} %collective-permute-done.2.block.refs_3_), channel_id=1, source_target_pairs={{0,1},{1,2},{2,3},{3,4},{4,5},{5,6},{6,7},{7,0},{8,9},{9,10},{10,1... | collective-permute-start | bytes 1474568 | tf_op jit(solution)/shard_map/ppermute | solution.py:31
  74.5 5.4 %copy-start.10 = (f32[1024]{0:T(1024)S(1)}, f32[1024]{0:T(1024)}, u32[]{:S(2)}) copy-start(f32[1024]{0:T(1024)} %param.16) | copy-start | bytes 12292
  92.1 0.7 copy-start.6
  92.8 0.6 copy-start.8
  93.4 33.6 %all-to-all-start = ((bf16[8,64,1280]{2,1,0:T(8,128)(2,1)}), bf16[8,64,1280]{2,1,0:T(8,128)(2,1)S(1)}, u32[]{:S(2)}, u32[]{:S(2)}) async-start(bf16[8,64,1280]{2,1,0:T(8,128)(2,1)} %bitcast.35), calls=%async_computation | async-start | bytes 2621440 | tf_op jit(solution)/shard_map/all_to_all | solution.py:388
  103.2 3.4 %copy-start.2 = (bf16[64,8,4,16,128]{4,3,2,1,0:T(8,128)(2,1)S(1)}, bf16[64,8,4,16,128]{4,3,2,1,0:T(8,128)(2,1)}, u32[]{:S(2)}) copy-start(bf16[64,8,4,16,128]{4,3,2,1,0:T(8,128)(2,1)} %all-gather.3.cloned.1.call-done) | copy-start | bytes 25165828
  106.6 20.5 %copy-start.7 = (bf16[64,1408]{1,0:T(8,128)(2,1)S(1)}, bf16[64,1408]{1,0:T(8,128)(2,1)}, u32[]{:S(2)}) copy-start(bf16[64,1408]{1,0:T(8,128)(2,1)} %copy-done.6) | copy-start | bytes 540676
  106.6 20.5 %copy-start.9 = (bf16[64,1024]{1,0:T(8,128)(2,1)S(1)}, bf16[64,1024]{1,0:T(8,128)(2,1)}, u32[]{:S(2)}) copy-start(bf16[64,1024]{1,0:T(8,128)(2,1)} %copy-done.8) | copy-start | bytes 393220
  107.8 1.9 copy-start.3
  109.7 1.6 copy-start.4
  127.1 32.1 %copy-start.12 = (f32[512,512]{1,0:T(8,128)S(1)}, f32[512,512]{1,0:T(8,128)}, u32[]{:S(2)}) copy-start(f32[512,512]{1,0:T(8,128)} %get-tuple-element.23.slope) | copy-start | bytes 3145732
  127.1 32.1 %copy-start.13 = (bf16[512,512]{1,0:T(8,128)(2,1)S(1)}, bf16[512,512]{1,0:T(8,128)(2,1)}, u32[]{:S(2)}) copy-start(bf16[512,512]{1,0:T(8,128)(2,1)} %get-tuple-element.22.active) | copy-start | bytes 1572868
  132.6 26.6 %copy-start.5 = (bf16[512,1024]{1,0:T(8,128)(2,1)S(1)}, bf16[512,1024]{1,0:T(8,128)(2,1)}, u32[]{:S(2)}) copy-start(bf16[512,1024]{1,0:T(8,128)(2,1)} %narrow.1) | copy-start | bytes 3145732
  132.6 26.6 %copy-start.11 = (bf16[512,1024]{1,0:T(8,128)(2,1)S(1)}, bf16[512,1024]{1,0:T(8,128)(2,1)}, u32[]{:S(2)}) copy-start(bf16[512,1024]{1,0:T(8,128)(2,1)} %get-tuple-element.21.normed) | copy-start | bytes 3145732
  165.0 4.6 %collective-permute-start.7 = (bf16[32,32,512]{2,1,0:T(8,128)(2,1)S(1)}, bf16[32,32,512]{2,1,0:T(8,128)(2,1)S(1)}, u32[]{:S(2)}, u32[]{:S(2)}) collective-permute-start(bf16[32,32,512]{2,1,0:T(8,128)(2,1)S(1)} %get-tuple-element.25), channel_id=1, source_target_pairs={{0,8},{8,0},{1,9},{9,1},{2,10},{10,2},{3,11},{11,3},{4,12},{12,4},... | collective-permute-start | bytes 3145736 | tf_op jit(solution)/shard_map/ppermute | solution.py:399
Sparse Core Ops, SparseCore 0:
  42.0 61.1 all-gather.2

commit v6 on v5

--- a/solution.py
+++ b/solution.py
@@ -36,18 +36,13 @@
     return held
 
 
-def to_tiles(shard):
+def to_tiles(shard, per_piece):
     rows, cols = shard.shape
     tiles = shard.reshape(rows // 16, 16, cols // 128, 128).transpose(0, 2, 1, 3)
     tiles = tiles.reshape(-1, 16, 128)
-    spare = 128 - tiles.shape[0]
+    spare = 16 * per_piece - tiles.shape[0]
     tiles = jnp.concatenate([tiles, jnp.zeros((spare, 16, 128), tiles.dtype)])
-    return tiles.reshape(64, 2, 16, 128)
-
-
-def to_everyone(array, axis, peers):
-    copies = jnp.broadcast_to(array, (peers, *array.shape))
-    return lax.all_to_all(copies, axis, 0, 0, tiled=True)
+    return tiles.reshape(16, per_piece, 16, 128)
 
 
 VMEM = pl.BlockSpec(memory_space=pltpu.VMEM)
@@ -261,26 +256,26 @@
 
 
 def assemble_body(pieces, out_full, head_full):
-    def shard(y, _):
-        for t in range(121):
-            rows = pl.ds(pl.multiple_of(y * 176 + 16 * (t // 11), 16), 16)
-            col = 128 * (t % 11)
-            out_full[rows, col : col + 128] = pieces[t // 8, t // 2 % 4, y, t % 2]
-        for t in range(88):
-            rows = pl.ds(pl.multiple_of(y * 176 + 16 * (t // 8), 16), 16)
-            col = 128 * (t % 8)
-            head_full[rows, col : col + 128] = pieces[t // 8, t // 2 % 4, y, 2 + t % 2]
-        return 0
-
-    lax.fori_loop(0, 8, shard, 0)
+    for t in range(121):
+        r, c = 16 * (t // 11), 128 * (t % 11)
+        out_full[r : r + 16, c : c + 128] = pieces[t // 8, 0, t % 8]
+    for t in range(88):
+        r, c = 16 * (t // 8), 128 * (t % 8)
+        head_full[r : r + 16, c : c + 128] = pieces[t // 6, 0, 8 + t % 6]
 
 
 def assemble(pieces):
-    return kernel_call(
+    return pl.pallas_call(
         assemble_body,
-        [jax.ShapeDtypeStruct((TD, TD), BF), jax.ShapeDtypeStruct((TD, 1024), BF)],
-        arrays=1,
-        moved=14_000_000,
+        grid=(8,),
+        out_shape=[jax.ShapeDtypeStruct((TD, TD), BF), jax.ShapeDtypeStruct((TD, 1024), BF)],
+        in_specs=[pl.BlockSpec((16, 1, 14, 16, 128), lambda y: (0, y, 0, 0, 0))],
+        out_specs=[
+            pl.BlockSpec((176, TD), lambda y: (y, 0)),
+            pl.BlockSpec((176, 1024), lambda y: (y, 0)),
+        ],
+        compiler_params=pltpu.CompilerParams(vmem_limit_bytes=56 << 20),
+        cost_estimate=pl.CostEstimate(flops=0, bytes_accessed=14_000_000, transcendentals=0),
     )(pieces)
 
 
@@ -362,16 +357,15 @@
     packed = jnp.concatenate([rows[128 * g : 128 * g + 128] for g in range(4)], axis=1)
     held = ring(jnp.concatenate([teacher_in[0], packed], axis=1))
 
-    at = lax.axis_index(("z", "c", "x"))
+    at = lax.axis_index(("z", "c"))
     mine = jnp.concatenate(
         [
-            lax.dynamic_index_in_dim(to_tiles(teacher_out), at, 0, False),
-            lax.dynamic_index_in_dim(to_tiles(target_head), at, 0, False),
+            lax.dynamic_index_in_dim(to_tiles(teacher_out, 8), at, 0, False),
+            lax.dynamic_index_in_dim(to_tiles(target_head, 6), at, 0, False),
         ]
     )
-    shares = to_everyone(to_everyone(mine, "mp", 8), "x", 4)
-    shares, _, _ = lax.optimization_barrier((shares, held[1], held[7]))
-    out_full, head_full = assemble(lax.all_gather(shares, ("z", "c"), axis=0))
+    pieces = lax.all_gather(mine, ("z", "c", "mp"), axis=0)
+    out_full, head_full = assemble(pieces.reshape(16, 8, 14, 16, 128))
 
     here = jnp.reshape(me, (1,)).astype(jnp.int32)
     made = [project(h, teacher_gain.reshape(1, -1), teacher_qkv) for h in held]

time: 222 us -> 218 us (0.982)
  waiting for transfers between devices: 42.1 us -> 59.5 us
  starting transfers between devices: 46 us -> 33.2 us
  local copies, waits for them, and re-layouts: 14.7 us -> 4.11 us
  Pallas kernels: 32 us -> 39.3 us
  blocking collectives: 70.2 us -> 64.7 us
    ppermute x4, waiting for transfers between devices: 14.4 us -> 32.5 us  [ring(): right = lax.ppermute(right, 'mp', shift(1))]
    all_gather x1, waiting for transfers between devices: 2.46 us -> 18 us  [on_device(): pieces = lax.all_gather(mine, ('z', 'c', 'mp'), axis=0)]
    all_to_all x2 -> x0, starting transfers between devices: 14.2 us -> none  [to_everyone(): return lax.all_to_all(copies, axis, 0, 0, tiled=True)]
    all_to_all x1, waiting for transfers between devices: 15.8 us -> 6.37 us  [on_device(): arrived = lax.all_to_all(joint.reshape(8, 64, 1280), 'mp', 0, 0, tiled=True)]
    all_to_all x1, blocking collectives: 43.6 us -> 35.4 us  [on_device(): kept = lax.all_to_all(kept, ('z', 'x'), 0, 0, tiled=True)]
    unnamed x41 -> x27, local copies, waits for them, and re-layouts: 8.36 us -> 0.19 us
    pallas_call x1, Pallas kernels: 1.22 us -> 8.55 us  [assemble(): pl.pallas_call(assemble_body, grid=(8,), out_shape=[jax.ShapeDtypeStruct(...]
    all_to_all x2 -> x0, waiting for transfers between devices: 5.02 us -> none  [to_everyone(): return lax.all_to_all(copies, axis, 0, 0, tiled=True)]
  transfers between devices with their start and end apart: 12 -> 10, of which waited for: 9 -> 7; matrix products, arithmetic and copies ran while one was open for 2% -> 1% of each run, Pallas kernels for 9% -> 13%
where the time goes in v6:
time: 218 us
  blocking collectives  64.7 us (30%)
  waiting for transfers between devices  59.5 us (27%)
  Pallas kernels  39.3 us (18%)
  starting transfers between devices  33.2 us (15%)
  between operations  15.2 us (7%)
  local copies, waits for them, and re-layouts  4.11 us (2%)
    all_to_all x1, blocking collectives, on_device(): kept = lax.all_to_all(kept, ('z', 'x'), 0, 0, tiled=True)  35.4 us
    ppermute x4, waiting for transfers between devices, ring(): right = lax.ppermute(right, 'mp', shift(1))  32.5 us
    all_to_all x1, blocking collectives, on_device(): back = lax.all_to_all(back_own, 'mp', 0, 0, tiled=True)  29.3 us
    all_gather x1, waiting for transfers between devices, on_device(): pieces = lax.all_gather(mine, ('z', 'c', 'mp'), axis=0)  18 us
    ppermute x3, starting transfers between devices, ring(): left = lax.ppermute(left, 'mp', shift(-1))  14.1 us
    pallas_call x1, Pallas kernels, middle(): pl.pallas_call(middle_body, grid=(4,), out_shape=[jax.ShapeDtypeStruct((5...  12.2 us
    ppermute x4, starting transfers between devices, ring(): right = lax.ppermute(right, 'mp', shift(1))  9.21 us
    pallas_call x1, Pallas kernels, assemble(): pl.pallas_call(assemble_body, grid=(8,), out_shape=[jax.ShapeDtypeStruct(...  8.55 us
  transfers between devices with their start and end apart: 10, of which 7 were waited for; matrix products, arithmetic and copies ran while one was open for 1% of the time, Pallas kernels for 13%

profile of v6, /device:TPU:2, one launch (start us, length us, event | category | flops | bytes accessed | tf_op | source)
XLA Modules:
  0.0 217.7 jit_solution(10244233937244952152)
XLA Ops:
  7.2 1.5 reshape.228
  10.5 1.3 gather_fusion
  12.0 3.5 %collective-permute-start = (bf16[128,1920]{1,0:T(8,128)(2,1)S(1)}, bf16[128,1920]{1,0:T(8,128)(2,1)S(1)}, u32[]{:S(2)}, u32[]{:S(2)}) collective-permute-start(bf16[128,1920]{1,0:T(8,128)(2,1)S(1)} %slice_dynamic-update-slice_fusion.block.refs_0_), channel_id=1, source_target_pairs={{0,1},{1,2},{2,3},{3,4},{4,5},{5,6},{6,7},{7,0},{8,9},{9,10},{10,1... | collective-permute-start | bytes 1474568 | tf_op jit(solution)/shard_map/ppermute | solution.py:31
  15.5 3.8 %collective-permute-start.4 = (bf16[128,1920]{1,0:T(8,128)(2,1)S(1)}, bf16[128,1920]{1,0:T(8,128)(2,1)S(1)}, u32[]{:S(2)}, u32[]{:S(2)}) collective-permute-start(bf16[128,1920]{1,0:T(8,128)(2,1)S(1)} %slice_dynamic-update-slice_fusion.block.refs_0_), channel_id=1, source_target_pairs={{0,7},{1,0},{2,1},{3,2},{4,3},{5,4},{6,5},{7,6},{8,15},{9,8},{10,9... | collective-permute-start | bytes 1474568 | tf_op jit(solution)/shard_map/ppermute | solution.py:34
  19.3 9.3 %collective-permute-done.block.refs_1_ = bf16[128,1920]{1,0:T(8,128)(2,1)S(1)} collective-permute-done((bf16[128,1920]{1,0:T(8,128)(2,1)S(1)}, bf16[128,1920]{1,0:T(8,128)(2,1)S(1)}, u32[]{:S(2)}, u32[]{:S(2)}) %collective-permute-start) | collective-permute-done | bytes 491552 | tf_op jit(solution)/shard_map/ppermute | solution.py:31
  28.6 1.9 collective-permute-start.1
  30.5 5.1 %collective-permute-start.5 = (bf16[128,1920]{1,0:T(8,128)(2,1)S(1)}, bf16[128,1920]{1,0:T(8,128)(2,1)S(1)}, u32[]{:S(2)}, u32[]{:S(2)}) collective-permute-start(bf16[128,1920]{1,0:T(8,128)(2,1)S(1)} %collective-permute-done.4.block.refs_7_), channel_id=1, source_target_pairs={{0,7},{1,0},{2,1},{3,2},{4,3},{5,4},{6,5},{7,6},{8,15},{9,8},{10,9... | collective-permute-start | bytes 1474568 | tf_op jit(solution)/shard_map/ppermute | solution.py:34
  35.6 9.4 %collective-permute-done.1.block.refs_2_ = bf16[128,1920]{1,0:T(8,128)(2,1)S(1)} collective-permute-done((bf16[128,1920]{1,0:T(8,128)(2,1)S(1)}, bf16[128,1920]{1,0:T(8,128)(2,1)S(1)}, u32[]{:S(2)}, u32[]{:S(2)}) %collective-permute-start.1) | collective-permute-done | bytes 491552 | tf_op jit(solution)/shard_map/ppermute | solution.py:31
  45.0 1.9 collective-permute-start.2
  46.9 5.1 %collective-permute-start.6 = (bf16[128,1920]{1,0:T(8,128)(2,1)S(1)}, bf16[128,1920]{1,0:T(8,128)(2,1)S(1)}, u32[]{:S(2)}, u32[]{:S(2)}) collective-permute-start(bf16[128,1920]{1,0:T(8,128)(2,1)S(1)} %collective-permute-done.5.block.refs_6_), channel_id=1, source_target_pairs={{0,7},{1,0},{2,1},{3,2},{4,3},{5,4},{6,5},{7,6},{8,15},{9,8},{10,9... | collective-permute-start | bytes 1474568 | tf_op jit(solution)/shard_map/ppermute | solution.py:34
  52.1 8.2 %collective-permute-done.2.block.refs_3_ = bf16[128,1920]{1,0:T(8,128)(2,1)S(1)} collective-permute-done((bf16[128,1920]{1,0:T(8,128)(2,1)S(1)}, bf16[128,1920]{1,0:T(8,128)(2,1)S(1)}, u32[]{:S(2)}, u32[]{:S(2)}) %collective-permute-start.2) | collective-permute-done | bytes 491552 | tf_op jit(solution)/shard_map/ppermute | solution.py:31
  60.3 1.9 collective-permute-start.3
  62.3 0.9 shard_map.130.refs_8_
  63.2 0.9 shard_map.131.refs_9_
  64.1 0.9 shard_map.137.refs_15_
  65.0 0.9 shard_map.132.refs_10_
  65.9 0.9 shard_map.136.refs_14_
  66.8 0.9 shard_map.133.refs_11_
  67.8 0.9 shard_map.135.refs_13_
  68.7 5.6 %collective-permute-done.3.block.refs_4_ = bf16[128,1920]{1,0:T(8,128)(2,1)S(1)} collective-permute-done((bf16[128,1920]{1,0:T(8,128)(2,1)S(1)}, bf16[128,1920]{1,0:T(8,128)(2,1)S(1)}, u32[]{:S(2)}, u32[]{:S(2)}) %collective-permute-start.3) | collective-permute-done | bytes 491552 | tf_op jit(solution)/shard_map/ppermute | solution.py:31
  74.2 0.9 shard_map.134.refs_12_
  75.2 12.2 %shard_map.138 = (bf16[512,1024]{1,0:T(8,128)(2,1)}, bf16[512,512]{1,0:T(8,128)(2,1)}, f32[512,512]{1,0:T(8,128)}, bf16[512,1280]{1,0:T(8,128)(2,1)}, bf16[64,10...) custom-call(s32[1]{0:T(128)} %bitcast.2.me_ref, bf16[128,1920]{1,0:T(8,128)(2,1)S(1)} %slice_dynamic-update-slice_fusion.block.refs_0_, ...), custom_call_target="tpu_custom_call" | custom-call | flops 2063597568 | bytes 12000000 | tf_op jit(solution)/shard_map/pallas_call | solution.py:171
  87.4 8.0 %all-to-all-start = ((bf16[8,64,1280]{2,1,0:T(8,128)(2,1)}), bf16[8,64,1280]{2,1,0:T(8,128)(2,1)S(1)}, u32[]{:S(2)}, u32[]{:S(2)}) async-start(bf16[8,64,1280]{2,1,0:T(8,128)(2,1)} %bitcast.35), calls=%async_computation | async-start | bytes 2621440 | tf_op jit(solution)/shard_map/all_to_all | solution.py:382
  96.1 18.0 %all-gather.3.cloned.1.call-done = bf16[1792,16,128]{2,1,0:T(8,128)(2,1)} async-done(((bf16[14,16,128]{2,1,0:T(8,128)(2,1)}), bf16[1792,16,128]{2,1,0:T(8,128)(2,1)}) %all-gather.3.cloned.1.call-update) | async-done | bytes 7340048 | tf_op jit(solution)/shard_map/all_gather | solution.py:367
  114.1 8.5 %shard_map.139 = (bf16[1408,1408]{1,0:T(8,128)(2,1)}, bf16[1408,1024]{1,0:T(8,128)(2,1)}) custom-call(bf16[16,8,14,16,128]{4,3,2,1,0:T(8,128)(2,1)} %bitcast.30), custom_call_target="tpu_custom_call" | custom-call | bytes 14000000 | tf_op jit(solution)/shard_map/pallas_call | solution.py:268
  122.7 6.4 %all-to-all-done.arrived = bf16[8,64,1280]{2,1,0:T(8,128)(2,1)S(1)} async-done(((bf16[8,64,1280]{2,1,0:T(8,128)(2,1)}), bf16[8,64,1280]{2,1,0:T(8,128)(2,1)S(1)}, u32[]{:S(2)}, u32[]{:S(2)}) %all-to-all-start) | async-done | bytes 1310752 | tf_op jit(solution)/shard_map/all_to_all | solution.py:382
  129.0 5.5 %shard_map.140 = bf16[8,33,16,128]{3,2,1,0:T(8,128)(2,1)S(1)} custom-call(f32[64,1]{1,0:T(8,128)S(1)} %fusion.6.weight, bf16[8,64,1280]{2,1,0:T(8,128)(2,1)S(1)} %all-to-all-done.arrived, bf16[64,1024]{1,0:T(8,128)(2,1)S(1)} %get-tuple-element.15.own, bf16[64,1408]{1,0:T(8,128)(2,1)S(1)} %get-tuple-element.16.picked, ...), custom_call_target="tpu_custom_call" | custom-call | flops 622854144 | bytes 10000000 | tf_op jit(solution)/shard_map/pallas_call | solution.py:241
  134.6 29.3 %all_to_all.15.back_in = bf16[8,33,16,128]{3,2,1,0:T(8,128)(2,1)S(1)} all-to-all(bf16[8,33,16,128]{3,2,1,0:T(8,128)(2,1)S(1)} %shard_map.140), channel_id=1, replica_groups=mesh['z'=8,'x'=4,'c'=2,'mp'=8] {'mp'}, dimensions={0} | all-to-all | bytes 2162688 | tf_op jit(solution)/shard_map/all_to_all | solution.py:389
  163.9 5.8 %shard_map.141 = (bf16[32,32,512]{2,1,0:T(8,128)(2,1)S(1)}, bf16[32,32,512]{2,1,0:T(8,128)(2,1)S(1)}, f32[1]{0:T(128)}) custom-call(s32[1]{0:T(128)} %bitcast.core_ref, bf16[8,33,16,128]{3,2,1,0:T(8,128)(2,1)S(1)} %all_to_all.15.back_in, bf16[512,1024]{1,0:T(8,128)(2,1)S(1)} %copy-done.4, bf16[512,512]{1,0:T(8,128)(2,1)S(1)} %copy-done.6, ...), custom_call_target="tpu_custom_call" | custom-call | flops 1610612736 | bytes 8000000 | tf_op jit(solution)/shard_map/pallas_call | solution.py:326
  169.7 1.9 collective-permute-start.7
  171.6 2.6 %collective-permute-done.7 = bf16[32,32,512]{2,1,0:T(8,128)(2,1)S(1)} collective-permute-done((bf16[32,32,512]{2,1,0:T(8,128)(2,1)S(1)}, bf16[32,32,512]{2,1,0:T(8,128)(2,1)S(1)}, u32[]{:S(2)}, u32[]{:S(2)}) %collective-permute-start.7) | collective-permute-done | bytes 1048608 | tf_op jit(solution)/shard_map/ppermute | solution.py:393
  174.6 35.4 %all_to_all.16 = bf16[32,32,512]{2,1,0:T(8,128)(2,1)S(1)} all-to-all(bf16[32,32,512]{2,1,0:T(8,128)(2,1)S(1)} %add_convert_fusion), channel_id=1, replica_groups=mesh['z'=8,'x'=4,'c'=2,'mp'=8] {'z','x'}, dimensions={0} | all-to-all | bytes 2097152 | tf_op jit(solution)/shard_map/all_to_all | solution.py:395
  (49 shorter events, 3.0 us)
Async XLA Ops:
  7.2 3.3 %copy-start = (bf16[1,1024,128]{2,1,0:T(8,128)(2,1)S(1)}, bf16[1,1024,128]{2,1,0:T(8,128)(2,1)}, u32[]{:S(2)}) copy-start(bf16[1,1024,128]{2,1,0:T(8,128)(2,1)} %param.15) | copy-start | bytes 786436
  7.2 1.7 copy-start.7
  7.2 106.9 %all-gather.3.cloned.1.call-start = ((), (), s32[]{:S(2)}) async-start(), calls=%async_computation.3 | async-start | bytes 7397376 | tf_op jit(solution)/shard_map/all_gather | solution.py:367
  8.9 1.0 copy-start.10
  9.1 2.8 %copy-start.8 = (bf16[1,128,1408]{2,1,0:T(8,128)(2,1)S(1)}, bf16[1,128,1408]{2,1,0:T(8,128)(2,1)}, u32[]{:S(2)}) copy-start(bf16[1,128,1408]{2,1,0:T(8,128)(2,1)} %param.11) | copy-start | bytes 1081348
  9.1 53.1 %copy-start.9 = (f32[1408]{0:T(1024)S(1)}, f32[1408]{0:T(1024)}, u32[]{:S(2)}) copy-start(f32[1408]{0:T(1024)} %param.12) | copy-start | bytes 16900
  9.1 53.1 %copy-start.1 = (bf16[3,176,1408]{2,1,0:T(8,128)(2,1)S(1)}, bf16[3,176,1408]{2,1,0:T(8,128)(2,1)}, u32[]{:S(2)}) copy-start(bf16[3,176,1408]{2,1,0:T(8,128)(2,1)} %weights.15) | copy-start | bytes 4460548
  12.0 16.6 %collective-permute-start = (bf16[128,1920]{1,0:T(8,128)(2,1)S(1)}, bf16[128,1920]{1,0:T(8,128)(2,1)S(1)}, u32[]{:S(2)}, u32[]{:S(2)}) collective-permute-start(bf16[128,1920]{1,0:T(8,128)(2,1)S(1)} %slice_dynamic-update-slice_fusion.block.refs_0_), channel_id=1, source_target_pairs={{0,1},{1,2},{2,3},{3,4},{4,5},{5,6},{6,7},{7,0},{8,9},{9,10},{10,1... | collective-permute-start | bytes 1474568 | tf_op jit(solution)/shard_map/ppermute | solution.py:31
  15.5 15.0 %collective-permute-start.4 = (bf16[128,1920]{1,0:T(8,128)(2,1)S(1)}, bf16[128,1920]{1,0:T(8,128)(2,1)S(1)}, u32[]{:S(2)}, u32[]{:S(2)}) collective-permute-start(bf16[128,1920]{1,0:T(8,128)(2,1)S(1)} %slice_dynamic-update-slice_fusion.block.refs_0_), channel_id=1, source_target_pairs={{0,7},{1,0},{2,1},{3,2},{4,3},{5,4},{6,5},{7,6},{8,15},{9,8},{10,9... | collective-permute-start | bytes 1474568 | tf_op jit(solution)/shard_map/ppermute | solution.py:34
  28.6 16.5 %collective-permute-start.1 = (bf16[128,1920]{1,0:T(8,128)(2,1)S(1)}, bf16[128,1920]{1,0:T(8,128)(2,1)S(1)}, u32[]{:S(2)}, u32[]{:S(2)}) collective-permute-start(bf16[128,1920]{1,0:T(8,128)(2,1)S(1)} %collective-permute-done.block.refs_1_), channel_id=1, source_target_pairs={{0,1},{1,2},{2,3},{3,4},{4,5},{5,6},{6,7},{7,0},{8,9},{9,10},{10,1... | collective-permute-start | bytes 1474568 | tf_op jit(solution)/shard_map/ppermute | solution.py:31
  30.5 16.5 %collective-permute-start.5 = (bf16[128,1920]{1,0:T(8,128)(2,1)S(1)}, bf16[128,1920]{1,0:T(8,128)(2,1)S(1)}, u32[]{:S(2)}, u32[]{:S(2)}) collective-permute-start(bf16[128,1920]{1,0:T(8,128)(2,1)S(1)} %collective-permute-done.4.block.refs_7_), channel_id=1, source_target_pairs={{0,7},{1,0},{2,1},{3,2},{4,3},{5,4},{6,5},{7,6},{8,15},{9,8},{10,9... | collective-permute-start | bytes 1474568 | tf_op jit(solution)/shard_map/ppermute | solution.py:34
  45.0 15.3 %collective-permute-start.2 = (bf16[128,1920]{1,0:T(8,128)(2,1)S(1)}, bf16[128,1920]{1,0:T(8,128)(2,1)S(1)}, u32[]{:S(2)}, u32[]{:S(2)}) collective-permute-start(bf16[128,1920]{1,0:T(8,128)(2,1)S(1)} %collective-permute-done.1.block.refs_2_), channel_id=1, source_target_pairs={{0,1},{1,2},{2,3},{3,4},{4,5},{5,6},{6,7},{7,0},{8,9},{9,10},{10,1... | collective-permute-start | bytes 1474568 | tf_op jit(solution)/shard_map/ppermute | solution.py:31
  46.9 20.8 %collective-permute-start.6 = (bf16[128,1920]{1,0:T(8,128)(2,1)S(1)}, bf16[128,1920]{1,0:T(8,128)(2,1)S(1)}, u32[]{:S(2)}, u32[]{:S(2)}) collective-permute-start(bf16[128,1920]{1,0:T(8,128)(2,1)S(1)} %collective-permute-done.5.block.refs_6_), channel_id=1, source_target_pairs={{0,7},{1,0},{2,1},{3,2},{4,3},{5,4},{6,5},{7,6},{8,15},{9,8},{10,9... | collective-permute-start | bytes 1474568 | tf_op jit(solution)/shard_map/ppermute | solution.py:34
  60.3 13.9 %collective-permute-start.3 = (bf16[128,1920]{1,0:T(8,128)(2,1)S(1)}, bf16[128,1920]{1,0:T(8,128)(2,1)S(1)}, u32[]{:S(2)}, u32[]{:S(2)}) collective-permute-start(bf16[128,1920]{1,0:T(8,128)(2,1)S(1)} %collective-permute-done.2.block.refs_3_), channel_id=1, source_target_pairs={{0,1},{1,2},{2,3},{3,4},{4,5},{5,6},{6,7},{7,0},{8,9},{9,10},{10,1... | collective-permute-start | bytes 1474568 | tf_op jit(solution)/shard_map/ppermute | solution.py:31
  67.7 7.4 %copy-start.3 = (f32[1024]{0:T(1024)S(1)}, f32[1024]{0:T(1024)}, u32[]{:S(2)}) copy-start(f32[1024]{0:T(1024)} %param.16) | copy-start | bytes 12292
  87.4 41.7 %all-to-all-start = ((bf16[8,64,1280]{2,1,0:T(8,128)(2,1)}), bf16[8,64,1280]{2,1,0:T(8,128)(2,1)S(1)}, u32[]{:S(2)}, u32[]{:S(2)}) async-start(bf16[8,64,1280]{2,1,0:T(8,128)(2,1)} %bitcast.35), calls=%async_computation | async-start | bytes 2621440 | tf_op jit(solution)/shard_map/all_to_all | solution.py:382
  129.0 34.8 %copy-start.5 = (f32[512,512]{1,0:T(8,128)S(1)}, f32[512,512]{1,0:T(8,128)}, u32[]{:S(2)}) copy-start(f32[512,512]{1,0:T(8,128)} %get-tuple-element.21.slope) | copy-start | bytes 3145732
  129.0 34.8 %copy-start.6 = (bf16[512,512]{1,0:T(8,128)(2,1)S(1)}, bf16[512,512]{1,0:T(8,128)(2,1)}, u32[]{:S(2)}) copy-start(bf16[512,512]{1,0:T(8,128)(2,1)} %get-tuple-element.20.active) | copy-start | bytes 1572868
  134.6 29.3 %copy-start.2 = (bf16[512,1024]{1,0:T(8,128)(2,1)S(1)}, bf16[512,1024]{1,0:T(8,128)(2,1)}, u32[]{:S(2)}) copy-start(bf16[512,1024]{1,0:T(8,128)(2,1)} %narrow.1) | copy-start | bytes 3145732
  134.6 29.3 %copy-start.4 = (bf16[512,1024]{1,0:T(8,128)(2,1)S(1)}, bf16[512,1024]{1,0:T(8,128)(2,1)}, u32[]{:S(2)}) copy-start(bf16[512,1024]{1,0:T(8,128)(2,1)} %get-tuple-element.19.normed) | copy-start | bytes 3145732
  169.7 4.6 %collective-permute-start.7 = (bf16[32,32,512]{2,1,0:T(8,128)(2,1)S(1)}, bf16[32,32,512]{2,1,0:T(8,128)(2,1)S(1)}, u32[]{:S(2)}, u32[]{:S(2)}) collective-permute-start(bf16[32,32,512]{2,1,0:T(8,128)(2,1)S(1)} %get-tuple-element.23), channel_id=1, source_target_pairs={{0,8},{8,0},{1,9},{9,1},{2,10},{10,2},{3,11},{11,3},{4,12},{12,4},... | collective-permute-start | bytes 3145736 | tf_op jit(solution)/shard_map/ppermute | solution.py:393
Sparse Core Ops, SparseCore 0:
  11.2 102.9 all-gather.2

commit v7 on v6

--- a/solution.py
+++ b/solution.py
@@ -36,13 +36,18 @@
     return held
 
 
-def to_tiles(shard, per_piece):
+def to_tiles(shard):
     rows, cols = shard.shape
     tiles = shard.reshape(rows // 16, 16, cols // 128, 128).transpose(0, 2, 1, 3)
     tiles = tiles.reshape(-1, 16, 128)
-    spare = 16 * per_piece - tiles.shape[0]
+    spare = 128 - tiles.shape[0]
     tiles = jnp.concatenate([tiles, jnp.zeros((spare, 16, 128), tiles.dtype)])
-    return tiles.reshape(16, per_piece, 16, 128)
+    return tiles.reshape(64, 2, 16, 128)
+
+
+def to_everyone(array, axis, peers):
+    copies = jnp.broadcast_to(array, (peers, *array.shape))
+    return lax.all_to_all(copies, axis, 0, 0, tiled=True)
 
 
 VMEM = pl.BlockSpec(memory_space=pltpu.VMEM)
@@ -258,10 +263,10 @@
 def assemble_body(pieces, out_full, head_full):
     for t in range(121):
         r, c = 16 * (t // 11), 128 * (t % 11)
-        out_full[r : r + 16, c : c + 128] = pieces[t // 8, 0, t % 8]
+        out_full[r : r + 16, c : c + 128] = pieces[t // 8, t // 2 % 4, 0, t % 2]
     for t in range(88):
         r, c = 16 * (t // 8), 128 * (t % 8)
-        head_full[r : r + 16, c : c + 128] = pieces[t // 6, 0, 8 + t % 6]
+        head_full[r : r + 16, c : c + 128] = pieces[t // 8, t // 2 % 4, 0, 2 + t % 2]
 
 
 def assemble(pieces):
@@ -269,7 +274,7 @@
         assemble_body,
         grid=(8,),
         out_shape=[jax.ShapeDtypeStruct((TD, TD), BF), jax.ShapeDtypeStruct((TD, 1024), BF)],
-        in_specs=[pl.BlockSpec((16, 1, 14, 16, 128), lambda y: (0, y, 0, 0, 0))],
+        in_specs=[pl.BlockSpec((16, 4, 1, 4, 16, 128), lambda y: (0, 0, y, 0, 0, 0))],
         out_specs=[
             pl.BlockSpec((176, TD), lambda y: (y, 0)),
             pl.BlockSpec((176, 1024), lambda y: (y, 0)),
@@ -357,15 +362,16 @@
     packed = jnp.concatenate([rows[128 * g : 128 * g + 128] for g in range(4)], axis=1)
     held = ring(jnp.concatenate([teacher_in[0], packed], axis=1))
 
-    at = lax.axis_index(("z", "c"))
+    at = lax.axis_index(("z", "c", "x"))
     mine = jnp.concatenate(
         [
-            lax.dynamic_index_in_dim(to_tiles(teacher_out, 8), at, 0, False),
-            lax.dynamic_index_in_dim(to_tiles(target_head, 6), at, 0, False),
+            lax.dynamic_index_in_dim(to_tiles(teacher_out), at, 0, False),
+            lax.dynamic_index_in_dim(to_tiles(target_head), at, 0, False),
         ]
     )
-    pieces = lax.all_gather(mine, ("z", "c", "mp"), axis=0)
-    out_full, head_full = assemble(pieces.reshape(16, 8, 14, 16, 128))
+    shares = to_everyone(to_everyone(mine, "mp", 8), "x", 4)
+    shares, _, _ = lax.optimization_barrier((shares, held[2], held[6]))
+    out_full, head_full = assemble(lax.all_gather(shares, ("z", "c"), axis=0))
 
     here = jnp.reshape(me, (1,)).astype(jnp.int32)
     made = [project(h, teacher_gain.reshape(1, -1), teacher_qkv) for h in held]

time: 218 us -> 220 us (level)
  waiting for transfers between devices: 59.5 us -> 30.8 us
  blocking collectives: 64.7 us -> 83.1 us
  local copies, waits for them, and re-layouts: 4.11 us -> 11 us
  Pallas kernels: 39.3 us -> 42.1 us
  starting transfers between devices: 33.2 us -> 35.9 us
    ppermute x4, waiting for transfers between devices: 32.5 us -> 7.26 us  [ring(): right = lax.ppermute(right, 'mp', shift(1))]
    all_to_all x0 -> x1, blocking collectives: none -> 12.5 us  [to_everyone(): return lax.all_to_all(copies, axis, 0, 0, tiled=True)]
    all_to_all x0 -> x1, starting transfers between devices: none -> 6.86 us  [to_everyone(): return lax.all_to_all(copies, axis, 0, 0, tiled=True)]
    all_to_all x1, blocking collectives: 29.3 us -> 33.7 us  [on_device(): back = lax.all_to_all(back_own, 'mp', 0, 0, tiled=True)]
    all_to_all x1, starting transfers between devices: 7.99 us -> 3.79 us  [on_device(): arrived = lax.all_to_all(joint.reshape(8, 64, 1280), 'mp', 0, 0, tiled=True)]
    all_to_all x1, waiting for transfers between devices: 6.37 us -> 2.83 us  [on_device(): arrived = lax.all_to_all(joint.reshape(8, 64, 1280), 'mp', 0, 0, tiled=True)]
    unnamed x27 -> x31, local copies, waits for them, and re-layouts: 0.19 us -> 3.47 us
    all_gather x1, waiting for transfers between devices: 18 us -> 15.3 us  [on_device(): out_full, head_full = assemble(lax.all_gather(shares, ('z', 'c'), axis=0))]
  transfers between devices with their start and end apart: 10 -> 11, of which waited for: 7 -> 6; matrix products, arithmetic and copies ran while one was open for 1% -> 3% of each run, Pallas kernels for 13% -> 14%
where the time goes in v7:
time: 220 us; the launch traced here: 219 us
  blocking collectives  83.1 us (38%)
  Pallas kernels  42.1 us (19%)
  starting transfers between devices  35.9 us (16%)
  waiting for transfers between devices  30.8 us (14%)
  between operations  15.2 us (7%)
  local copies, waits for them, and re-layouts  11 us (5%)
    all_to_all x1, blocking collectives, on_device(): kept = lax.all_to_all(kept, ('z', 'x'), 0, 0, tiled=True)  36.9 us
    all_to_all x1, blocking collectives, on_device(): back = lax.all_to_all(back_own, 'mp', 0, 0, tiled=True)  33.7 us
    all_gather x1, waiting for transfers between devices, on_device(): out_full, head_full = assemble(lax.all_gather(shares, ('z', 'c'), axis=0))  15.3 us
    pallas_call x1, Pallas kernels, middle(): pl.pallas_call(middle_body, grid=(4,), out_shape=[jax.ShapeDtypeStruct((5...  12.6 us
    all_to_all x1, blocking collectives, to_everyone(): return lax.all_to_all(copies, axis, 0, 0, tiled=True)  12.5 us
    ppermute x3, starting transfers between devices, ring(): left = lax.ppermute(left, 'mp', shift(-1))  12 us
    ppermute x4, starting transfers between devices, ring(): right = lax.ppermute(right, 'mp', shift(1))  11.3 us
    pallas_call x8, Pallas kernels, project(): kernel_call(project_body, [jax.ShapeDtypeStruct((128, 768), BF)], flops=2...  9.3 us
  transfers between devices with their start and end apart: 11, of which 6 were waited for; matrix products, arithmetic and copies ran while one was open for 3% of the time, Pallas kernels for 14%

profile of v7, /device:TPU:2, one launch (start us, length us, event | category | flops | bytes accessed | tf_op | source)
XLA Modules:
  0.0 219.0 jit_solution(88570358699661616)
XLA Ops:
  8.5 1.0 bitcast_dynamic-update-slice_fusion
  9.6 1.3 gather_fusion
  11.0 3.5 %collective-permute-start = (bf16[128,1920]{1,0:T(8,128)(2,1)S(1)}, bf16[128,1920]{1,0:T(8,128)(2,1)S(1)}, u32[]{:S(2)}, u32[]{:S(2)}) collective-permute-start(bf16[128,1920]{1,0:T(8,128)(2,1)S(1)} %slice_dynamic-update-slice_fusion.block.refs_0_), channel_id=1, source_target_pairs={{0,1},{1,2},{2,3},{3,4},{4,5},{5,6},{6,7},{7,0},{8,9},{9,10},{10,1... | collective-permute-start | bytes 1474568 | tf_op jit(solution)/shard_map/ppermute | solution.py:31
  14.5 3.8 %collective-permute-start.4 = (bf16[128,1920]{1,0:T(8,128)(2,1)S(1)}, bf16[128,1920]{1,0:T(8,128)(2,1)S(1)}, u32[]{:S(2)}, u32[]{:S(2)}) collective-permute-start(bf16[128,1920]{1,0:T(8,128)(2,1)S(1)} %slice_dynamic-update-slice_fusion.block.refs_0_), channel_id=1, source_target_pairs={{0,7},{1,0},{2,1},{3,2},{4,3},{5,4},{6,5},{7,6},{8,15},{9,8},{10,9... | collective-permute-start | bytes 1474568 | tf_op jit(solution)/shard_map/ppermute | solution.py:34
  18.8 1.0 copy.37
  23.1 6.9 %all-to-all-start.1 = ((bf16[8,4,16,128]{3,2,1,0:T(8,128)(2,1)}), bf16[8,4,16,128]{3,2,1,0:T(8,128)(2,1)}, u32[]{:S(2)}, u32[]{:S(2)}) async-start(bf16[8,4,16,128]{3,2,1,0:T(8,128)(2,1)} %broadcast_in_dim.19), calls=%async_computation.1 | async-start | bytes 262144 | tf_op jit(solution)/shard_map/all_to_all | solution.py:50
  30.0 3.9 %collective-permute-start.1 = (bf16[128,1920]{1,0:T(8,128)(2,1)S(1)}, bf16[128,1920]{1,0:T(8,128)(2,1)}, u32[]{:S(2)}, u32[]{:S(2)}) collective-permute-start(bf16[128,1920]{1,0:T(8,128)(2,1)S(1)} %collective-permute-done.block.refs_1_), channel_id=1, source_target_pairs={{0,1},{1,2},{2,3},{3,4},{4,5},{5,6},{6,7},{7,0},{8,9},{9,10},{10,1... | collective-permute-start | bytes 1474568 | tf_op jit(solution)/shard_map/ppermute | solution.py:31
  33.9 3.2 %collective-permute-start.5 = (bf16[128,1920]{1,0:T(8,128)(2,1)S(1)}, bf16[128,1920]{1,0:T(8,128)(2,1)}, u32[]{:S(2)}, u32[]{:S(2)}) collective-permute-start(bf16[128,1920]{1,0:T(8,128)(2,1)S(1)} %collective-permute-done.4.block.refs_7_), channel_id=1, source_target_pairs={{0,7},{1,0},{2,1},{3,2},{4,3},{5,4},{6,5},{7,6},{8,15},{9,8},{10,9... | collective-permute-start | bytes 1474568 | tf_op jit(solution)/shard_map/ppermute | solution.py:34
  37.1 2.8 %all-to-all-done.1 = bf16[8,4,16,128]{3,2,1,0:T(8,128)(2,1)} async-done(((bf16[8,4,16,128]{3,2,1,0:T(8,128)(2,1)}), bf16[8,4,16,128]{3,2,1,0:T(8,128)(2,1)}, u32[]{:S(2)}, u32[]{:S(2)}) %all-to-all-start.1) | async-done | bytes 131104 | tf_op jit(solution)/shard_map/all_to_all | solution.py:50
  39.9 1.0 broadcast_in_dim.20
  40.9 12.5 %all_to_all.25 = bf16[4,8,4,16,128]{4,3,2,1,0:T(8,128)(2,1)} all-to-all(bf16[4,8,4,16,128]{4,3,2,1,0:T(8,128)(2,1)S(1)} %broadcast_in_dim.20), channel_id=1, replica_groups=mesh['z'=8,'x'=4,'c'=2,'mp'=8] {'x'}, dimensions={0} | all-to-all | bytes 1048576 | tf_op jit(solution)/shard_map/all_to_all | solution.py:50
  53.4 2.1 collective-permute-start.2
  55.4 5.0 %collective-permute-start.6 = (bf16[128,1920]{1,0:T(8,128)(2,1)}, bf16[128,1920]{1,0:T(8,128)(2,1)S(1)}, u32[]{:S(2)}, u32[]{:S(2)}) collective-permute-start(bf16[128,1920]{1,0:T(8,128)(2,1)} %collective-permute-done.5.block.refs_6_), channel_id=1, source_target_pairs={{0,7},{1,0},{2,1},{3,2},{4,3},{5,4},{6,5},{7,6},{8,15},{9,8},{10,9... | collective-permute-start | bytes 1474568 | tf_op jit(solution)/shard_map/ppermute | solution.py:34
  60.4 5.8 %collective-permute-done.2.block.refs_3_ = bf16[128,1920]{1,0:T(8,128)(2,1)S(1)} collective-permute-done((bf16[128,1920]{1,0:T(8,128)(2,1)}, bf16[128,1920]{1,0:T(8,128)(2,1)S(1)}, u32[]{:S(2)}, u32[]{:S(2)}) %collective-permute-start.2) | collective-permute-done | bytes 491552 | tf_op jit(solution)/shard_map/ppermute | solution.py:31
  66.2 1.9 collective-permute-start.3
  70.0 0.9 shard_map.137.refs_15_
  70.9 1.9 shard_map.132.refs_10_
  72.8 1.9 shard_map.136.refs_14_
  74.8 0.9 shard_map.133.refs_11_
  76.6 1.5 collective-permute-done.3.block.refs_4_
  78.1 0.9 shard_map.134.refs_12_
  79.0 12.6 %shard_map.138 = (bf16[512,1024]{1,0:T(8,128)(2,1)}, bf16[512,512]{1,0:T(8,128)(2,1)}, f32[512,512]{1,0:T(8,128)}, bf16[512,1280]{1,0:T(8,128)(2,1)}, bf16[64,10...) custom-call(s32[1]{0:T(128)} %bitcast.2.me_ref, bf16[128,1920]{1,0:T(8,128)(2,1)S(1)} %slice_dynamic-update-slice_fusion.block.refs_0_, ...), custom_call_target="tpu_custom_call" | custom-call | flops 2063597568 | bytes 12000000 | tf_op jit(solution)/shard_map/pallas_call | solution.py:176
  93.0 3.8 %all-to-all-start = ((bf16[8,64,1280]{2,1,0:T(8,128)(2,1)}), bf16[8,64,1280]{2,1,0:T(8,128)(2,1)S(1)}, u32[]{:S(2)}, u32[]{:S(2)}) async-start(bf16[8,64,1280]{2,1,0:T(8,128)(2,1)} %bitcast.35), calls=%async_computation | async-start | bytes 2621440 | tf_op jit(solution)/shard_map/all_to_all | solution.py:388
  97.5 15.3 %all-gather.3.cloned.1.call-done = bf16[64,8,4,16,128]{4,3,2,1,0:T(8,128)(2,1)} async-done(((bf16[4,8,4,16,128]{4,3,2,1,0:T(8,128)(2,1)}), bf16[64,8,4,16,128]{4,3,2,1,0:T(8,128)(2,1)}) %all-gather.3.cloned.1.call-update) | async-done | bytes 8388624 | tf_op jit(solution)/shard_map/all_gather | solution.py:374
  112.8 8.9 %shard_map.139 = (bf16[1408,1408]{1,0:T(8,128)(2,1)}, bf16[1408,1024]{1,0:T(8,128)(2,1)}) custom-call(bf16[16,4,8,4,16,128]{5,4,3,2,1,0:T(8,128)(2,1)} %bitcast.30), custom_call_target="tpu_custom_call" | custom-call | bytes 14000000 | tf_op jit(solution)/shard_map/pallas_call | solution.py:273
  121.6 2.8 %all-to-all-done.arrived = bf16[8,64,1280]{2,1,0:T(8,128)(2,1)S(1)} async-done(((bf16[8,64,1280]{2,1,0:T(8,128)(2,1)}), bf16[8,64,1280]{2,1,0:T(8,128)(2,1)S(1)}, u32[]{:S(2)}, u32[]{:S(2)}) %all-to-all-start) | async-done | bytes 1310752 | tf_op jit(solution)/shard_map/all_to_all | solution.py:388
  124.5 5.5 %shard_map.140 = bf16[8,33,16,128]{3,2,1,0:T(8,128)(2,1)S(1)} custom-call(f32[64,1]{1,0:T(8,128)S(1)} %fusion.6.weight, bf16[8,64,1280]{2,1,0:T(8,128)(2,1)S(1)} %all-to-all-done.arrived, bf16[64,1024]{1,0:T(8,128)(2,1)S(1)} %copy-done.6, bf16[64,1408]{1,0:T(8,128)(2,1)S(1)} %copy-done.4, bf16[1408,1408]{1,0:T(8,128)(2,1)} %get-tuple-element.19.out_far, ...), custom_call_target="tpu_custom_call" | custom-call | flops 622854144 | bytes 10000000 | tf_op jit(solution)/shard_map/pallas_call | solution.py:246
  130.0 33.7 %all_to_all.26.back_in = bf16[8,33,16,128]{3,2,1,0:T(8,128)(2,1)S(1)} all-to-all(bf16[8,33,16,128]{3,2,1,0:T(8,128)(2,1)S(1)} %shard_map.140), channel_id=1, replica_groups=mesh['z'=8,'x'=4,'c'=2,'mp'=8] {'mp'}, dimensions={0} | all-to-all | bytes 2162688 | tf_op jit(solution)/shard_map/all_to_all | solution.py:395
  163.7 5.8 %shard_map.141 = (bf16[32,32,512]{2,1,0:T(8,128)(2,1)S(1)}, bf16[32,32,512]{2,1,0:T(8,128)(2,1)S(1)}, f32[1]{0:T(128)}) custom-call(s32[1]{0:T(128)} %bitcast.core_ref, bf16[8,33,16,128]{3,2,1,0:T(8,128)(2,1)S(1)} %all_to_all.26.back_in, bf16[512,1024]{1,0:T(8,128)(2,1)S(1)} %copy-done.8, bf16[512,512]{1,0:T(8,128)(2,1)S(1)} %copy-done.10, ...), custom_call_target="tpu_custom_call" | custom-call | flops 1610612736 | bytes 8000000 | tf_op jit(solution)/shard_map/pallas_call | solution.py:331
  169.5 1.9 collective-permute-start.7
  171.5 2.6 %collective-permute-done.7 = bf16[32,32,512]{2,1,0:T(8,128)(2,1)S(1)} collective-permute-done((bf16[32,32,512]{2,1,0:T(8,128)(2,1)S(1)}, bf16[32,32,512]{2,1,0:T(8,128)(2,1)S(1)}, u32[]{:S(2)}, u32[]{:S(2)}) %collective-permute-start.7) | collective-permute-done | bytes 1048608 | tf_op jit(solution)/shard_map/ppermute | solution.py:399
  174.5 36.9 %all_to_all.27 = bf16[32,32,512]{2,1,0:T(8,128)(2,1)S(1)} all-to-all(bf16[32,32,512]{2,1,0:T(8,128)(2,1)S(1)} %add_convert_fusion), channel_id=1, replica_groups=mesh['z'=8,'x'=4,'c'=2,'mp'=8] {'z','x'}, dimensions={0} | all-to-all | bytes 2097152 | tf_op jit(solution)/shard_map/all_to_all | solution.py:401
  (57 shorter events, 10.4 us)
Async XLA Ops:
  7.2 2.4 %copy-start = (bf16[1,1024,128]{2,1,0:T(8,128)(2,1)S(1)}, bf16[1,1024,128]{2,1,0:T(8,128)(2,1)}, u32[]{:S(2)}) copy-start(bf16[1,1024,128]{2,1,0:T(8,128)(2,1)} %param.15) | copy-start | bytes 786436
  7.2 11.1 %copy-start.11 = (bf16[176,1408]{1,0:T(8,128)(2,1)S(1)}, bf16[176,1408]{1,0:T(8,128)(2,1)}, u32[]{:S(2)}) copy-start(bf16[176,1408]{1,0:T(8,128)(2,1)} %param.14) | copy-start | bytes 1486852
  11.0 19.0 %collective-permute-start = (bf16[128,1920]{1,0:T(8,128)(2,1)S(1)}, bf16[128,1920]{1,0:T(8,128)(2,1)S(1)}, u32[]{:S(2)}, u32[]{:S(2)}) collective-permute-start(bf16[128,1920]{1,0:T(8,128)(2,1)S(1)} %slice_dynamic-update-slice_fusion.block.refs_0_), channel_id=1, source_target_pairs={{0,1},{1,2},{2,3},{3,4},{4,5},{5,6},{6,7},{7,0},{8,9},{9,10},{10,1... | collective-permute-start | bytes 1474568 | tf_op jit(solution)/shard_map/ppermute | solution.py:31
  14.5 19.4 %collective-permute-start.4 = (bf16[128,1920]{1,0:T(8,128)(2,1)S(1)}, bf16[128,1920]{1,0:T(8,128)(2,1)S(1)}, u32[]{:S(2)}, u32[]{:S(2)}) collective-permute-start(bf16[128,1920]{1,0:T(8,128)(2,1)S(1)} %slice_dynamic-update-slice_fusion.block.refs_0_), channel_id=1, source_target_pairs={{0,7},{1,0},{2,1},{3,2},{4,3},{5,4},{6,5},{7,6},{8,15},{9,8},{10,9... | collective-permute-start | bytes 1474568 | tf_op jit(solution)/shard_map/ppermute | solution.py:34
  19.9 48.2 %copy-start.12 = (f32[1408]{0:T(1024)S(1)}, f32[1408]{0:T(1024)}, u32[]{:S(2)}) copy-start(f32[1408]{0:T(1024)} %param.12) | copy-start | bytes 16900
  20.0 48.2 %copy-start.1 = (bf16[3,176,1408]{2,1,0:T(8,128)(2,1)S(1)}, bf16[3,176,1408]{2,1,0:T(8,128)(2,1)}, u32[]{:S(2)}) copy-start(bf16[3,176,1408]{2,1,0:T(8,128)(2,1)} %weights.15) | copy-start | bytes 4460548
  23.1 16.7 %all-to-all-start.1 = ((bf16[8,4,16,128]{3,2,1,0:T(8,128)(2,1)}), bf16[8,4,16,128]{3,2,1,0:T(8,128)(2,1)}, u32[]{:S(2)}, u32[]{:S(2)}) async-start(bf16[8,4,16,128]{3,2,1,0:T(8,128)(2,1)} %broadcast_in_dim.19), calls=%async_computation.1 | async-start | bytes 262144 | tf_op jit(solution)/shard_map/all_to_all | solution.py:50
  30.0 82.8 %all-gather.3.cloned.1.call-start = ((), (), s32[]{:S(2)}) async-start(), calls=%async_computation.5 | async-start | bytes 8912896 | tf_op jit(solution)/shard_map/all_gather | solution.py:374
  30.0 23.3 %collective-permute-start.1 = (bf16[128,1920]{1,0:T(8,128)(2,1)S(1)}, bf16[128,1920]{1,0:T(8,128)(2,1)}, u32[]{:S(2)}, u32[]{:S(2)}) collective-permute-start(bf16[128,1920]{1,0:T(8,128)(2,1)S(1)} %collective-permute-done.block.refs_1_), channel_id=1, source_target_pairs={{0,1},{1,2},{2,3},{3,4},{4,5},{5,6},{6,7},{7,0},{8,9},{9,10},{10,1... | collective-permute-start | bytes 1474568 | tf_op jit(solution)/shard_map/ppermute | solution.py:31
  33.9 19.4 %collective-permute-start.5 = (bf16[128,1920]{1,0:T(8,128)(2,1)S(1)}, bf16[128,1920]{1,0:T(8,128)(2,1)}, u32[]{:S(2)}, u32[]{:S(2)}) collective-permute-start(bf16[128,1920]{1,0:T(8,128)(2,1)S(1)} %collective-permute-done.4.block.refs_7_), channel_id=1, source_target_pairs={{0,7},{1,0},{2,1},{3,2},{4,3},{5,4},{6,5},{7,6},{8,15},{9,8},{10,9... | collective-permute-start | bytes 1474568 | tf_op jit(solution)/shard_map/ppermute | solution.py:34
  53.4 12.8 %collective-permute-start.2 = (bf16[128,1920]{1,0:T(8,128)(2,1)}, bf16[128,1920]{1,0:T(8,128)(2,1)S(1)}, u32[]{:S(2)}, u32[]{:S(2)}) collective-permute-start(bf16[128,1920]{1,0:T(8,128)(2,1)} %collective-permute-done.1.block.refs_2_), channel_id=1, source_target_pairs={{0,1},{1,2},{2,3},{3,4},{4,5},{5,6},{6,7},{7,0},{8,9},{9,10},{10,1... | collective-permute-start | bytes 1474568 | tf_op jit(solution)/shard_map/ppermute | solution.py:31
  55.4 20.3 %collective-permute-start.6 = (bf16[128,1920]{1,0:T(8,128)(2,1)}, bf16[128,1920]{1,0:T(8,128)(2,1)S(1)}, u32[]{:S(2)}, u32[]{:S(2)}) collective-permute-start(bf16[128,1920]{1,0:T(8,128)(2,1)} %collective-permute-done.5.block.refs_6_), channel_id=1, source_target_pairs={{0,7},{1,0},{2,1},{3,2},{4,3},{5,4},{6,5},{7,6},{8,15},{9,8},{10,9... | collective-permute-start | bytes 1474568 | tf_op jit(solution)/shard_map/ppermute | solution.py:34
  66.2 11.9 %collective-permute-start.3 = (bf16[128,1920]{1,0:T(8,128)(2,1)S(1)}, bf16[128,1920]{1,0:T(8,128)(2,1)S(1)}, u32[]{:S(2)}, u32[]{:S(2)}) collective-permute-start(bf16[128,1920]{1,0:T(8,128)(2,1)S(1)} %collective-permute-done.2.block.refs_3_), channel_id=1, source_target_pairs={{0,1},{1,2},{2,3},{3,4},{4,5},{5,6},{6,7},{7,0},{8,9},{9,10},{10,1... | collective-permute-start | bytes 1474568 | tf_op jit(solution)/shard_map/ppermute | solution.py:31
  75.7 3.3 %copy-start.7 = (f32[1024]{0:T(1024)S(1)}, f32[1024]{0:T(1024)}, u32[]{:S(2)}) copy-start(f32[1024]{0:T(1024)} %param.16) | copy-start | bytes 12292
  91.7 0.7 copy-start.3
  92.3 0.7 copy-start.5
  93.0 31.4 %all-to-all-start = ((bf16[8,64,1280]{2,1,0:T(8,128)(2,1)}), bf16[8,64,1280]{2,1,0:T(8,128)(2,1)S(1)}, u32[]{:S(2)}, u32[]{:S(2)}) async-start(bf16[8,64,1280]{2,1,0:T(8,128)(2,1)} %bitcast.35), calls=%async_computation | async-start | bytes 2621440 | tf_op jit(solution)/shard_map/all_to_all | solution.py:388
  112.8 11.7 %copy-start.4 = (bf16[64,1408]{1,0:T(8,128)(2,1)S(1)}, bf16[64,1408]{1,0:T(8,128)(2,1)}, u32[]{:S(2)}) copy-start(bf16[64,1408]{1,0:T(8,128)(2,1)} %copy-done.3) | copy-start | bytes 540676
  112.8 11.7 %copy-start.6 = (bf16[64,1024]{1,0:T(8,128)(2,1)S(1)}, bf16[64,1024]{1,0:T(8,128)(2,1)}, u32[]{:S(2)}) copy-start(bf16[64,1024]{1,0:T(8,128)(2,1)} %copy-done.5) | copy-start | bytes 393220
  124.4 39.3 %copy-start.9 = (f32[512,512]{1,0:T(8,128)S(1)}, f32[512,512]{1,0:T(8,128)}, u32[]{:S(2)}) copy-start(f32[512,512]{1,0:T(8,128)} %get-tuple-element.23.slope) | copy-start | bytes 3145732
  124.4 39.3 %copy-start.10 = (bf16[512,512]{1,0:T(8,128)(2,1)S(1)}, bf16[512,512]{1,0:T(8,128)(2,1)}, u32[]{:S(2)}) copy-start(bf16[512,512]{1,0:T(8,128)(2,1)} %get-tuple-element.22.active) | copy-start | bytes 1572868
  130.0 33.7 %copy-start.2 = (bf16[512,1024]{1,0:T(8,128)(2,1)S(1)}, bf16[512,1024]{1,0:T(8,128)(2,1)}, u32[]{:S(2)}) copy-start(bf16[512,1024]{1,0:T(8,128)(2,1)} %narrow.1) | copy-start | bytes 3145732
  130.0 33.7 %copy-start.8 = (bf16[512,1024]{1,0:T(8,128)(2,1)S(1)}, bf16[512,1024]{1,0:T(8,128)(2,1)}, u32[]{:S(2)}) copy-start(bf16[512,1024]{1,0:T(8,128)(2,1)} %get-tuple-element.21.normed) | copy-start | bytes 3145732
  169.5 4.6 %collective-permute-start.7 = (bf16[32,32,512]{2,1,0:T(8,128)(2,1)S(1)}, bf16[32,32,512]{2,1,0:T(8,128)(2,1)S(1)}, u32[]{:S(2)}, u32[]{:S(2)}) collective-permute-start(bf16[32,32,512]{2,1,0:T(8,128)(2,1)S(1)} %get-tuple-element.25), channel_id=1, source_target_pairs={{0,8},{8,0},{1,9},{9,1},{2,10},{10,2},{3,11},{11,3},{4,12},{12,4},... | collective-permute-start | bytes 3145736 | tf_op jit(solution)/shard_map/ppermute | solution.py:399
Sparse Core Ops, SparseCore 0:
  53.5 59.2 all-gather.2

commit v8 on v6

--- a/solution.py
+++ b/solution.py
@@ -63,7 +63,7 @@
     )
 
 
-def project_body(block, gain, weights, made):
+def project_body(block, gain, weights, place, before, made, after):
     values = block[:, :TD].astype(F32)
     normed = layer_norm(values, gain[...]).astype(BF)
     gap = jnp.zeros((128, 40), F32)
@@ -71,22 +71,26 @@
         part = lax.dot_general(normed, weights[j], LANES, preferred_element_type=F32)
         part = jnp.concatenate([part[:, :88], gap, part[:, 88:], gap], axis=1)
         made[:, 256 * j : 256 * j + 256] = part.astype(BF)
-
-
-def project(block, gain, weights):
+    spots = lax.broadcasted_iota(jnp.int32, (64, 128), 1)
+    chosen = jnp.where(spots == place[...], 1.0, 0.0).astype(BF)
+    own = jnp.dot(chosen, block[:, :TD], preferred_element_type=F32)
+    after[...] = (before[...].astype(F32) + own).astype(BF)
+
+
+def project(block, gain, weights, place, before):
     return kernel_call(
         project_body,
-        [jax.ShapeDtypeStruct((128, 768), BF)],
-        flops=2 * 128 * 528 * TD,
-        arrays=3,
+        [jax.ShapeDtypeStruct((128, 768), BF), jax.ShapeDtypeStruct((64, TD), BF)],
+        flops=2 * 128 * (528 + 64) * TD,
+        arrays=5,
         moved=2_500_000,
-    )(block, gain, weights)[0]
+    )(block, gain, weights, place, before)
 
 
 def middle_body(me_ref, *refs):
     held, made, (place, gain, widen, narrow) = refs[:8], refs[8:16], refs[16:20]
-    *far, joint, own_out, picked_out = refs[20:26]
-    rows_by, queries, keys, values, normed_out, active_out, slope_out, sent = refs[26:]
+    *far, joint, own_out = refs[20:25]
+    rows_by, queries, keys, values, normed_out, active_out, slope_out, sent = refs[25:]
 
     def prepare():
         me = me_ref[0]
@@ -100,14 +104,6 @@
                 ]
         for b in range(8):
             own_out[:, 128 * b : 128 * b + 128] = rows_by[b, mine, :]
-
-        spots = lax.broadcasted_iota(jnp.int32, (64, 128), 1)
-        own_place = place[mine, :]
-        total = jnp.zeros((64, TD), F32)
-        for s in range(8):
-            chosen = jnp.where(spots + 128 * s == own_place, 1.0, 0.0).astype(BF)
-            total += jnp.dot(chosen, held[s][:, :TD], preferred_element_type=F32)
-        picked_out[...] = total.astype(BF)
 
         for s in range(8):
             queries[128 * s : 128 * s + 128, :] = made[s][:, :256]
@@ -177,10 +173,9 @@
             jax.ShapeDtypeStruct((512, 512), F32),
             jax.ShapeDtypeStruct((512, 1280), BF),
             jax.ShapeDtypeStruct((64, 1024), BF),
-            jax.ShapeDtypeStruct((64, TD), BF),
         ],
         in_specs=[SMEM] + [VMEM] * 20,
-        out_specs=[HBM, HBM, HBM, banded(1280), once(1024), once(TD)],
+        out_specs=[HBM, HBM, HBM, banded(1280), once(1024)],
         scratch_shapes=[pltpu.VMEM((8, 512, 128), BF)]
         + [pltpu.VMEM((1024, 256), BF)] * 3
         + [
@@ -191,7 +186,7 @@
         ],
         compiler_params=pltpu.CompilerParams(vmem_limit_bytes=48 << 20),
         cost_estimate=pl.CostEstimate(
-            flops=2 * 512 * 1024 * (1024 + 768) + 2 * 64 * 1024 * TD,
+            flops=2 * 512 * 1024 * (1024 + 768),
             bytes_accessed=12_000_000,
             transcendentals=0,
         ),
@@ -368,9 +363,15 @@
     out_full, head_full = assemble(pieces.reshape(16, 8, 14, 16, 128))
 
     here = jnp.reshape(me, (1,)).astype(jnp.int32)
-    made = [project(h, teacher_gain.reshape(1, -1), teacher_qkv) for h in held]
     place = ((me - picked // 128) % 8) * 128 + picked % 128
-    normed_rows, activity, slope_pre, joint, own_rows, own_patches = middle(
+    own_place = lax.dynamic_slice_in_dim(place, me * 64, 64, 0).reshape(64, 1)
+    made = [None] * 8
+    own_patches = jnp.zeros((64, TD), BF)
+    for s in (0, 1, 7, 2, 6, 3, 5, 4):
+        made[s], own_patches = project(
+            held[s], teacher_gain.reshape(1, -1), teacher_qkv, own_place - 128 * s, own_patches
+        )
+    normed_rows, activity, slope_pre, joint, own_rows = middle(
         here,
         held,
         made,

time: 218 us -> 226 us (1.037)
  waiting for transfers between devices: 59.5 us -> 50.2 us
  local copies, waits for them, and re-layouts: 4.11 us -> 12 us
  blocking collectives: 64.7 us -> 70 us
  Pallas kernels: 39.3 us -> 44.1 us
    all_gather x1, waiting for transfers between devices: 18 us -> 7.32 us  [on_device(): pieces = lax.all_gather(mine, ('z', 'c', 'mp'), axis=0)]
    all_to_all x1, waiting for transfers between devices: 6.37 us -> 14 us  [on_device(): arrived = lax.all_to_all(joint.reshape(8, 64, 1280), 'mp', 0, 0, tiled=True)]
    ppermute x4, waiting for transfers between devices: 32.5 us -> 26.3 us  [ring(): right = lax.ppermute(right, 'mp', shift(1))]
    pallas_call x8, Pallas kernels: 7.23 us -> 11.8 us  [project(): kernel_call(project_body, [jax.ShapeDtypeStruct((128, 768), BF), jax.Shap...]
    sub x0 -> x7, local copies, waits for them, and re-layouts: none -> 4.34 us  [on_device(): own_place - 128 * s]
    all_to_all x1, blocking collectives: 29.3 us -> 32.2 us  [on_device(): back = lax.all_to_all(back_own, 'mp', 0, 0, tiled=True)]
    unnamed x27 -> x53, local copies, waits for them, and re-layouts: 0.19 us -> 3.04 us
    all_to_all x1, blocking collectives: 35.4 us -> 37.8 us  [on_device(): kept = lax.all_to_all(kept, ('z', 'x'), 0, 0, tiled=True)]
  transfers between devices with their start and end apart: 10 -> 10, of which waited for: 7 -> 6; matrix products, arithmetic and copies ran while one was open for 1% -> 3% of each run, Pallas kernels for 13% -> 15%
where the time goes in v8:
time: 226 us; the launch traced here: 225 us
  blocking collectives  70 us (31%)
  waiting for transfers between devices  50.2 us (22%)
  Pallas kernels  44.1 us (20%)
  starting transfers between devices  31.6 us (14%)
  between operations  15.3 us (7%)
  local copies, waits for them, and re-layouts  12 us (5%)
    all_to_all x1, blocking collectives, on_device(): kept = lax.all_to_all(kept, ('z', 'x'), 0, 0, tiled=True)  37.8 us
    all_to_all x1, blocking collectives, on_device(): back = lax.all_to_all(back_own, 'mp', 0, 0, tiled=True)  32.2 us
    ppermute x4, waiting for transfers between devices, ring(): right = lax.ppermute(right, 'mp', shift(1))  26.3 us
    ppermute x3, starting transfers between devices, ring(): left = lax.ppermute(left, 'mp', shift(-1))  14.1 us
    all_to_all x1, waiting for transfers between devices, on_device(): arrived = lax.all_to_all(joint.reshape(8, 64, 1280), 'mp', 0, 0, tiled=True)  14 us
    pallas_call x1, Pallas kernels, middle(): pl.pallas_call(middle_body, grid=(4,), out_shape=[jax.ShapeDtypeStruct((5...  12.4 us
    pallas_call x8, Pallas kernels, project(): kernel_call(project_body, [jax.ShapeDtypeStruct((128, 768), BF), jax.Shap...  11.8 us
    ppermute x4, starting transfers between devices, ring(): right = lax.ppermute(right, 'mp', shift(1))  9.21 us
  transfers between devices with their start and end apart: 10, of which 6 were waited for; matrix products, arithmetic and copies ran while one was open for 3% of the time, Pallas kernels for 15%

profile of v8, /device:TPU:2, one launch (start us, length us, event | category | flops | bytes accessed | tf_op | source)
XLA Modules:
  0.0 225.0 jit_solution(10679813381505044458)
XLA Ops:
  7.2 1.5 reshape.239
  10.5 1.3 gather_fusion
  12.0 3.5 %collective-permute-start = (bf16[128,1920]{1,0:T(8,128)(2,1)S(1)}, bf16[128,1920]{1,0:T(8,128)(2,1)S(1)}, u32[]{:S(2)}, u32[]{:S(2)}) collective-permute-start(bf16[128,1920]{1,0:T(8,128)(2,1)S(1)} %slice_dynamic-update-slice_fusion.block.refs_0_), channel_id=1, source_target_pairs={{0,1},{1,2},{2,3},{3,4},{4,5},{5,6},{6,7},{7,0},{8,9},{9,10},{10,1... | collective-permute-start | bytes 1474568 | tf_op jit(solution)/shard_map/ppermute | solution.py:31
  15.5 3.8 %collective-permute-start.4 = (bf16[128,1920]{1,0:T(8,128)(2,1)S(1)}, bf16[128,1920]{1,0:T(8,128)(2,1)S(1)}, u32[]{:S(2)}, u32[]{:S(2)}) collective-permute-start(bf16[128,1920]{1,0:T(8,128)(2,1)S(1)} %slice_dynamic-update-slice_fusion.block.refs_0_), channel_id=1, source_target_pairs={{0,7},{1,0},{2,1},{3,2},{4,3},{5,4},{6,5},{7,6},{8,15},{9,8},{10,9... | collective-permute-start | bytes 1474568 | tf_op jit(solution)/shard_map/ppermute | solution.py:34
  19.3 9.3 %collective-permute-done.block.refs_1_ = bf16[128,1920]{1,0:T(8,128)(2,1)S(1)} collective-permute-done((bf16[128,1920]{1,0:T(8,128)(2,1)S(1)}, bf16[128,1920]{1,0:T(8,128)(2,1)S(1)}, u32[]{:S(2)}, u32[]{:S(2)}) %collective-permute-start) | collective-permute-done | bytes 491552 | tf_op jit(solution)/shard_map/ppermute | solution.py:31
  28.6 1.9 collective-permute-start.1
  30.5 5.1 %collective-permute-start.5 = (bf16[128,1920]{1,0:T(8,128)(2,1)S(1)}, bf16[128,1920]{1,0:T(8,128)(2,1)}, u32[]{:S(2)}, u32[]{:S(2)}) collective-permute-start(bf16[128,1920]{1,0:T(8,128)(2,1)S(1)} %collective-permute-done.4.block.refs_7_), channel_id=1, source_target_pairs={{0,7},{1,0},{2,1},{3,2},{4,3},{5,4},{6,5},{7,6},{8,15},{9,8},{10,9... | collective-permute-start | bytes 1474568 | tf_op jit(solution)/shard_map/ppermute | solution.py:34
  35.6 9.4 %collective-permute-done.1.block.refs_2_ = bf16[128,1920]{1,0:T(8,128)(2,1)S(1)} collective-permute-done((bf16[128,1920]{1,0:T(8,128)(2,1)S(1)}, bf16[128,1920]{1,0:T(8,128)(2,1)S(1)}, u32[]{:S(2)}, u32[]{:S(2)}) %collective-permute-start.1) | collective-permute-done | bytes 491552 | tf_op jit(solution)/shard_map/ppermute | solution.py:31
  45.0 1.9 collective-permute-start.2
  46.9 0.8 copy-done.2
  47.7 5.1 %collective-permute-start.6 = (bf16[128,1920]{1,0:T(8,128)(2,1)}, bf16[128,1920]{1,0:T(8,128)(2,1)}, u32[]{:S(2)}, u32[]{:S(2)}) collective-permute-start(bf16[128,1920]{1,0:T(8,128)(2,1)} %collective-permute-done.5.block.refs_6_), channel_id=1, source_target_pairs={{0,7},{1,0},{2,1},{3,2},{4,3},{5,4},{6,5},{7,6},{8,15},{9,8},{10,9... | collective-permute-start | bytes 1474568 | tf_op jit(solution)/shard_map/ppermute | solution.py:34
  52.8 7.6 %collective-permute-done.2.block.refs_3_ = bf16[128,1920]{1,0:T(8,128)(2,1)} collective-permute-done((bf16[128,1920]{1,0:T(8,128)(2,1)S(1)}, bf16[128,1920]{1,0:T(8,128)(2,1)}, u32[]{:S(2)}, u32[]{:S(2)}) %collective-permute-start.2) | collective-permute-done | bytes 491552 | tf_op jit(solution)/shard_map/ppermute | solution.py:31
  60.4 1.9 collective-permute-start.3
  68.3 1.0 shard_map.130
  69.3 1.0 shard_map.131
  70.3 1.0 shard_map.132
  71.3 1.0 shard_map.133
  72.3 2.0 shard_map.134
  74.3 2.0 shard_map.135
  76.3 2.0 shard_map.136
  78.3 2.0 shard_map.137
  81.0 12.4 %shard_map.138 = (bf16[512,1024]{1,0:T(8,128)(2,1)}, bf16[512,512]{1,0:T(8,128)(2,1)}, f32[512,512]{1,0:T(8,128)}, bf16[512,1280]{1,0:T(8,128)(2,1)}, bf16[64,1024]{1,0:T(8,128)(2,1)S(1)}) custom-call(s32[1]{0:T(128)} %bitcast.2.me_ref, bf16[128,1920]{1,0:T(8,128)(2,1)S(1)} %slice_dynamic-update-slice_fusion.block.refs_0_, ...), custom_call_target="tpu_custom_call" | custom-call | flops 1879048192 | bytes 12000000 | tf_op jit(solution)/shard_map/pallas_call | solution.py:167
  94.1 6.4 %all-to-all-start = ((bf16[8,64,1280]{2,1,0:T(8,128)(2,1)}), bf16[8,64,1280]{2,1,0:T(8,128)(2,1)S(1)}, u32[]{:S(2)}, u32[]{:S(2)}) async-start(bf16[8,64,1280]{2,1,0:T(8,128)(2,1)} %bitcast.51), calls=%async_computation | async-start | bytes 2621440 | tf_op jit(solution)/shard_map/all_to_all | solution.py:383
  101.1 7.3 %all-gather.3.cloned.1.call-done = bf16[1792,16,128]{2,1,0:T(8,128)(2,1)} async-done(((bf16[14,16,128]{2,1,0:T(8,128)(2,1)}), bf16[1792,16,128]{2,1,0:T(8,128)(2,1)}) %all-gather.3.cloned.1.call-update) | async-done | bytes 7340048 | tf_op jit(solution)/shard_map/all_gather | solution.py:362
  108.5 8.6 %shard_map.139 = (bf16[1408,1408]{1,0:T(8,128)(2,1)}, bf16[1408,1024]{1,0:T(8,128)(2,1)}) custom-call(bf16[16,8,14,16,128]{4,3,2,1,0:T(8,128)(2,1)} %bitcast.46), custom_call_target="tpu_custom_call" | custom-call | bytes 14000000 | tf_op jit(solution)/shard_map/pallas_call | solution.py:263
  117.0 14.0 %all-to-all-done.arrived = bf16[8,64,1280]{2,1,0:T(8,128)(2,1)S(1)} async-done(((bf16[8,64,1280]{2,1,0:T(8,128)(2,1)}), bf16[8,64,1280]{2,1,0:T(8,128)(2,1)S(1)}, u32[]{:S(2)}, u32[]{:S(2)}) %all-to-all-start) | async-done | bytes 1310752 | tf_op jit(solution)/shard_map/all_to_all | solution.py:383
  131.1 5.5 %shard_map.140 = bf16[8,33,16,128]{3,2,1,0:T(8,128)(2,1)S(1)} custom-call(f32[64,1]{1,0:T(8,128)S(1)} %fusion.6.weight, bf16[8,64,1280]{2,1,0:T(8,128)(2,1)S(1)} %all-to-all-done.arrived, bf16[64,1024]{1,0:T(8,128)(2,1)S(1)} %copy-done.8, bf16[64,1408]{1,0:T(8,128)(2,1)S(1)} %copy-done.6, bf16[1408,1408]{1,0:T(8,128)(2,1)} %get-tuple-element.47.out_far, ...), custom_call_target="tpu_custom_call" | custom-call | flops 622854144 | bytes 10000000 | tf_op jit(solution)/shard_map/pallas_call | solution.py:236
  136.6 32.2 %all_to_all.15.back_in = bf16[8,33,16,128]{3,2,1,0:T(8,128)(2,1)S(1)} all-to-all(bf16[8,33,16,128]{3,2,1,0:T(8,128)(2,1)S(1)} %shard_map.140), channel_id=1, replica_groups=mesh['z'=8,'x'=4,'c'=2,'mp'=8] {'mp'}, dimensions={0} | all-to-all | bytes 2162688 | tf_op jit(solution)/shard_map/all_to_all | solution.py:390
  168.9 5.8 %shard_map.141 = (bf16[32,32,512]{2,1,0:T(8,128)(2,1)S(1)}, bf16[32,32,512]{2,1,0:T(8,128)(2,1)S(1)}, f32[1]{0:T(128)}) custom-call(s32[1]{0:T(128)} %bitcast.core_ref, bf16[8,33,16,128]{3,2,1,0:T(8,128)(2,1)S(1)} %all_to_all.15.back_in, bf16[512,1024]{1,0:T(8,128)(2,1)S(1)} %copy-done.17, bf16[512,512]{1,0:T(8,128)(2,1)S(1)} %copy-done.19, ...), custom_call_target="tpu_custom_call" | custom-call | flops 1610612736 | bytes 8000000 | tf_op jit(solution)/shard_map/pallas_call | solution.py:321
  174.6 1.9 collective-permute-start.7
  176.6 2.6 %collective-permute-done.7 = bf16[32,32,512]{2,1,0:T(8,128)(2,1)S(1)} collective-permute-done((bf16[32,32,512]{2,1,0:T(8,128)(2,1)S(1)}, bf16[32,32,512]{2,1,0:T(8,128)(2,1)S(1)}, u32[]{:S(2)}, u32[]{:S(2)}) %collective-permute-start.7) | collective-permute-done | bytes 1048608 | tf_op jit(solution)/shard_map/ppermute | solution.py:394
  179.6 37.8 %all_to_all.16 = bf16[32,32,512]{2,1,0:T(8,128)(2,1)S(1)} all-to-all(bf16[32,32,512]{2,1,0:T(8,128)(2,1)S(1)} %add_convert_fusion), channel_id=1, replica_groups=mesh['z'=8,'x'=4,'c'=2,'mp'=8] {'z','x'}, dimensions={0} | all-to-all | bytes 2097152 | tf_op jit(solution)/shard_map/all_to_all | solution.py:396
  (87 shorter events, 10.3 us)
Async XLA Ops:
  7.2 3.3 %copy-start = (bf16[1,1024,128]{2,1,0:T(8,128)(2,1)S(1)}, bf16[1,1024,128]{2,1,0:T(8,128)(2,1)}, u32[]{:S(2)}) copy-start(bf16[1,1024,128]{2,1,0:T(8,128)(2,1)} %param.15) | copy-start | bytes 786436
  7.2 1.7 copy-start.20
  7.2 101.3 %all-gather.3.cloned.1.call-start = ((), (), s32[]{:S(2)}) async-start(), calls=%async_computation.3 | async-start | bytes 7397376 | tf_op jit(solution)/shard_map/all_gather | solution.py:362
  8.9 1.0 copy-start.22
  9.1 2.8 %copy-start.21 = (bf16[1,128,1408]{2,1,0:T(8,128)(2,1)S(1)}, bf16[1,128,1408]{2,1,0:T(8,128)(2,1)}, u32[]{:S(2)}) copy-start(bf16[1,128,1408]{2,1,0:T(8,128)(2,1)} %param.11) | copy-start | bytes 1081348
  9.1 54.0 %copy-start.23 = (f32[1408]{0:T(1024)S(1)}, f32[1408]{0:T(1024)}, u32[]{:S(2)}) copy-start(f32[1408]{0:T(1024)} %param.12) | copy-start | bytes 16900
  9.1 58.4 %copy-start.1 = (bf16[3,176,1408]{2,1,0:T(8,128)(2,1)S(1)}, bf16[3,176,1408]{2,1,0:T(8,128)(2,1)}, u32[]{:S(2)}) copy-start(bf16[3,176,1408]{2,1,0:T(8,128)(2,1)} %weights.15) | copy-start | bytes 4460548
  12.0 16.6 %collective-permute-start = (bf16[128,1920]{1,0:T(8,128)(2,1)S(1)}, bf16[128,1920]{1,0:T(8,128)(2,1)S(1)}, u32[]{:S(2)}, u32[]{:S(2)}) collective-permute-start(bf16[128,1920]{1,0:T(8,128)(2,1)S(1)} %slice_dynamic-update-slice_fusion.block.refs_0_), channel_id=1, source_target_pairs={{0,1},{1,2},{2,3},{3,4},{4,5},{5,6},{6,7},{7,0},{8,9},{9,10},{10,1... | collective-permute-start | bytes 1474568 | tf_op jit(solution)/shard_map/ppermute | solution.py:31
  15.5 15.0 %collective-permute-start.4 = (bf16[128,1920]{1,0:T(8,128)(2,1)S(1)}, bf16[128,1920]{1,0:T(8,128)(2,1)S(1)}, u32[]{:S(2)}, u32[]{:S(2)}) collective-permute-start(bf16[128,1920]{1,0:T(8,128)(2,1)S(1)} %slice_dynamic-update-slice_fusion.block.refs_0_), channel_id=1, source_target_pairs={{0,7},{1,0},{2,1},{3,2},{4,3},{5,4},{6,5},{7,6},{8,15},{9,8},{10,9... | collective-permute-start | bytes 1474568 | tf_op jit(solution)/shard_map/ppermute | solution.py:34
  28.6 16.5 %collective-permute-start.1 = (bf16[128,1920]{1,0:T(8,128)(2,1)S(1)}, bf16[128,1920]{1,0:T(8,128)(2,1)S(1)}, u32[]{:S(2)}, u32[]{:S(2)}) collective-permute-start(bf16[128,1920]{1,0:T(8,128)(2,1)S(1)} %collective-permute-done.block.refs_1_), channel_id=1, source_target_pairs={{0,1},{1,2},{2,3},{3,4},{4,5},{5,6},{6,7},{7,0},{8,9},{9,10},{10,1... | collective-permute-start | bytes 1474568 | tf_op jit(solution)/shard_map/ppermute | solution.py:31
  30.5 17.2 %collective-permute-start.5 = (bf16[128,1920]{1,0:T(8,128)(2,1)S(1)}, bf16[128,1920]{1,0:T(8,128)(2,1)}, u32[]{:S(2)}, u32[]{:S(2)}) collective-permute-start(bf16[128,1920]{1,0:T(8,128)(2,1)S(1)} %collective-permute-done.4.block.refs_7_), channel_id=1, source_target_pairs={{0,7},{1,0},{2,1},{3,2},{4,3},{5,4},{6,5},{7,6},{8,15},{9,8},{10,9... | collective-permute-start | bytes 1474568 | tf_op jit(solution)/shard_map/ppermute | solution.py:34
  45.0 15.4 %collective-permute-start.2 = (bf16[128,1920]{1,0:T(8,128)(2,1)S(1)}, bf16[128,1920]{1,0:T(8,128)(2,1)}, u32[]{:S(2)}, u32[]{:S(2)}) collective-permute-start(bf16[128,1920]{1,0:T(8,128)(2,1)S(1)} %collective-permute-done.1.block.refs_2_), channel_id=1, source_target_pairs={{0,1},{1,2},{2,3},{3,4},{4,5},{5,6},{6,7},{7,0},{8,9},{9,10},{10,1... | collective-permute-start | bytes 1474568 | tf_op jit(solution)/shard_map/ppermute | solution.py:31
  46.9 0.8 copy-start.2
  47.7 28.6 %collective-permute-start.6 = (bf16[128,1920]{1,0:T(8,128)(2,1)}, bf16[128,1920]{1,0:T(8,128)(2,1)}, u32[]{:S(2)}, u32[]{:S(2)}) collective-permute-start(bf16[128,1920]{1,0:T(8,128)(2,1)} %collective-permute-done.5.block.refs_6_), channel_id=1, source_target_pairs={{0,7},{1,0},{2,1},{3,2},{4,3},{5,4},{6,5},{7,6},{8,15},{9,8},{10,9... | collective-permute-start | bytes 1474568 | tf_op jit(solution)/shard_map/ppermute | solution.py:34
  60.4 17.9 %collective-permute-start.3 = (bf16[128,1920]{1,0:T(8,128)(2,1)}, bf16[128,1920]{1,0:T(8,128)(2,1)}, u32[]{:S(2)}, u32[]{:S(2)}) collective-permute-start(bf16[128,1920]{1,0:T(8,128)(2,1)} %collective-permute-done.2.block.refs_3_), channel_id=1, source_target_pairs={{0,1},{1,2},{2,3},{3,4},{4,5},{5,6},{6,7},{7,0},{8,9},{9,10},{10,1... | collective-permute-start | bytes 1474568 | tf_op jit(solution)/shard_map/ppermute | solution.py:31
  67.5 1.8 copy-start.15
  67.5 0.8 copy-start.13
  68.3 2.0 copy-start.14
  69.3 2.0 copy-start.3
  69.3 2.0 copy-start.12
  70.3 2.0 copy-start.11
  71.3 3.0 %copy-start.10 = (s32[64,1]{1,0:T(8,128)S(1)}, s32[64,1]{1,0:T(8,128)}, u32[]{:S(2)}) copy-start(s32[64,1]{1,0:T(8,128)} %copy.61.place) | copy-start | bytes 772
  72.3 4.0 %copy-start.9 = (s32[64,1]{1,0:T(8,128)S(1)}, s32[64,1]{1,0:T(8,128)}, u32[]{:S(2)}) copy-start(s32[64,1]{1,0:T(8,128)} %copy.62.place) | copy-start | bytes 772
  76.3 4.7 %copy-start.16 = (f32[1024]{0:T(1024)S(1)}, f32[1024]{0:T(1024)}, u32[]{:S(2)}) copy-start(f32[1024]{0:T(1024)} %param.16) | copy-start | bytes 12292
  94.1 37.0 %all-to-all-start = ((bf16[8,64,1280]{2,1,0:T(8,128)(2,1)}), bf16[8,64,1280]{2,1,0:T(8,128)(2,1)S(1)}, u32[]{:S(2)}, u32[]{:S(2)}) async-start(bf16[8,64,1280]{2,1,0:T(8,128)(2,1)} %bitcast.51), calls=%async_computation | async-start | bytes 2621440 | tf_op jit(solution)/shard_map/all_to_all | solution.py:383
  108.5 22.6 %copy-start.6 = (bf16[64,1408]{1,0:T(8,128)(2,1)S(1)}, bf16[64,1408]{1,0:T(8,128)(2,1)}, u32[]{:S(2)}) copy-start(bf16[64,1408]{1,0:T(8,128)(2,1)} %copy-done.5) | copy-start | bytes 540676
  108.5 22.6 %copy-start.8 = (bf16[64,1024]{1,0:T(8,128)(2,1)S(1)}, bf16[64,1024]{1,0:T(8,128)(2,1)}, u32[]{:S(2)}) copy-start(bf16[64,1024]{1,0:T(8,128)(2,1)} %copy-done.7) | copy-start | bytes 393220
  131.0 37.8 %copy-start.18 = (f32[512,512]{1,0:T(8,128)S(1)}, f32[512,512]{1,0:T(8,128)}, u32[]{:S(2)}) copy-start(f32[512,512]{1,0:T(8,128)} %get-tuple-element.51.slope) | copy-start | bytes 3145732
  131.0 37.8 %copy-start.19 = (bf16[512,512]{1,0:T(8,128)(2,1)S(1)}, bf16[512,512]{1,0:T(8,128)(2,1)}, u32[]{:S(2)}) copy-start(bf16[512,512]{1,0:T(8,128)(2,1)} %get-tuple-element.50.active) | copy-start | bytes 1572868
  136.6 32.3 %copy-start.4 = (bf16[512,1024]{1,0:T(8,128)(2,1)S(1)}, bf16[512,1024]{1,0:T(8,128)(2,1)}, u32[]{:S(2)}) copy-start(bf16[512,1024]{1,0:T(8,128)(2,1)} %narrow.1) | copy-start | bytes 3145732
  136.6 32.3 %copy-start.17 = (bf16[512,1024]{1,0:T(8,128)(2,1)S(1)}, bf16[512,1024]{1,0:T(8,128)(2,1)}, u32[]{:S(2)}) copy-start(bf16[512,1024]{1,0:T(8,128)(2,1)} %get-tuple-element.49.normed) | copy-start | bytes 3145732
  174.6 4.6 %collective-permute-start.7 = (bf16[32,32,512]{2,1,0:T(8,128)(2,1)S(1)}, bf16[32,32,512]{2,1,0:T(8,128)(2,1)S(1)}, u32[]{:S(2)}, u32[]{:S(2)}) collective-permute-start(bf16[32,32,512]{2,1,0:T(8,128)(2,1)S(1)} %get-tuple-element.53), channel_id=1, source_target_pairs={{0,8},{8,0},{1,9},{9,1},{2,10},{10,2},{3,11},{11,3},{4,12},{12,4},... | collective-permute-start | bytes 3145736 | tf_op jit(solution)/shard_map/ppermute | solution.py:394
  (2 other events, 1.3 us)
Sparse Core Ops, SparseCore 0:
  11.2 97.2 all-gather.2
